TPU v7x, 32 devices: a whole 2x2x4 slice. The times are simulated.
32 devices in a mesh: seq: 8 (over z, x), head: 4 (over y, core).
Axes of the slice: x: 2, y: 2, z: 4, core: 2. Of those that a mesh axis runs over, the one named last changes fastest.
Arguments:
- inputs: bfloat16 [1, 2048, 1024], P(None, 'seq'), may hold values from -6 to 6
- cotangent: bfloat16 [1, 2048, 1024], P(None, 'seq'), may hold values from -6 to 6
- query_weight: bfloat16 [1024, 1024], P(None, 'head'), may hold values from -0.1875 to 0.1875
- key_weight: bfloat16 [1024, 1024], P(None, 'head'), may hold values from -0.1875 to 0.1875
- value_weight: bfloat16 [1024, 1024], P(None, 'head'), may hold values from -0.1875 to 0.1875
- output_weight: bfloat16 [1024, 1024], P('head'), may hold values from -1.5 to 1.5
- up_weight: bfloat16 [1024, 4096], P(None, 'head'), may hold values from -0.1875 to 0.1875
- down_weight: bfloat16 [4096, 1024], P('head'), may hold values from -0.09375 to 0.09375
- first_gain: float32 [1024], replicated, may hold values from 0.5 to 1.5
- second_gain: float32 [1024], replicated, may hold values from 0.5 to 1.5
- position_bias: float32 [8, 32], P('head'), may hold values from -3 to 3
- gate_bias: float32 [8], P('head'), may hold values from -2 to 2
- memory_table: bfloat16 [65536, 8, 256], P('seq', 'head'), may hold values from -6 to 6
- retrieved: int32 [1, 2048, 8, 32], P(None, 'seq', 'head'), may hold values from 0 to 65535, as said below
- lengths: int32 [1, 4], replicated, may hold values from 1 to 1024, 2048 in all within a row
Outputs:
- layer_out: bfloat16 [1, 2048, 1024], P(None, 'seq')
- input_grad: float32 [1, 2048, 1024], P(None, 'seq')
- query_grad: float32 [1024, 1024], P('seq', 'head')
- key_grad: float32 [1024, 1024], P('seq', 'head')
- value_grad: float32 [1024, 1024], P('seq', 'head')
- output_grad: float32 [1024, 1024], P('head', 'seq')
- up_grad: float32 [1024, 4096], P('seq', 'head')
- down_grad: float32 [4096, 1024], P('head', 'seq')
- first_gain_grad: float32 [1024], P('seq')
- second_gain_grad: float32 [1024], P('seq')
- position_grad: float32 [8, 32], P('head')
- gate_grad: float32 [8], P('head')
- rms_values: float32 [3], replicated
Inputs may be any that keep to these rules, and one draw needn't show every extreme that they name: `retrieved`: for every stream, head and aligned block of 256 positions, each range of 8192 consecutive slots (starting at a multiple of 8192) holds exactly 1024 of the block's recalled slots. `lengths`: each row sums to 2048.
All inputs are finite; a program needn't handle non-finite values.
Results may differ from a plain program's by a relative error of at most 0.018.
Values may be sent and summed in bfloat16 or wider, within the bound.
A program may use at most 320 MiB of HBM per device.

v0:
```python
import math

import jax
import jax.numpy as jnp
import numpy as np
from jax import lax
from jax.sharding import PartitionSpec as P

W = 512


eps = 1e-06
exact_span = 16
far_distance = 128
highest = lax.Precision.HIGHEST


def from_behind(value, axis, steps):
    count = lax.axis_size(axis)
    first, last = (max(0, -steps), min(count, count - steps))
    return lax.ppermute(value, axis, [(source, source + steps) for source in range(first, last)])


def bucket_table(key_span, bucket_total):
    found = []
    for distance in range(key_span):
        if distance < exact_span:
            found.append(distance)
        else:
            scaled = math.log(distance / exact_span) / math.log(far_distance / exact_span)
            found.append(
                min(bucket_total - 1, exact_span + math.floor(scaled * (bucket_total - exact_span)))
            )
    return np.asarray(found)


def window_layout(block_len, window_len, bucket_total):
    key_span = window_len + block_len
    delta = np.arange(block_len)[:, None] + window_len - np.arange(key_span)[None, :]
    in_window = (delta >= 0) & (delta < window_len)
    table = bucket_table(key_span, bucket_total)
    return (table[np.clip(delta, 0, key_span - 1)], in_window)


def norm_stats(values):
    row_scale = lax.rsqrt(jnp.mean(values * values, axis=-1, keepdims=True) + eps)
    return (values * row_scale, row_scale)


def norm_back(grad_normed, gain, normed_hat, row_scale):
    grad_hat = grad_normed * gain
    inner = jnp.mean(grad_hat * normed_hat, axis=-1, keepdims=True)
    return row_scale * (grad_hat - normed_hat * inner)


def softmax_rows(scores):
    top_score = jnp.max(scores, axis=-1, keepdims=True)
    raised = jnp.exp(scores - top_score)
    return raised / jnp.sum(raised, axis=-1, keepdims=True)


def document_ids(lengths, first_place, count):
    doc_ends = jnp.cumsum(lengths, axis=-1)
    places = first_place + jnp.arange(count, dtype=jnp.int32)
    found_ids = jnp.sum((doc_ends[:, None, :] <= places[None, :, None]).astype(jnp.int32), axis=-1)
    return jnp.where(places[None, :] >= 0, found_ids, -1)


def diagonal_sums(values, window_len):
    head_count, row_count, col_count = values.shape
    flipped = jnp.pad(values[..., ::-1], ((0, 0), (0, 0), (0, row_count)))
    full_width = col_count + row_count
    sheared = flipped.reshape(head_count, row_count * full_width)[:, : row_count * (full_width - 1)]
    totals = jnp.sum(sheared.reshape(head_count, row_count, full_width - 1), axis=1)
    return totals[:, row_count - 1 : row_count - 1 + window_len]


def request_order(retrieved, slot_count, device_count):
    head_count = retrieved.shape[2]
    owners = retrieved // slot_count
    slot_codes = (
        retrieved % slot_count * head_count
        + jnp.arange(head_count, dtype=jnp.int32)[None, None, :, None]
    )
    sort_order = jnp.argsort(owners.reshape(-1), stable=True)
    sorted_codes = jnp.take(slot_codes.reshape(-1), sort_order).reshape(device_count, -1)
    return (sort_order, sorted_codes)


def restore_order(arrived, sort_order, lead_shape):
    flat_rows = arrived.reshape(sort_order.shape[0], -1)
    positions_back = (
        jnp.zeros_like(sort_order)
        .at[sort_order]
        .set(jnp.arange(sort_order.shape[0], dtype=jnp.int32))
    )
    return jnp.take(flat_rows, positions_back, axis=0).reshape(lead_shape + (flat_rows.shape[1],))


def fetch_rows(retrieved, memory_table):
    sort_order, sorted_codes = request_order(retrieved, memory_table.shape[0], lax.axis_size("seq"))
    slot_table = memory_table.reshape(-1, memory_table.shape[2])

    def serve_rows(requests):
        found_rows = jnp.take(slot_table, requests, axis=0)
        return lax.all_to_all(found_rows, "seq", split_axis=0, concat_axis=0, tiled=True)

    arrived = serve_rows(
        lax.all_to_all(sorted_codes, "seq", split_axis=0, concat_axis=0, tiled=True)
    )
    return restore_order(arrived, sort_order, retrieved.shape)


def fetch_again(retrieved, memory_table):
    sort_order, sorted_codes = request_order(retrieved, memory_table.shape[0], lax.axis_size("seq"))
    slot_table = memory_table.reshape(-1, memory_table.shape[2])

    def serve_rows(requests):
        found_rows = jnp.take(slot_table, requests, axis=0)
        return lax.all_to_all(found_rows, "seq", split_axis=0, concat_axis=0, tiled=True)

    arrived = serve_rows(
        lax.all_to_all(sorted_codes, "seq", split_axis=0, concat_axis=0, tiled=True)
    )
    return restore_order(arrived, sort_order, retrieved.shape)


def per_device(
    inputs,
    cotangent,
    query_weight,
    key_weight,
    value_weight,
    output_weight,
    up_weight,
    down_weight,
    first_gain,
    second_gain,
    position_bias,
    gate_bias,
    memory_table,
    retrieved,
    lengths,
):
    batch_size, block_len, model_width = inputs.shape
    head_count = gate_bias.shape[0]
    head_size = query_weight.shape[1] // head_count
    bucket_total = position_bias.shape[1]
    hop_count = W // block_len
    key_span = W + block_len
    score_scale = head_size ** (-0.5)
    seq_index = lax.axis_index("seq")
    bucket_index, in_window = window_layout(block_len, W, bucket_total)
    doc_query = document_ids(lengths, seq_index * block_len, block_len)
    doc_key = document_ids(lengths, seq_index * block_len - W, key_span)
    allowed = jnp.asarray(in_window)[None, None] & (
        doc_query[:, None, :, None] == doc_key[:, None, None, :]
    )
    bias_full = jnp.take(position_bias, jnp.asarray(bucket_index), axis=1)[None]
    tokens = inputs.astype(jnp.float32)
    hat_one, scale_one = norm_stats(tokens)
    normed_one = (hat_one * first_gain).astype(jnp.bfloat16)
    queries = jnp.dot(normed_one, query_weight, preferred_element_type=jnp.float32).astype(
        jnp.bfloat16
    )
    keys_own = jnp.dot(normed_one, key_weight, preferred_element_type=jnp.float32).astype(
        jnp.bfloat16
    )
    values_own = jnp.dot(normed_one, value_weight, preferred_element_type=jnp.float32).astype(
        jnp.bfloat16
    )
    current = jnp.stack((keys_own, values_own))
    pieces = [current]
    for hop_index in range(hop_count):
        current = from_behind(current, "seq", 1)
        pieces.insert(0, current)
    pair_window = jnp.concatenate(pieces, axis=2)
    query_four = queries.reshape(batch_size, block_len, head_count, head_size)
    key_four = pair_window[0].reshape(batch_size, key_span, head_count, head_size)
    value_four = pair_window[1].reshape(batch_size, key_span, head_count, head_size)

    def window_scores():
        raw_scores = (
            jnp.einsum("bihd,bjhd->bhij", query_four, key_four, preferred_element_type=jnp.float32)
            * score_scale
            + bias_full
        )
        return jnp.where(allowed, raw_scores, -1e30)

    scores = window_scores()
    top_score = jnp.max(scores, axis=-1, keepdims=True)
    raised = jnp.exp(scores - top_score)
    total = jnp.sum(raised, axis=-1, keepdims=True)
    log_total = top_score + jnp.log(total)
    window_weights = raised / total
    local_out = jnp.einsum(
        "bhij,bjhd->bihd",
        window_weights.astype(jnp.bfloat16),
        value_four,
        preferred_element_type=jnp.float32,
    )
    fetched = fetch_rows(retrieved, memory_table)

    def recall_softmax(rows_in):
        recall_scores = (
            jnp.einsum(
                "bihd,bihkd->bihk",
                query_four,
                rows_in[..., :head_size],
                preferred_element_type=jnp.float32,
            )
            * score_scale
        )
        return softmax_rows(recall_scores)

    recall_weights = recall_softmax(fetched)
    recalled = jnp.einsum(
        "bihk,bihkd->bihd",
        recall_weights.astype(jnp.bfloat16),
        fetched[..., head_size:],
        preferred_element_type=jnp.float32,
    )
    gate_flat = jax.nn.sigmoid(gate_bias)
    gate_values = gate_flat[:, None]
    mixed = (
        (gate_values * recalled + (1.0 - gate_values) * local_out)
        .reshape(batch_size, block_len, -1)
        .astype(jnp.bfloat16)
    )
    branch_attn = lax.psum(
        jnp.dot(mixed, output_weight, preferred_element_type=jnp.float32), "head"
    )
    middle = tokens + branch_attn
    hat_two, scale_two = norm_stats(middle)
    normed_two = (hat_two * second_gain).astype(jnp.bfloat16)
    upward = jnp.dot(normed_two, up_weight, preferred_element_type=jnp.float32)
    gelu_value, gelu_back = jax.vjp(jax.nn.gelu, upward)
    hidden = gelu_value.astype(jnp.bfloat16)
    branch_feed = lax.psum(
        jnp.dot(hidden, down_weight, preferred_element_type=jnp.float32).astype(jnp.bfloat16),
        "head",
    ).astype(jnp.float32)
    layer_sum = middle + branch_feed
    down_grad = jnp.einsum("bti,btd->id", hidden, cotangent, preferred_element_type=jnp.float32)
    grad_hidden = jnp.einsum(
        "btd,id->bti", cotangent, down_weight, preferred_element_type=jnp.float32
    )
    grad_upward = gelu_back(grad_hidden)[0].astype(jnp.bfloat16)
    up_grad = jnp.einsum("btd,bti->di", normed_two, grad_upward, preferred_element_type=jnp.float32)
    grad_normed_two = lax.psum(
        jnp.einsum("bti,di->btd", grad_upward, up_weight, preferred_element_type=jnp.float32),
        "head",
    )
    second_gain_part = jnp.sum(grad_normed_two * hat_two, axis=(0, 1))
    grad_middle = cotangent.astype(jnp.float32) + norm_back(
        grad_normed_two, second_gain, hat_two, scale_two
    )
    grad_branch = grad_middle.astype(jnp.bfloat16)
    output_grad = jnp.einsum("bte,btd->ed", mixed, grad_branch, preferred_element_type=jnp.float32)
    grad_mixed_low = jnp.einsum(
        "btd,ed->bte", grad_branch, output_weight, preferred_element_type=jnp.float32
    ).astype(jnp.bfloat16)
    grad_mixed = (
        lax.optimization_barrier(grad_mixed_low)
        .astype(jnp.float32)
        .reshape(batch_size, block_len, head_count, head_size)
    )
    gate_part = (
        jnp.sum(grad_mixed * (recalled - local_out), axis=(0, 1, 3)) * gate_flat * (1.0 - gate_flat)
    )
    grad_recalled = gate_values * grad_mixed
    grad_local = (1.0 - gate_values) * grad_mixed
    rows_back = fetch_again(retrieved, memory_table)
    recall_back = recall_softmax(rows_back)
    grad_recall_weights = jnp.einsum(
        "bihd,bihkd->bihk",
        grad_recalled,
        rows_back[..., head_size:],
        precision=highest,
        preferred_element_type=jnp.float32,
    )
    grad_recall_scores = (
        recall_back
        * (grad_recall_weights - jnp.sum(recall_back * grad_recall_weights, axis=-1, keepdims=True))
    ).astype(jnp.bfloat16)
    grad_query_recall = (
        jnp.einsum(
            "bihk,bihkd->bihd",
            grad_recall_scores,
            rows_back[..., :head_size],
            preferred_element_type=jnp.float32,
        )
        * score_scale
    )
    window_again = jnp.exp(window_scores() - log_total)
    grad_window_weights = jnp.einsum(
        "bihd,bjhd->bhij",
        grad_local,
        value_four,
        precision=highest,
        preferred_element_type=jnp.float32,
    )
    grad_window_scores = (
        window_again
        * (
            grad_window_weights
            - jnp.sum(window_again * grad_window_weights, axis=-1, keepdims=True)
        )
    ).astype(jnp.bfloat16)
    distance_sums = diagonal_sums(jnp.sum(grad_window_scores.astype(jnp.float32), axis=0), W)
    bucket_onehot = (
        jnp.asarray(bucket_table(W, bucket_total))[:, None] == jnp.arange(bucket_total)[None, :]
    ).astype(jnp.float32)
    position_part = jnp.dot(distance_sums, bucket_onehot, precision=highest)
    grad_query_window = (
        jnp.einsum(
            "bhij,bjhd->bihd", grad_window_scores, key_four, preferred_element_type=jnp.float32
        )
        * score_scale
    )
    grad_key_window = (
        jnp.einsum(
            "bhij,bihd->bjhd", grad_window_scores, query_four, preferred_element_type=jnp.float32
        )
        * score_scale
    )
    grad_value_window = jnp.einsum(
        "bhij,bihd->bjhd",
        window_again.astype(jnp.bfloat16),
        grad_local,
        precision=highest,
        preferred_element_type=jnp.float32,
    )
    grad_pair = jnp.stack((grad_key_window, grad_value_window))

    def pair_piece(hop_index):
        return grad_pair[:, :, W - hop_index * block_len : W - hop_index * block_len + block_len]

    carried = pair_piece(hop_count)
    for hop_index in range(hop_count - 1, -1, -1):
        carried = from_behind(carried.astype(jnp.bfloat16), "seq", -1).astype(
            carried.dtype
        ) + pair_piece(hop_index)
    grad_keys = carried[0].reshape(batch_size, block_len, -1).astype(jnp.bfloat16)
    grad_values = carried[1].reshape(batch_size, block_len, -1).astype(jnp.bfloat16)
    grad_queries = (
        (grad_query_window + grad_query_recall)
        .reshape(batch_size, block_len, -1)
        .astype(jnp.bfloat16)
    )
    query_grad = jnp.einsum(
        "btd,bte->de", normed_one, grad_queries, preferred_element_type=jnp.float32
    )
    key_grad = jnp.einsum("btd,bte->de", normed_one, grad_keys, preferred_element_type=jnp.float32)
    value_grad = jnp.einsum(
        "btd,bte->de", normed_one, grad_values, preferred_element_type=jnp.float32
    )
    grad_normed_part = jnp.einsum(
        "bte,de->btd", grad_queries, query_weight, preferred_element_type=jnp.float32
    )
    grad_normed_part = grad_normed_part + jnp.einsum(
        "bte,de->btd", grad_keys, key_weight, preferred_element_type=jnp.float32
    )
    grad_normed_part = grad_normed_part + jnp.einsum(
        "bte,de->btd", grad_values, value_weight, preferred_element_type=jnp.float32
    )
    grad_normed_one = lax.psum(grad_normed_part, "head")
    first_gain_part = jnp.sum(grad_normed_one * hat_one, axis=(0, 1))
    input_grad = grad_middle + norm_back(grad_normed_one, first_gain, hat_one, scale_one)
    reduced = (
        lax.psum_scatter(query_grad, "seq", scatter_dimension=0, tiled=True),
        lax.psum_scatter(key_grad, "seq", scatter_dimension=0, tiled=True),
        lax.psum_scatter(value_grad, "seq", scatter_dimension=0, tiled=True),
        lax.psum_scatter(output_grad, "seq", scatter_dimension=1, tiled=True),
        lax.psum_scatter(up_grad, "seq", scatter_dimension=0, tiled=True),
        lax.psum_scatter(down_grad, "seq", scatter_dimension=1, tiled=True),
        lax.psum_scatter(first_gain_part, "seq", scatter_dimension=0, tiled=True),
        lax.psum_scatter(second_gain_part, "seq", scatter_dimension=0, tiled=True),
    )
    square_parts = jnp.stack(
        [
            jnp.sum(layer_sum * layer_sum),
            jnp.sum(branch_attn * branch_attn),
            jnp.sum(branch_feed * branch_feed),
        ]
    )
    position_grad, gate_grad, square_sums = lax.psum(
        (position_part, gate_part, square_parts), "seq"
    )
    entry_count = float(batch_size * block_len * model_width * lax.axis_size("seq"))
    rms_values = jnp.sqrt(square_sums / entry_count)
    return (
        layer_sum.astype(jnp.bfloat16),
        input_grad,
        reduced[0],
        reduced[1],
        reduced[2],
        reduced[3],
        reduced[4],
        reduced[5],
        reduced[6],
        reduced[7],
        position_grad,
        gate_grad,
        rms_values,
    )


def solution(mesh):
    in_specs = (
        P(None, "seq", None),
        P(None, "seq", None),
        P(None, "head"),
        P(None, "head"),
        P(None, "head"),
        P("head", None),
        P(None, "head"),
        P("head", None),
        P(),
        P(),
        P("head", None),
        P("head"),
        P("seq", "head", None),
        P(None, "seq", "head", None),
        P(),
    )
    out_specs = (
        P(None, "seq", None),
        P(None, "seq", None),
        P("seq", "head"),
        P("seq", "head"),
        P("seq", "head"),
        P("head", "seq"),
        P("seq", "head"),
        P("head", "seq"),
        P("seq"),
        P("seq"),
        P("head", None),
        P("head"),
        P(),
    )
    return jax.shard_map(
        per_device, mesh=mesh, in_specs=in_specs, out_specs=out_specs, check_vma=False
    )
```

profile of v0, /device:TPU:0, one launch (start us, length us, event | category | flops | bytes accessed | tf_op | source)
XLA Modules:
  0.0 1860.2 jit_solution(3940897175574714171)
XLA Ops:
  8.6 7.8 sort.19
  16.8 90.5 %gather_fusion.1 = s32[16384]{0:T(1024)S(1)} fusion(s32[16384]{0:T(1024)S(1)} %reshape.569, s32[16384]{0:T(1024)S(1)} %get-tuple-element.40), kind=kCustom, calls=%fused_computation.clone | custom fusion | bytes 196608 | tf_op jit(solution)/shard_map/jit(_take)/gather | solution.py:86
  108.0 7.3 all-to-all-start
  115.2 13.1 reshape.568
  128.4 65.3 %gather_fusion.2 = bf16[16384,256]{1,0:T(8,128)(2,1)} fusion(bf16[16384,256]{1,0:T(8,128)(2,1)} %reshape.568, s32[16384]{0:T(1024)S(1)} %broadcast_clamp_fusion.1), kind=kCustom, calls=%fused_computation.1.clone | custom fusion | bytes 16842752 | tf_op jit(solution)/shard_map/jit(_take)/gather | solution.py:105
  193.7 8.0 broadcast_select_fusion.1
  201.7 6.1 all-to-all-start.1
  210.7 4.6 collective-permute-start
  215.5 60.5 %scatter_custom_fusion = s32[16384]{0:T(1024)S(1)} fusion(s32[16384]{0:T(1024)S(1)} %get-tuple-element.39, s32[16384]{0:T(1024)S(1)} %iota.34, s32[]{:T(128)} %constant.83.clone.1), kind=kCustom, calls=%fused_computation.159 | custom fusion | bytes 65540 | tf_op jit(solution)/shard_map/scatter | solution.py:95
  282.1 73.0 %collective-permute-start.1 = (bf16[2,1,256,256]{3,2,1,0:T(8,128)(2,1)}, bf16[2,1,256,256]{3,2,1,0:T(8,128)(2,1)S(1)}, u32[]{:S(2)}, u32[]{:S(2)}) collective-permute-start(bf16[2,1,256,256]{3,2,1,0:T(8,128)(2,1)} %collective-permute-done), channel_id=1, source_target_pairs={{0,4},{4,8},{8,12},{12,16},{16,20},{20,24},{24,28},{1,5},{5,9},{9,... | collective-permute-start | bytes 786440 | tf_op jit(solution)/shard_map/ppermute | solution.py:21
  357.0 645.2 %gather_fusion = f32[196608,2]{1,0:T(8,128)} fusion(f32[2,32]{0,1:T(8,128)S(1)} %copy.69, s32[196608]{0:T(1024)S(1)} %broadcast_clamp_fusion), kind=kCustom, calls=%fused_computation.3 | custom fusion | bytes 3932160 | tf_op jit(solution)/shard_map/jit(_take)/gather | solution.py:159
  1002.3 55.6 %copy.101 = f32[256,768,2]{1,0,2:T(8,128)} copy(f32[256,768,2]{2,1,0:T(8,128)} %bitcast.16) | data formatting | bytes 3145728 | tf_op jit(solution)/shard_map/jit(_take)/gather | solution.py:159
  1064.9 65.3 %gather_fusion.3 = bf16[16384,256]{1,0:T(8,128)(2,1)} fusion(bf16[16384,256]{1,0:T(8,128)(2,1)} %bitcast.6, s32[16384]{0:T(1024)S(1)} %copy-done.38), kind=kCustom, calls=%fused_computation.2.clone | custom fusion | bytes 16842752 | tf_op jit(solution)/shard_map/jit(_take)/gather | solution.py:97
  1130.2 9.7 broadcast_select_fusion
  1146.7 4.7 multiply_reduce_fusion.2
  1156.1 78.5 %all-reduce.9.cloned.1.call-done = f32[1,256,1024]{2,1,0:T(8,128)} async-done(((f32[1,256,1024]{2,1,0:T(8,128)}), f32[1,256,1024]{2,1,0:T(8,128)}) %all-reduce.9.cloned.1.call-update) | async-done | bytes 1048592 | tf_op jit(solution)/shard_map/psum | solution.py:230
  1248.1 29.5 %all-reduce.11.cloned.1.call-done = bf16[1,256,1024]{2,1,0:T(8,128)(2,1)} async-done(((bf16[1,256,1024]{2,1,0:T(8,128)(2,1)}), bf16[1,256,1024]{2,1,0:T(8,128)(2,1)}) %all-reduce.11.cloned.1.call-update) | async-done | bytes 524304 | tf_op jit(solution)/shard_map/psum | solution.py:239
  1277.6 38.6 %all-reduce.13.cloned.1.call-done = f32[1,256,1024]{2,1,0:T(8,128)} async-done(((f32[1,256,1024]{2,1,0:T(8,128)}), f32[1,256,1024]{2,1,0:T(8,128)}) %all-reduce.13.cloned.1.call-update) | async-done | bytes 1048592 | tf_op jit(solution)/shard_map/psum | solution.py:250
  1332.4 5.4 multiply_reduce_fusion.1
  1340.6 5.5 multiply_reduce_fusion
  1352.7 8.4 collective-permute-done.3
  1374.2 3.8 fusion.93
  1379.3 3.9 fusion.55
  1385.1 8.9 rev.3
  1398.6 5.5 reshape.583
  1410.1 36.1 %all-reduce.3 = (f32[1024]{0:T(1024)S(1)}, f32[1024]{0:T(1024)S(1)}, f32[2,32]{1,0:T(2,128)}, f32[2]{0:T(128)}, f32[3]{0:T(128)S(1)}) all-reduce(f32[1024]{0:T(1024)S(1)} %get-tuple-element.20, f32[1024]{0:T(1024)S(1)} %copy-done.46, f32[2,32]{1,0:T(2,128)S(1)} %fusion.69, ...), channel_id=8, replica_groups=mesh['seq'=8,'head'=4] {'seq'}, use_global_device_ids=true, to_apply=%region_26.30.clone | all-reduce | flops 2117 | bytes 16936
  1450.7 18.4 reduce-scatter.13.cloned.1.call-done
  1469.1 66.4 %reduce-scatter.7.cloned.1.call-done = f32[128,256]{1,0:T(8,128)} async-done(((f32[1024,256]{1,0:T(8,128)}), f32[128,256]{1,0:T(8,128)}) %reduce-scatter.7.cloned.1.call-update) | async-done | bytes 131088 | tf_op jit(solution)/shard_map/reduce_scatter | solution.py:371
  1535.4 66.9 %reduce-scatter.11.cloned.1.call-done = f32[128,256]{1,0:T(8,128)} async-done(((f32[1024,256]{1,0:T(8,128)}), f32[128,256]{1,0:T(8,128)}) %reduce-scatter.11.cloned.1.call-update) | async-done | bytes 131088 | tf_op jit(solution)/shard_map/reduce_scatter | solution.py:373
  1602.4 66.4 %reduce-scatter.9.cloned.1.call-done = f32[128,256]{1,0:T(8,128)} async-done(((f32[1024,256]{1,0:T(8,128)}), f32[128,256]{1,0:T(8,128)}) %reduce-scatter.9.cloned.1.call-update) | async-done | bytes 131088 | tf_op jit(solution)/shard_map/reduce_scatter | solution.py:372
  1668.8 91.7 %reduce-scatter.15.cloned.1.call-done = f32[128,1024]{1,0:T(8,128)} async-done(((f32[1024,1024]{1,0:T(8,128)}), f32[128,1024]{1,0:T(8,128)}) %reduce-scatter.15.cloned.1.call-update) | async-done | bytes 524304 | tf_op jit(solution)/shard_map/reduce_scatter | solution.py:375
  1760.5 92.4 %reduce-scatter.17.cloned.1.call-done = f32[1024,128]{1,0:T(8,128)} async-done(((f32[1024,1024]{1,0:T(8,128)}), f32[1024,128]{1,0:T(8,128)}) %reduce-scatter.17.cloned.1.call-update) | async-done | bytes 524304 | tf_op jit(solution)/shard_map/reduce_scatter | solution.py:376
  (237 shorter events, 101.3 us)
Async XLA Ops:
  7.2 1231.6 %copy-start = (bf16[1024,1024]{1,0:T(8,128)(2,1)S(1)}, bf16[1024,1024]{1,0:T(8,128)(2,1)}, u32[]{:S(2)}) copy-start(bf16[1024,1024]{1,0:T(8,128)(2,1)} %param.31) | copy-start | bytes 6291460
  108.0 20.4 %all-to-all-start = ((s32[8,1,2048]{2,1,0:T(1,128)}), s32[8,1,2048]{2,1,0:T(1,128)S(1)}, u32[]{:S(2)}, u32[]{:S(2)}) async-start(s32[8,1,2048]{2,1,0:T(1,128)} %bitcast.4), calls=%async_computation | async-start | bytes 131072 | tf_op jit(solution)/shard_map/all_to_all | solution.py:109
  201.7 6.2 copy-start.4
  201.7 6.4 copy-start.33
  201.7 6.4 copy-start.40
  201.7 863.1 %all-to-all-start.1 = ((bf16[8,2048,256]{2,1,0:T(8,128)(2,1)}), bf16[8,2048,256]{2,1,0:T(8,128)(2,1)}, u32[]{:S(2)}, u32[]{:S(2)}) async-start(bf16[8,2048,256]{2,1,0:T(8,128)(2,1)} %broadcast_select_fusion.1), calls=%async_computation.1 | async-start | bytes 16777216 | tf_op jit(solution)/shard_map/all_to_all | solution.py:106
  207.9 7.4 copy-start.54
  207.9 1026.7 %all-reduce.9.cloned.1.call-start = ((), (), s32[]{:S(2)}) async-start(), calls=%async_computation.8 | async-start | bytes 2097152 | tf_op jit(solution)/shard_map/psum | solution.py:230
  210.7 71.4 %collective-permute-start = (bf16[2,1,256,256]{3,2,1,0:T(8,128)(2,1)}, bf16[2,1,256,256]{3,2,1,0:T(8,128)(2,1)}, u32[]{:S(2)}, u32[]{:S(2)}) collective-permute-start(bf16[2,1,256,256]{3,2,1,0:T(8,128)(2,1)} %pad_maximum_fusion.1), channel_id=1, source_target_pairs={{0,4},{4,8},{8,12},{12,16},{16,20},{20,24},{24,28},{1,5},{5,9},{9,... | collective-permute-start | bytes 786440 | tf_op jit(solution)/shard_map/ppermute | solution.py:21
  282.1 777.5 %collective-permute-start.1 = (bf16[2,1,256,256]{3,2,1,0:T(8,128)(2,1)}, bf16[2,1,256,256]{3,2,1,0:T(8,128)(2,1)S(1)}, u32[]{:S(2)}, u32[]{:S(2)}) collective-permute-start(bf16[2,1,256,256]{3,2,1,0:T(8,128)(2,1)} %collective-permute-done), channel_id=1, source_target_pairs={{0,4},{4,8},{8,12},{12,16},{16,20},{20,24},{24,28},{1,5},{5,9},{9,... | collective-permute-start | bytes 786440 | tf_op jit(solution)/shard_map/ppermute | solution.py:21
  1002.3 56.4 %copy-start.39 = (pred[256,768]{1,0:T(32,128)(4,1)S(1)}, pred[256,768]{1,0:T(32,128)(4,1)}, u32[]{:S(2)}) copy-start(pred[256,768]{1,0:T(32,128)(4,1)} %constant.145.clone) | copy-start | bytes 589828
  1002.3 57.3 %copy-start.30 = (bf16[1,1,256,256]{3,2,1,0:T(8,128)(2,1)S(1)}, bf16[1,1,256,256]{3,2,1,0:T(8,128)(2,1)}, u32[]{:S(2)}) copy-start(bf16[1,1,256,256]{3,2,1,0:T(8,128)(2,1)} %copy-done.29) | copy-start | bytes 393220
  1002.3 57.3 %copy-start.32 = (bf16[1,1,256,256]{3,2,1,0:T(8,128)(2,1)S(1)}, bf16[1,1,256,256]{3,2,1,0:T(8,128)(2,1)}, u32[]{:S(2)}) copy-start(bf16[1,1,256,256]{3,2,1,0:T(8,128)(2,1)} %copy-done.31) | copy-start | bytes 393220
  1061.0 90.7 %copy-start.21 = (bf16[768,2,128]{2,1,0:T(2,128)(2,1)}, bf16[768,2,128]{2,1,0:T(2,128)(2,1)S(1)}, u32[]{:S(2)}) copy-start(bf16[768,2,128]{2,1,0:T(2,128)(2,1)S(1)} %reshape.575) | copy-start | bytes 1179652
  1063.2 88.4 %copy-start.44 = (f32[2,256]{1,0:T(2,128)}, f32[2,256]{1,0:T(2,128)S(1)}, u32[]{:S(2)}) copy-start(f32[2,256]{1,0:T(2,128)S(1)} %get-tuple-element.43) | copy-start | bytes 6148
  1064.8 86.8 %copy-start.47 = (f32[2,256]{1,0:T(2,128)}, f32[2,256]{1,0:T(2,128)S(1)}, u32[]{:S(2)}) copy-start(f32[2,256]{1,0:T(2,128)S(1)} %fusion.8) | copy-start | bytes 6148
  1064.9 65.3 %copy-start.42 = (pred[16384]{0:T(1024)(128)(4,1)S(1)}, pred[16384]{0:T(1024)(128)(4,1)}, u32[]{:S(2)}) copy-start(pred[16384]{0:T(1024)(128)(4,1)} %compare_and_fusion.1) | copy-start | bytes 49156
  1130.2 12.9 copy-start.25
  1155.8 81.2 %copy-start.41 = (f32[1024]{0:T(1024)S(1)}, f32[1024]{0:T(1024)}, u32[]{:S(2)}) copy-start(f32[1024]{0:T(1024)} %param.33) | copy-start | bytes 12292
  1155.8 121.7 %all-reduce.11.cloned.1.call-start = ((), (), s32[]{:S(2)}) async-start(), calls=%async_computation.9 | async-start | bytes 1048576 | tf_op jit(solution)/shard_map/psum | solution.py:239
  1243.9 72.3 %all-reduce.13.cloned.1.call-start = ((), (), s32[]{:S(2)}) async-start(), calls=%async_computation.10 | async-start | bytes 2097152 | tf_op jit(solution)/shard_map/psum | solution.py:250
  1247.4 160.9 %all-reduce.15.cloned.1.call-start = ((), (), s32[]{:S(2)}) async-start(), calls=%async_computation.11 | async-start | bytes 2097152 | tf_op jit(solution)/shard_map/psum | solution.py:367
  1329.3 20.4 %collective-permute-start.2 = (bf16[2,1,256,2,128]{2,4,3,1,0:T(8,128)(2,1)}, bf16[2,1,256,2,128]{2,4,3,1,0:T(8,128)(2,1)}, u32[]{:S(2)}, u32[]{:S(2)}) collective-permute-start(bf16[2,1,256,2,128]{2,4,3,1,0:T(8,128)(2,1)} %fusion.50), channel_id=1, source_target_pairs={{4,0},{8,4},{12,8},{16,12},{20,16},{24,20},{28,24},{5,1},{9,5},{13... | collective-permute-start | bytes 786440 | tf_op jit(solution)/shard_map/ppermute | solution.py:21
  1350.7 10.4 collective-permute-start.3
  1352.3 8.9 copy-start.34
  1363.7 105.4 %reduce-scatter.13.cloned.1.call-start = ((), (), s32[]{:S(2)}) async-start(), calls=%async_computation.15 | async-start | bytes 1179648 | tf_op jit(solution)/shard_map/reduce_scatter | solution.py:374
  1366.4 169.0 %reduce-scatter.7.cloned.1.call-start = ((), (), s32[]{:S(2)}) async-start(), calls=%async_computation.12 | async-start | bytes 1179648 | tf_op jit(solution)/shard_map/reduce_scatter | solution.py:371
  1368.9 233.4 %reduce-scatter.11.cloned.1.call-start = ((), (), s32[]{:S(2)}) async-start(), calls=%async_computation.14 | async-start | bytes 1179648 | tf_op jit(solution)/shard_map/reduce_scatter | solution.py:373
  1371.6 297.2 %reduce-scatter.9.cloned.1.call-start = ((), (), s32[]{:S(2)}) async-start(), calls=%async_computation.13 | async-start | bytes 1179648 | tf_op jit(solution)/shard_map/reduce_scatter | solution.py:372
  1374.2 386.4 %reduce-scatter.15.cloned.1.call-start = ((), (), s32[]{:S(2)}) async-start(), calls=%async_computation.16 | async-start | bytes 4718592 | tf_op jit(solution)/shard_map/reduce_scatter | solution.py:375
  1378.1 474.8 %reduce-scatter.17.cloned.1.call-start = ((), (), s32[]{:S(2)}) async-start(), calls=%async_computation.17 | async-start | bytes 4718592 | tf_op jit(solution)/shard_map/reduce_scatter | solution.py:376
  1404.1 6.0 copy-start.46
  (41 other events, 100.8 us)
Sparse Core Ops, SparseCore 0:
  1156.0 78.5 all-reduce.8
  1244.0 33.5 all-reduce.10
  1280.1 36.0 all-reduce.12
  1363.8 37.0 all-reduce.14
  1405.1 63.9 reduce-scatter.12
  1472.9 62.4 reduce-scatter.6
  1539.8 62.5 reduce-scatter.10
  1606.3 62.4 reduce-scatter.8
  1673.4 87.0 reduce-scatter.14
  1764.6 88.2 reduce-scatter.16
where the time goes:
time: 1870 us; the launch traced here: 1860 us
  local copies, waits for them, and re-layouts  1040 us (56%)
  waiting for transfers between devices  559 us (30%)
  starting transfers between devices  94.4 us (5%)
  other arithmetic  73.3 us (4%)
  matrix products  45.9 us (2%)
  blocking collectives  36.1 us (2%)
    gather x2, local copies, waits for them, and re-layouts, per_device(): bias_full = jnp.take(position_bias, jnp.asarray(bucket_index), axis=1)[None]  701 us
    reduce_scatter x1, waiting for transfers between devices, per_device(): lax.psum_scatter(down_grad, 'seq', scatter_dimension=1, tiled=True)  92.4 us
    reduce_scatter x1, waiting for transfers between devices, per_device(): lax.psum_scatter(up_grad, 'seq', scatter_dimension=0, tiled=True)  91.7 us
    gather x1, local copies, waits for them, and re-layouts, request_order(): jnp.take(slot_codes.reshape(-1), sort_order).reshape(device_count, -1)  90.5 us
    ppermute x4, starting transfers between devices, from_behind(): lax.ppermute(value, axis, [(source, source + steps) for source in range(f...  80.3 us
    psum x1, waiting for transfers between devices, per_device(): lax.psum(jnp.dot(mixed, output_weight, preferred_element_type=jnp.float32...  78.5 us
    reduce_scatter x1, waiting for transfers between devices, per_device(): lax.psum_scatter(value_grad, 'seq', scatter_dimension=0, tiled=True)  66.9 us
    reduce_scatter x1, waiting for transfers between devices, per_device(): lax.psum_scatter(key_grad, 'seq', scatter_dimension=0, tiled=True)  66.4 us
  transfers between devices with their start and end apart: 16, of which 11 were waited for; matrix products, arithmetic and copies ran while one was open for 46% of the time, Pallas kernels for 0%

commit v1 on v0

v1 whole, which is shorter than its diff:
```python
import functools
import math

import jax
import jax.numpy as jnp
import numpy as np
from jax import lax
from jax.experimental import pallas as pl
from jax.experimental.pallas import tpu as pltpu
from jax.sharding import PartitionSpec as P

W = 512
eps = 1e-06
exact_span = 16
far_distance = 128
highest = lax.Precision.HIGHEST
f32 = jnp.float32
bf16 = jnp.bfloat16
NEG = -1e30
MIB = 2**20


def bucket_table(key_span, bucket_total):
    found = []
    for distance in range(key_span):
        if distance < exact_span:
            found.append(distance)
        else:
            scaled = math.log(distance / exact_span) / math.log(far_distance / exact_span)
            found.append(
                min(bucket_total - 1, exact_span + math.floor(scaled * (bucket_total - exact_span)))
            )
    return np.asarray(found)


def diagonal_buckets(block_len, bucket_total):
    span = W + block_len
    table = bucket_table(W, bucket_total)
    hot = np.zeros((bucket_total, span), np.float32)
    for u in range(1, W + 1):
        hot[table[W - u], u] = 1.0
    outside = np.where(hot.sum(0) > 0, 0.0, NEG).astype(np.float32)
    return hot, outside


def nt(a, b):
    return lax.dot_general(a, b, (((1,), (1,)), ((), ())), preferred_element_type=f32)


def nn(a, b):
    return lax.dot_general(a, b, (((1,), (0,)), ((), ())), preferred_element_type=f32)


def tn(a, b):
    return lax.dot_general(a, b, (((0,), (0,)), ((), ())), preferred_element_type=f32)


def gather_kernel(codes_ref, table_ref, out_ref, wide, buf, *, rows, chunk, chunks, unroll, group):
    step = pl.program_id(0)
    part = 32

    @pl.when(step < chunks)
    def _():
        def widen(q, carry):
            x = table_ref[pl.ds(q * part, part)].astype(f32)
            base = step * chunk + q * part
            for r in range(part):
                wide[pl.ds(4 * (base + r), 2), :] = x[r, :, 0:128]
                wide[pl.ds(4 * (base + r) + 2, 2), :] = x[r, :, 128:256]
            return carry

        lax.fori_loop(0, chunk // part, widen, 0)

    @pl.when(step >= chunks)
    def _():
        head = (step - chunks) % 2

        def copy_rows(i, carry):
            base = i * unroll
            for g in range(0, unroll, group):
                found = [
                    wide[pl.ds(codes_ref[0, 0, 0, base + g + u] * 4 + head, 2, 2), :]
                    for u in range(group)
                ]
                for u in range(group):
                    buf[pl.ds(2 * (base + g + u), 2), :] = found[u]
            return carry

        lax.fori_loop(0, rows // unroll, copy_rows, 0)
        out_ref[0, 0, :, 0:128] = buf[pl.ds(0, rows, 2), :].astype(bf16)
        out_ref[0, 0, :, 128:256] = buf[pl.ds(1, rows, 2), :].astype(bf16)


def gather_rows(slots, table):
    parts, heads, rows = slots.shape
    total = table.shape[0]
    chunk = min(1024, total)
    chunks = total // chunk
    unroll = min(64, rows)

    def place(i):
        at = jnp.maximum(i - chunks, 0)
        return (at // 2, at % 2, 0, 0)

    return pl.pallas_call(
        functools.partial(
            gather_kernel, rows=rows, chunk=chunk, chunks=chunks, unroll=unroll, group=unroll // 2
        ),
        out_shape=jax.ShapeDtypeStruct((parts, heads, rows, 256), bf16),
        grid=(chunks + parts * heads,),
        in_specs=[
            pl.BlockSpec((1, 1, 1, rows), place, memory_space=pltpu.SMEM),
            pl.BlockSpec((chunk, 2, 256), lambda i: (jnp.minimum(i, chunks - 1), 0, 0)),
        ],
        out_specs=pl.BlockSpec((1, 1, rows, 256), place),
        scratch_shapes=[pltpu.VMEM((4 * total, 128), f32), pltpu.VMEM((2 * rows, 128), f32)],
        compiler_params=pltpu.CompilerParams(vmem_limit_bytes=40 * MIB),
        cost_estimate=pl.CostEstimate(flops=0, bytes_accessed=100 * MIB, transcendentals=0),
        name="gather_rows",
    )(slots.reshape(parts, heads, 1, rows), table)


def recall_fwd_kernel(q_ref, rows_ref, tok_ref, o_ref, st_ref, *, scale):
    count, rows = q_ref.shape[1], rows_ref.shape[2]
    ids = lax.broadcasted_iota(jnp.int32, (count, rows), 0)
    logs = []
    for h in range(2):
        cols = slice(h * 128, h * 128 + 128)
        keep = tok_ref[0, h : h + 1, :] == ids
        s = jnp.where(keep, nt(q_ref[0, :, cols], rows_ref[0, h, :, 0:128]) * scale, NEG)
        top = jnp.max(s, axis=1, keepdims=True)
        p = jnp.where(keep, jnp.exp(s - top), 0.0)
        total = jnp.sum(p, axis=1, keepdims=True)
        some = total > 0.0
        safe = jnp.where(some, total, 1.0)
        o = nn(p.astype(bf16), rows_ref[0, h, :, 128:256]) / safe
        o_ref[0, h] = o.astype(bf16)
        logs.append(jnp.where(some, top + jnp.log(safe), NEG))
    lane = lax.broadcasted_iota(jnp.int32, (count, 128), 1)
    st_ref[0] = jnp.where(lane == 0, logs[0], logs[1]).T[0:8]


def recall_fwd(q_all, rows, tok):
    parts, count, width = q_all.shape
    per = rows.shape[2]
    return pl.pallas_call(
        functools.partial(recall_fwd_kernel, scale=128**-0.5),
        out_shape=(
            jax.ShapeDtypeStruct((parts, 2, count, 128), bf16),
            jax.ShapeDtypeStruct((parts, 8, count), f32),
        ),
        grid=(parts,),
        in_specs=[
            pl.BlockSpec((1, count, width), lambda i: (i, 0, 0)),
            pl.BlockSpec((1, 2, per, 256), lambda i: (i, 0, 0, 0)),
            pl.BlockSpec((1, 2, per), lambda i: (i, 0, 0)),
        ],
        out_specs=(
            pl.BlockSpec((1, 2, count, 128), lambda i: (i, 0, 0, 0)),
            pl.BlockSpec((1, 8, count), lambda i: (i, 0, 0)),
        ),
        compiler_params=pltpu.CompilerParams(vmem_limit_bytes=40 * MIB),
        name="recall_fwd",
    )(q_all, rows, tok)


def recall_bwd_kernel(gate_ref, q_ref, g_ref, st_ref, rows_ref, tok_ref, dq_ref, *, scale):
    count, rows = q_ref.shape[1], rows_ref.shape[2]
    ids = lax.broadcasted_iota(jnp.int32, (count, rows), 0)
    stats = st_ref[0].T
    for h in range(2):
        cols = slice(h * 128, h * 128 + 128)
        keep = tok_ref[0, h : h + 1, :] == ids
        s = nt(q_ref[0, :, cols], rows_ref[0, h, :, 0:128]) * scale
        p = jnp.exp(jnp.where(keep, s - stats[:, h : h + 1], NEG))
        e = nt(g_ref[0, :, cols], rows_ref[0, h, :, 128:256]) * gate_ref[h]
        ds = (p * (e - stats[:, 2 + h : 3 + h])).astype(bf16)
        dq_ref[0, h] = (nn(ds, rows_ref[0, h, :, 0:128]) * scale).astype(bf16)


def recall_bwd(gate, q_all, g_all, stats, rows, tok):
    parts, count, width = q_all.shape
    per = rows.shape[2]
    return pl.pallas_call(
        functools.partial(recall_bwd_kernel, scale=128**-0.5),
        out_shape=jax.ShapeDtypeStruct((parts, 2, count, 128), bf16),
        grid=(parts,),
        in_specs=[
            pl.BlockSpec(memory_space=pltpu.SMEM),
            pl.BlockSpec((1, count, width), lambda i: (i, 0, 0)),
            pl.BlockSpec((1, count, width), lambda i: (i, 0, 0)),
            pl.BlockSpec((1, 8, count), lambda i: (i, 0, 0)),
            pl.BlockSpec((1, 2, per, 256), lambda i: (i, 0, 0, 0)),
            pl.BlockSpec((1, 2, per), lambda i: (i, 0, 0)),
        ],
        out_specs=pl.BlockSpec((1, 2, count, 128), lambda i: (i, 0, 0, 0)),
        compiler_params=pltpu.CompilerParams(vmem_limit_bytes=40 * MIB),
        name="recall_bwd",
    )(gate, q_all, g_all, stats, rows, tok)


def doc_starts(lengths_ref, first, count):
    place = first + lax.broadcasted_iota(jnp.int32, (count, 1), 0)
    start = jnp.zeros((count, 1), jnp.int32)
    end = jnp.int32(0)
    for c in range(lengths_ref.shape[0]):
        end = end + lengths_ref[c]
        start = jnp.where(end <= place, end, start)
    return start


def window_fwd_kernel(place_ref, lengths_ref, q_ref, k_ref, v_ref, bias_ref, o_ref, p_ref, *, scale):
    count, span = q_ref.shape[0], k_ref.shape[0]
    first = place_ref[0] * count
    start = doc_starts(lengths_ref, first, count)
    key_place = first - W + lax.broadcasted_iota(jnp.int32, (count, span), 1)
    seen = key_place >= start
    for h in range(2):
        cols = slice(h * 128, h * 128 + 128)
        bias = pltpu.roll(
            jnp.broadcast_to(bias_ref[h : h + 1, :], (count, span)), 0, 1, stride=1, stride_axis=0
        )
        s = nt(q_ref[:, cols], k_ref[:, cols]) * scale + bias
        s = jnp.where(seen, s, NEG)
        top = jnp.max(s, axis=1, keepdims=True)
        raised = jnp.exp(s - top)
        p = raised / jnp.sum(raised, axis=1, keepdims=True)
        p_ref[h] = p
        o_ref[:, cols] = nn(p.astype(bf16), v_ref[:, cols])


def window_fwd(place, lengths, q, k, v, bias):
    count, span = q.shape[0], k.shape[0]
    smem = pl.BlockSpec(memory_space=pltpu.SMEM)
    vmem = pl.BlockSpec(memory_space=pltpu.VMEM)
    return pl.pallas_call(
        functools.partial(window_fwd_kernel, scale=128**-0.5),
        out_shape=(
            jax.ShapeDtypeStruct((count, 256), f32),
            jax.ShapeDtypeStruct((2, count, span), f32),
        ),
        in_specs=[smem, smem, vmem, vmem, vmem, vmem],
        out_specs=(vmem, vmem),
        compiler_params=pltpu.CompilerParams(vmem_limit_bytes=40 * MIB),
        name="window_fwd",
    )(place, lengths, q, k, v, bias)


def window_bwd_kernel(gate_ref, p_ref, g_ref, q_ref, k_ref, v_ref, dq_ref, dk_ref, dv_ref, pos_ref, *, scale):
    count, span = q_ref.shape[0], k_ref.shape[0]
    for h in range(2):
        cols = slice(h * 128, h * 128 + 128)
        rest = 1.0 - gate_ref[h]
        p = p_ref[h]
        e = nt(g_ref[:, cols], v_ref[:, cols]) * rest
        delta = jnp.sum(p * e, axis=1, keepdims=True)
        ds = (p * (e - delta)).astype(bf16)
        dq_ref[:, cols] = nn(ds, k_ref[:, cols]) * scale
        dk_ref[:, cols] = tn(ds, q_ref[:, cols]) * scale
        dv_ref[:, cols] = tn(p.astype(bf16), g_ref[:, cols]) * rest
        low = ds.astype(f32)
        acc = low[0:8]
        for a in range(1, count // 8):
            acc = acc + pltpu.roll(low[8 * a : 8 * a + 8], (span - 8 * a) % span, 1)
        row = acc[0:1]
        for b in range(1, 8):
            row = row + pltpu.roll(acc[b : b + 1], span - b, 1)
        pos_ref[h : h + 1, :] = row


def window_bwd(gate, p, g, q, k, v):
    count, span = q.shape[0], k.shape[0]
    smem = pl.BlockSpec(memory_space=pltpu.SMEM)
    vmem = pl.BlockSpec(memory_space=pltpu.VMEM)
    return pl.pallas_call(
        functools.partial(window_bwd_kernel, scale=128**-0.5),
        out_shape=(
            jax.ShapeDtypeStruct((count, 256), f32),
            jax.ShapeDtypeStruct((span, 256), f32),
            jax.ShapeDtypeStruct((span, 256), f32),
            jax.ShapeDtypeStruct((2, span), f32),
        ),
        in_specs=[smem] + [vmem] * 5,
        out_specs=(vmem,) * 4,
        compiler_params=pltpu.CompilerParams(vmem_limit_bytes=40 * MIB),
        name="window_bwd",
    )(gate, p, g, q, k, v)


def from_behind(value, axis, steps):
    count = lax.axis_size(axis)
    first, last = (max(0, -steps), min(count, count - steps))
    return lax.ppermute(value, axis, [(source, source + steps) for source in range(first, last)])


def norm_stats(values):
    row_scale = lax.rsqrt(jnp.mean(values * values, axis=-1, keepdims=True) + eps)
    return (values * row_scale, row_scale)


def norm_back(grad_normed, gain, normed_hat, row_scale):
    grad_hat = grad_normed * gain
    inner = jnp.mean(grad_hat * normed_hat, axis=-1, keepdims=True)
    return row_scale * (grad_hat - normed_hat * inner)


def exchange(value):
    return lax.all_to_all(value, "seq", split_axis=0, concat_axis=0, tiled=True)


def head_sum(value):
    return lax.psum(value.astype(bf16), "head").astype(f32)


def per_device(
    inputs,
    cotangent,
    query_weight,
    key_weight,
    value_weight,
    output_weight,
    up_weight,
    down_weight,
    first_gain,
    second_gain,
    position_bias,
    gate_bias,
    memory_table,
    retrieved,
    lengths,
):
    _, block_len, model_width = inputs.shape
    bucket_total = position_bias.shape[1]
    hop_count = W // block_len
    seq_count = lax.axis_size("seq")
    place = lax.axis_index("seq").astype(jnp.int32).reshape(1)
    slot_count = memory_table.shape[0]

    wanted = jnp.transpose(retrieved[0], (1, 0, 2))
    token = jnp.arange(block_len, dtype=jnp.int32)[None, :, None]
    codes = (wanted // slot_count) * (block_len * slot_count) + token * slot_count + wanted % slot_count
    codes = lax.sort(codes.reshape(2, -1), dimension=1, is_stable=False)
    codes = jnp.transpose(codes.reshape(2, seq_count, -1), (1, 0, 2))
    codes = exchange(codes)
    slots = codes % slot_count
    tok = (codes // slot_count) % block_len
    rows = gather_rows(slots, memory_table)

    hot, outside = diagonal_buckets(block_len, bucket_total)
    bias_row = jnp.dot(position_bias, hot, precision=highest) + outside[None]

    tokens = inputs[0].astype(f32)
    cot = cotangent[0]
    hat_one, scale_one = norm_stats(tokens)
    normed_one = (hat_one * first_gain).astype(bf16)
    queries = nn(normed_one, query_weight).astype(bf16)
    keys = nn(normed_one, key_weight).astype(bf16)
    values = nn(normed_one, value_weight).astype(bf16)
    q_all = lax.all_gather(queries, "seq", axis=0)
    pair = jnp.stack((keys, values))
    pieces = [pair] + [from_behind(pair, "seq", hop) for hop in range(1, hop_count + 1)]
    pair_window = jnp.concatenate(pieces[::-1], axis=1)
    key_window, value_window = pair_window[0], pair_window[1]

    local_out, window_weights = window_fwd(place, lengths[0], queries, key_window, value_window, bias_row)

    part_out, part_log = recall_fwd(q_all, rows, tok)
    got_out = exchange(part_out)
    got_log = exchange(part_log)[:, 0:2]
    log_total = jax.nn.logsumexp(got_log, axis=0)
    shares = jnp.exp(got_log - log_total[None])
    recalled = jnp.sum(shares[..., None] * got_out.astype(f32), axis=0)
    recalled = jnp.transpose(recalled, (1, 0, 2)).reshape(block_len, 256)

    gate_flat = jax.nn.sigmoid(gate_bias)
    gate_wide = jnp.repeat(gate_flat, 128)[None]
    mixed = (gate_wide * recalled + (1.0 - gate_wide) * local_out).astype(bf16)
    branch_attn = head_sum(nn(mixed, output_weight))
    middle = tokens + branch_attn
    hat_two, scale_two = norm_stats(middle)
    normed_two = (hat_two * second_gain).astype(bf16)
    upward = nn(normed_two, up_weight)
    gelu_value, gelu_back = jax.vjp(jax.nn.gelu, upward)
    hidden = gelu_value.astype(bf16)
    branch_feed = head_sum(nn(hidden, down_weight))
    layer_sum = middle + branch_feed
    grad_upward = gelu_back(nt(cot, down_weight))[0].astype(bf16)
    grad_normed_two = head_sum(nt(grad_upward, up_weight))
    feed_grads = jnp.concatenate((tn(normed_two, grad_upward), tn(cot, hidden)), axis=1).astype(bf16)
    feed_grads = lax.psum_scatter(feed_grads, "seq", scatter_dimension=0, tiled=True).astype(f32)

    second_gain_part = jnp.sum(grad_normed_two * hat_two, axis=0)
    grad_middle = cot.astype(f32) + norm_back(grad_normed_two, second_gain, hat_two, scale_two)
    grad_branch = grad_middle.astype(bf16)
    grad_mixed = nt(grad_branch, output_weight).astype(bf16)
    grad_wide = grad_mixed.astype(f32)
    gate_part = jnp.sum((grad_wide * (recalled - local_out)).reshape(block_len, 2, 128), axis=(0, 2))
    gate_part = gate_part * gate_flat * (1.0 - gate_flat)
    delta = jnp.sum((grad_wide * gate_wide * recalled).reshape(block_len, 2, 128), axis=2).T
    stats = jnp.concatenate((log_total, delta, jnp.zeros((4, block_len), f32)), axis=0)
    g_all = lax.all_gather(grad_mixed, "seq", axis=0)
    stats_all = lax.all_gather(stats, "seq", axis=0)

    dq_window, dk_window, dv_window, pos_rows = window_bwd(
        gate_flat, window_weights, grad_mixed, queries, key_window, value_window
    )
    grad_pair = jnp.stack((dk_window, dv_window))
    own = grad_pair[:, W:]
    for hop in range(1, hop_count + 1):
        piece = grad_pair[:, W - hop * block_len : W - (hop - 1) * block_len].astype(bf16)
        own = own + from_behind(piece, "seq", -hop).astype(f32)
    grad_keys, grad_values = own[0].astype(bf16), own[1].astype(bf16)

    dq_parts = exchange(recall_bwd(gate_flat, q_all, g_all, stats_all, rows, tok))
    dq_recall = jnp.transpose(jnp.sum(dq_parts.astype(f32), axis=0), (1, 0, 2)).reshape(block_len, 256)
    grad_queries = (dq_window + dq_recall).astype(bf16)

    attn_grads = jnp.concatenate(
        (
            tn(normed_one, grad_queries),
            tn(normed_one, grad_keys),
            tn(normed_one, grad_values),
            tn(grad_branch, mixed),
        ),
        axis=1,
    ).astype(bf16)
    attn_grads = lax.psum_scatter(attn_grads, "seq", scatter_dimension=0, tiled=True).astype(f32)
    grad_normed_one = head_sum(
        nt(grad_queries, query_weight) + nt(grad_keys, key_weight) + nt(grad_values, value_weight)
    )
    first_gain_part = jnp.sum(grad_normed_one * hat_one, axis=0)
    input_grad = grad_middle + norm_back(grad_normed_one, first_gain, hat_one, scale_one)

    position_part = jnp.dot(pos_rows, hot.T, precision=highest)
    square_parts = jnp.stack(
        [
            jnp.sum(layer_sum * layer_sum),
            jnp.sum(branch_attn * branch_attn),
            jnp.sum(branch_feed * branch_feed),
        ]
    )
    position_grad, gate_grad, square_sums, gain_sums = lax.psum(
        (position_part, gate_part, square_parts, jnp.stack((first_gain_part, second_gain_part))), "seq"
    )
    entry_count = float(block_len * model_width * seq_count)
    share = model_width // seq_count
    own_gains = lax.dynamic_slice_in_dim(gain_sums, place[0] * share, share, 1)
    return (
        layer_sum.astype(bf16)[None],
        input_grad[None],
        attn_grads[:, 0:256],
        attn_grads[:, 256:512],
        attn_grads[:, 512:768],
        attn_grads[:, 768:1024].T,
        feed_grads[:, : up_weight.shape[1]],
        feed_grads[:, up_weight.shape[1] :].T,
        own_gains[0],
        own_gains[1],
        position_grad,
        gate_grad,
        jnp.sqrt(square_sums / entry_count),
    )


def solution(mesh):
    in_specs = (
        P(None, "seq", None),
        P(None, "seq", None),
        P(None, "head"),
        P(None, "head"),
        P(None, "head"),
        P("head", None),
        P(None, "head"),
        P("head", None),
        P(),
        P(),
        P("head", None),
        P("head"),
        P("seq", "head", None),
        P(None, "seq", "head", None),
        P(),
    )
    out_specs = (
        P(None, "seq", None),
        P(None, "seq", None),
        P("seq", "head"),
        P("seq", "head"),
        P("seq", "head"),
        P("head", "seq"),
        P("seq", "head"),
        P("head", "seq"),
        P("seq"),
        P("seq"),
        P("head", None),
        P("head"),
        P(),
    )
    return jax.shard_map(
        per_device, mesh=mesh, in_specs=in_specs, out_specs=out_specs, check_vma=False
    )
```

time: 1870 us -> 510 us (0.27)
  local copies, waits for them, and re-layouts: 1040 us -> 53.7 us
  waiting for transfers between devices: 559 us -> 226 us
  starting transfers between devices: 94.4 us -> 30 us
  Pallas kernels: 0 us -> 63.5 us
  other arithmetic: 73.3 us -> 24.9 us
  blocking collectives: 36.1 us -> 69 us
  matrix products: 45.9 us -> 25 us
    gather x5 -> x0, local copies, waits for them, and re-layouts: 922 us -> none  [the longest x2 701 us: per_device(): bias_full = jnp.take(position_bias, jnp.asarray(bucket_index), axis=1)[None]]
    reduce_scatter x6 -> x0, waiting for transfers between devices: 402 us -> none  [the longest x1 92.4 us: per_device(): lax.psum_scatter(down_grad, 'seq', scatter_dimension=1, tiled=True)]
    unnamed x10 -> x9, waiting for transfers between devices: 0.16 us -> 89.5 us
    ppermute x4, starting transfers between devices: 80.3 us -> 10 us  [from_behind(): lax.ppermute(value, axis, [(source, source + steps) for source in range(f...]
    pallas_call x0 -> x5, Pallas kernels: none -> 63.5 us  [the longest x1 34.5 us: gather_rows(): pl.pallas_call(functools.partial(gather_kernel, rows=rows, chunk=chunk, c...]
    psum x4 -> x3, waiting for transfers between devices: 147 us -> 83.1 us  [head_sum(): return lax.psum(value.astype(bf16), 'head').astype(f32)]
    scatter x1 -> x0, local copies, waits for them, and re-layouts: 60.5 us -> none  [restore_order(): positions_back = jnp.zeros_like(sort_order).at[sort_order].set(jnp.arange...]
    psum x0 -> x1, blocking collectives: none -> 38.2 us  [per_device(): lax.psum((position_part, gate_part, square_parts, jnp.stack((first_gain_p...]
  transfers between devices with their start and end apart: 16 -> 15, of which waited for: 11 -> 10; matrix products, arithmetic and copies ran while one was open for 46% -> 8% of each run, Pallas kernels for 0% -> 10%
where the time goes in v1:
time: 510 us; the launch traced here: 508 us
  waiting for transfers between devices  226 us (44%)
  blocking collectives  69 us (14%)
  Pallas kernels  63.5 us (12%)
  local copies, waits for them, and re-layouts  53.7 us (11%)
  starting transfers between devices  30 us (6%)
  matrix products  25 us (5%)
  other arithmetic  24.9 us (5%)
  between operations  16.1 us (3%)
    unnamed x9, waiting for transfers between devices  89.5 us
    psum x3, waiting for transfers between devices, head_sum(): return lax.psum(value.astype(bf16), 'head').astype(f32)  83.1 us
    psum x1, blocking collectives, per_device(): lax.psum((position_part, gate_part, square_parts, jnp.stack((first_gain_p...  38.2 us
    unnamed x89, local copies, waits for them, and re-layouts  34.8 us
    pallas_call x1, Pallas kernels, gather_rows(): pl.pallas_call(functools.partial(gather_kernel, rows=rows, chunk=chunk, c...  34.5 us
    all_gather x1, blocking collectives, per_device(): stats_all = lax.all_gather(stats, 'seq', axis=0)  30.8 us
    all_to_all x4, waiting for transfers between devices, exchange(): return lax.all_to_all(value, 'seq', split_axis=0, concat_axis=0, tiled=True)  26.5 us
    all_to_all x4, starting transfers between devices, exchange(): return lax.all_to_all(value, 'seq', split_axis=0, concat_axis=0, tiled=True)  19.5 us
  transfers between devices with their start and end apart: 15, of which 10 were waited for; matrix products, arithmetic and copies ran while one was open for 8% of the time, Pallas kernels for 10%

profile of v1, /device:TPU:0, one launch (start us, length us, event | category | flops | bytes accessed | tf_op | source)
XLA Modules:
  0.0 507.8 jit_solution(17400316373574077186)
XLA Ops:
  15.5 13.6 %sort.9.cloned.1.call-done = s32[2,8192]{1,0:T(2,128)} async-done(((s32[2,8192]{1,0:T(2,128)}), s32[2,8192]{1,0:T(2,128)}) %sort.9.cloned.1.call-update) | async-done | bytes 65552 | tf_op jit(solution)/shard_map/sort | solution.py:342
  29.1 7.2 %all-to-all-start = ((s32[8,2,1024]{2,1,0:T(2,128)}), s32[8,2,1024]{2,1,0:T(2,128)S(1)}, u32[]{:S(2)}, u32[]{:S(2)}) async-start(s32[8,2,1024]{2,1,0:T(2,128)} %bitcast.219), calls=%async_computation | async-start | bytes 131072 | tf_op jit(solution)/shard_map/all_to_all | solution.py:308
  36.4 3.9 collective-permute-start
  40.3 3.4 collective-permute-start.1
  44.1 34.5 %gather_rows.1.rows_ref = bf16[8,2,1024,256]{3,2,1,0:T(8,128)(2,1)S(1)} custom-call(s32[8,2,1,1024]{3,2,1,0:T(1,128)S(1)} %copy.55.codes_ref, bf16[8192,2,256]{2,1,0:T(2,128)(2,1)} %table_ref.1), custom_call_target="tpu_custom_call" | custom-call | bytes 104857600 | tf_op jit(solution)/shard_map/gather_rows/pallas_call | solution.py:105
  78.7 3.2 copy-done.2
  81.9 3.4 copy-done.3
  86.5 12.6 %recall_fwd.1 = (bf16[8,2,256,128]{3,2,1,0:T(8,128)(2,1)}, f32[8,8,256]{2,1,0:T(8,128)}) custom-call(bf16[8,256,256]{2,1,0:T(8,128)(2,1)S(1)} %bitcast.209, bf16[8,2,1024,256]{3,2,1,0:T(8,128)(2,1)S(1)} %copy-done.3, s32[8,2,1024]{2,1,0:T(2,128)S(1)} %get-tuple-element.104.tok_ref), custom_call_target="tpu_custom_call" | custom-call | tf_op jit(solution)/shard_map/recall_fwd/pallas_call | solution.py:146
  99.1 3.8 all-to-all-start.1
  102.9 6.9 %all-to-all-done.1 = f32[8,8,256]{2,1,0:T(8,128)S(1)} async-done(((f32[8,8,256]{2,1,0:T(8,128)}), f32[8,8,256]{2,1,0:T(8,128)S(1)}, u32[]{:S(2)}, u32[]{:S(2)}) %all-to-all-start.1) | async-done | bytes 65568 | tf_op jit(solution)/shard_map/all_to_all | solution.py:308
  109.8 4.2 all-to-all-start.2
  118.2 19.6 %all-to-all-done.2 = bf16[8,2,256,128]{3,2,1,0:T(8,128)(2,1)} async-done(((bf16[8,2,256,128]{3,2,1,0:T(8,128)(2,1)}), bf16[8,2,256,128]{3,2,1,0:T(8,128)(2,1)}, u32[]{:S(2)}, u32[]{:S(2)}) %all-to-all-start.2) | async-done | bytes 1048608 | tf_op jit(solution)/shard_map/all_to_all | solution.py:308
  141.5 32.2 %all-reduce.6.cloned.1.call-done = bf16[256,1024]{1,0:T(8,128)(2,1)} async-done(((bf16[256,1024]{1,0:T(8,128)(2,1)}), bf16[256,1024]{1,0:T(8,128)(2,1)}) %all-reduce.6.cloned.1.call-update) | async-done | bytes 524304 | tf_op jit(solution)/shard_map/psum | solution.py:312
  183.4 36.1 %all-reduce.10.cloned.1.call-done = (bf16[256,1024]{1,0:T(8,128)(2,1)}, bf16[256,1024]{1,0:T(8,128)(2,1)}) async-done(((bf16[256,1024]{1,0:T(8,128)(2,1)}, bf16[256,1024]{1,0:T(8,128)(2,1)}), (bf16[256,1024]{1,0:T(8,128)(2,1)}, bf16[256,1024]{1,0:T(8,128)(2,1)})) %all-reduce.10.cloned.1.call-update) | async-done | bytes 1048592 | tf_op jit(solution)/shard_map/psum | solution.py:312
  219.5 3.4 fusion.23
  222.9 2.7 fusion.50
  227.3 30.8 %all-gather.2 = f32[64,256]{1,0:T(8,128)S(1)} all-gather(f32[8,256]{1,0:T(8,128)S(1)} %maximum_maximum_fusion.1), channel_id=4, replica_groups=mesh['seq'=8,'head'=4] {'seq'}, dimensions={0}, use_global_device_ids=true | all-gather | bytes 73728 | tf_op jit(solution)/shard_map/all_gather | solution.py:402
  258.0 8.5 %all-gather.8.cloned.1.call-done = bf16[2048,256]{1,0:T(8,128)(2,1)} async-done(((bf16[256,256]{1,0:T(8,128)(2,1)}), bf16[2048,256]{1,0:T(8,128)(2,1)}) %all-gather.8.cloned.1.call-update) | async-done | bytes 1048592 | tf_op jit(solution)/shard_map/all_gather | solution.py:401
  266.5 3.4 copy-done.4
  271.2 12.5 %recall_bwd.1 = bf16[8,2,256,128]{3,2,1,0:T(8,128)(2,1)} custom-call(f32[2]{0:T(128)S(1)} %add_divide_fusion.gate_ref, bf16[8,256,256]{2,1,0:T(8,128)(2,1)S(1)} %bitcast.210, bf16[8,256,256]{2,1,0:T(8,128)(2,1)S(1)} %bitcast.215, f32[8,8,256]{2,1,0:T(8,128)S(1)} %bitcast.216, bf16[8,2,1024,256]{3,2,1,0:T(8,128)(2,1)S(1)} %copy-done.4, ...), custom_call_target="tpu_custom_call" | custom-call | tf_op jit(solution)/shard_map/recall_bwd/pallas_call | solution.py:184
  283.6 4.2 all-to-all-start.3
  288.0 3.7 convolution_convert_fusion
  298.9 7.3 %collective-permute-done.2 = bf16[2,256,256]{2,1,0:T(8,128)(2,1)S(1)} collective-permute-done((bf16[2,256,256]{2,1,0:T(8,128)(2,1)S(1)}, bf16[2,256,256]{2,1,0:T(8,128)(2,1)S(1)}, u32[]{:S(2)}, u32[]{:S(2)}) %collective-permute-start.2) | collective-permute-done | bytes 262176 | tf_op jit(solution)/shard_map/ppermute | solution.py:293
  306.2 10.7 %collective-permute-done.3 = bf16[2,256,256]{2,1,0:T(8,128)(2,1)S(1)} collective-permute-done((bf16[2,256,256]{2,1,0:T(8,128)(2,1)S(1)}, bf16[2,256,256]{2,1,0:T(8,128)(2,1)S(1)}, u32[]{:S(2)}, u32[]{:S(2)}) %collective-permute-start.3) | collective-permute-done | bytes 262176 | tf_op jit(solution)/shard_map/ppermute | solution.py:293
  320.7 4.7 pad_maximum_fusion
  325.4 6.5 %copy.67 = bf16[1024,2048]{1,0:T(8,128)(2,1)} copy(bf16[1024,2048]{0,1:T(8,128)(2,1)} %pad_maximum_fusion) | data formatting | bytes 8388608
  336.9 4.0 copy.65
  343.4 14.8 %all-reduce.8.cloned.1.call-done = bf16[256,1024]{1,0:T(8,128)(2,1)} async-done(((bf16[256,1024]{1,0:T(8,128)(2,1)}), bf16[256,1024]{1,0:T(8,128)(2,1)}) %all-reduce.8.cloned.1.call-update) | async-done | bytes 524304 | tf_op jit(solution)/shard_map/psum | solution.py:312
  359.7 38.2 %all-reduce = (f32[2,1024]{1,0:T(2,128)S(1)}, f32[2,32]{1,0:T(2,128)}, f32[2]{0:T(128)}, f32[3]{0:T(128)S(1)}) all-reduce(f32[2,1024]{1,0:T(2,128)S(1)} %pad_maximum_fusion.4, f32[2,32]{1,0:T(2,128)S(1)} %fusion.84, f32[2]{0:T(128)S(1)} %subtract_multiply_fusion, f32[3]{0:T(128)S(1)} %pad_maximum_fusion.5), channel_id=1, replica_groups=mesh['seq'=8,'head'=4] {'seq'}, use_global_device_ids=true, to_apply=%region_18.19 | all-reduce | flops 2117 | bytes 16936 | tf_op jit(solution)/shard_map/psum | solution.py:442
  399.0 2.7 fusion.17
  401.7 23.1 %reduce-scatter.9.cloned.1.call-done = bf16[128,2048]{1,0:T(8,128)(2,1)} async-done(((bf16[1024,2048]{1,0:T(8,128)(2,1)}), bf16[128,2048]{1,0:T(8,128)(2,1)}) %reduce-scatter.9.cloned.1.call-update) | async-done | bytes 524304
  430.1 66.2 %reduce-scatter.7.cloned.1.call-done = bf16[128,1024]{1,0:T(8,128)(2,1)} async-done(((bf16[1024,1024]{1,0:T(8,128)(2,1)}), bf16[128,1024]{1,0:T(8,128)(2,1)}) %reduce-scatter.7.cloned.1.call-update) | async-done | bytes 262160
  (177 shorter events, 59.7 us)
Async XLA Ops:
  8.0 169.8 %copy-start = (bf16[1024,1024]{1,0:T(8,128)(2,1)S(1)}, bf16[1024,1024]{1,0:T(8,128)(2,1)}, u32[]{:S(2)}) copy-start(bf16[1024,1024]{1,0:T(8,128)(2,1)} %param.25) | copy-start | bytes 6291460
  8.0 5.6 %copy-start.13 = (bf16[1,256,1024]{2,1,0:T(8,128)(2,1)S(1)}, bf16[1,256,1024]{2,1,0:T(8,128)(2,1)}, u32[]{:S(2)}) copy-start(bf16[1,256,1024]{2,1,0:T(8,128)(2,1)} %param.18) | copy-start | bytes 1572868
  8.0 5.6 %copy-start.36 = (f32[1024]{0:T(1024)S(1)}, f32[1024]{0:T(1024)}, u32[]{:S(2)}) copy-start(f32[1024]{0:T(1024)} %param.26) | copy-start | bytes 12292
  8.1 21.1 %sort.9.cloned.1.call-start = ((), (), s32[]{:S(2)}) async-start(), calls=%async_computation.13 | async-start | bytes 196640 | tf_op jit(solution)/shard_map/sort | solution.py:342
  9.3 5.8 %copy-start.24 = (bf16[1024,256]{1,0:T(8,128)(2,1)S(1)}, bf16[1024,256]{1,0:T(8,128)(2,1)}, u32[]{:S(2)}) copy-start(bf16[1024,256]{1,0:T(8,128)(2,1)} %param.22) | copy-start | bytes 1572868
  10.1 71.8 %all-gather.6.cloned.1.call-start = ((), (), s32[]{:S(2)}) async-start(), calls=%async_computation.8 | async-start | bytes 1179648 | tf_op jit(solution)/shard_map/all_gather | solution.py:359
  29.1 14.6 %all-to-all-start = ((s32[8,2,1024]{2,1,0:T(2,128)}), s32[8,2,1024]{2,1,0:T(2,128)S(1)}, u32[]{:S(2)}, u32[]{:S(2)}) async-start(s32[8,2,1024]{2,1,0:T(2,128)} %bitcast.219), calls=%async_computation | async-start | bytes 131072 | tf_op jit(solution)/shard_map/all_to_all | solution.py:308
  36.4 78.1 %collective-permute-start = (bf16[2,256,256]{2,1,0:T(8,128)(2,1)S(1)}, bf16[2,256,256]{2,1,0:T(8,128)(2,1)S(1)}, u32[]{:S(2)}, u32[]{:S(2)}) collective-permute-start(bf16[2,256,256]{2,1,0:T(8,128)(2,1)S(1)} %pad_maximum_fusion.3), channel_id=1, source_target_pairs={{0,8},{4,12},{8,16},{12,20},{16,24},{20,28},{1,9},{5,13},{9,17},{1... | collective-permute-start | bytes 786440 | tf_op jit(solution)/shard_map/ppermute | solution.py:293
  40.3 74.1 %collective-permute-start.1 = (bf16[2,256,256]{2,1,0:T(8,128)(2,1)S(1)}, bf16[2,256,256]{2,1,0:T(8,128)(2,1)S(1)}, u32[]{:S(2)}, u32[]{:S(2)}) collective-permute-start(bf16[2,256,256]{2,1,0:T(8,128)(2,1)S(1)} %pad_maximum_fusion.3), channel_id=1, source_target_pairs={{0,4},{4,8},{8,12},{12,16},{16,20},{20,24},{24,28},{1,5},{5,9},{9,... | collective-permute-start | bytes 786440 | tf_op jit(solution)/shard_map/ppermute | solution.py:293
  86.5 16.3 %copy-start.39 = (f32[2]{0:T(128)S(1)}, f32[2]{0:T(128)}, u32[]{:S(2)}) copy-start(f32[2]{0:T(128)} %param.29) | copy-start | bytes 28
  99.1 15.1 %copy-start.35 = (f32[32,768]{1,0:T(8,128)S(1)}, f32[32,768]{1,0:T(8,128)}, u32[]{:S(2)}) copy-start(f32[32,768]{1,0:T(8,128)} %constant.108.clone) | copy-start | bytes 294916
  99.1 15.1 %copy-start.37 = (f32[768]{0:T(1024)S(1)}, f32[768]{0:T(1024)}, u32[]{:S(2)}) copy-start(f32[768]{0:T(1024)} %constant.115) | copy-start | bytes 9220
  99.1 15.1 %copy-start.38 = (f32[2,32]{1,0:T(2,128)S(1)}, f32[2,32]{1,0:T(2,128)}, u32[]{:S(2)}) copy-start(f32[2,32]{1,0:T(2,128)} %param.28) | copy-start | bytes 772
  99.1 10.7 %all-to-all-start.1 = ((f32[8,8,256]{2,1,0:T(8,128)}), f32[8,8,256]{2,1,0:T(8,128)S(1)}, u32[]{:S(2)}, u32[]{:S(2)}) async-start(f32[8,8,256]{2,1,0:T(8,128)} %get-tuple-element.21), calls=%async_computation.1 | async-start | bytes 131072 | tf_op jit(solution)/shard_map/all_to_all | solution.py:308
  109.8 27.9 %all-to-all-start.2 = ((bf16[8,2,256,128]{3,2,1,0:T(8,128)(2,1)}), bf16[8,2,256,128]{3,2,1,0:T(8,128)(2,1)}, u32[]{:S(2)}, u32[]{:S(2)}) async-start(bf16[8,2,256,128]{3,2,1,0:T(8,128)(2,1)} %get-tuple-element.22), calls=%async_computation.2 | async-start | bytes 2097152 | tf_op jit(solution)/shard_map/all_to_all | solution.py:308
  114.1 59.6 %all-reduce.6.cloned.1.call-start = ((), (), s32[]{:S(2)}) async-start(), calls=%async_computation.6 | async-start | bytes 1048576 | tf_op jit(solution)/shard_map/psum | solution.py:312
  118.1 57.0 %copy-start.34 = (f32[1024]{0:T(1024)S(1)}, f32[1024]{0:T(1024)}, u32[]{:S(2)}) copy-start(f32[1024]{0:T(1024)} %param.27) | copy-start | bytes 12292
  141.4 78.1 %all-reduce.10.cloned.1.call-start = ((), (), s32[]{:S(2)}) async-start(), calls=%async_computation.12 | async-start | bytes 2097152 | tf_op jit(solution)/shard_map/psum | solution.py:312
  181.6 37.9 %copy-start.14 = (bf16[1,256,1024]{2,1,0:T(8,128)(2,1)S(1)}, bf16[1,256,1024]{2,1,0:T(8,128)(2,1)}, u32[]{:S(2)}) copy-start(bf16[1,256,1024]{2,1,0:T(8,128)(2,1)} %param.18) | copy-start | bytes 1572868
  181.6 37.9 %copy-start.16 = (bf16[256,1024]{1,0:T(8,128)(2,1)S(1)}, bf16[256,1024]{1,0:T(8,128)(2,1)}, u32[]{:S(2)}) copy-start(bf16[256,1024]{1,0:T(8,128)(2,1)} %all-reduce.6.cloned.1.call-done) | copy-start | bytes 1572868
  183.1 83.4 %all-gather.8.cloned.1.call-start = ((), (), s32[]{:S(2)}) async-start(), calls=%async_computation.9 | async-start | bytes 1179648 | tf_op jit(solution)/shard_map/all_gather | solution.py:401
  222.9 43.6 %copy-start.6 = (bf16[2048,256]{1,0:T(8,128)(2,1)S(1)}, bf16[2048,256]{1,0:T(8,128)(2,1)}, u32[]{:S(2)}) copy-start(bf16[2048,256]{1,0:T(8,128)(2,1)} %all-gather.6.cloned.1.call-done) | copy-start | bytes 3145732
  283.6 33.4 %all-to-all-start.3 = ((bf16[8,2,256,128]{3,2,1,0:T(8,128)(2,1)}), bf16[8,2,256,128]{3,2,1,0:T(8,128)(2,1)}, u32[]{:S(2)}, u32[]{:S(2)}) async-start(bf16[8,2,256,128]{3,2,1,0:T(8,128)(2,1)} %recall_bwd.1), calls=%async_computation.3 | async-start | bytes 2097152 | tf_op jit(solution)/shard_map/all_to_all | solution.py:308
  287.9 3.7 copy-start.8
  287.9 3.7 copy-start.11
  287.9 70.3 %all-reduce.8.cloned.1.call-start = ((), (), s32[]{:S(2)}) async-start(), calls=%async_computation.7 | async-start | bytes 1048576 | tf_op jit(solution)/shard_map/psum | solution.py:312
  293.9 12.3 %collective-permute-start.2 = (bf16[2,256,256]{2,1,0:T(8,128)(2,1)S(1)}, bf16[2,256,256]{2,1,0:T(8,128)(2,1)S(1)}, u32[]{:S(2)}, u32[]{:S(2)}) collective-permute-start(bf16[2,256,256]{2,1,0:T(8,128)(2,1)S(1)} %get-tuple-element.94), channel_id=1, source_target_pairs={{4,0},{8,4},{12,8},{16,12},{20,16},{24,20},{28,24},{5,1},{9,5},{13... | collective-permute-start | bytes 786440 | tf_op jit(solution)/shard_map/ppermute | solution.py:293
  295.3 21.6 %collective-permute-start.3 = (bf16[2,256,256]{2,1,0:T(8,128)(2,1)S(1)}, bf16[2,256,256]{2,1,0:T(8,128)(2,1)S(1)}, u32[]{:S(2)}, u32[]{:S(2)}) collective-permute-start(bf16[2,256,256]{2,1,0:T(8,128)(2,1)S(1)} %get-tuple-element.95), channel_id=1, source_target_pairs={{8,0},{12,4},{16,8},{20,12},{24,16},{28,20},{9,1},{13,5},{17,9},{2... | collective-permute-start | bytes 786440 | tf_op jit(solution)/shard_map/ppermute | solution.py:293
  298.9 19.6 %copy-start.28 = (bf16[1024,256]{1,0:T(8,128)(2,1)S(1)}, bf16[1024,256]{1,0:T(8,128)(2,1)}, u32[]{:S(2)}) copy-start(bf16[1024,256]{1,0:T(8,128)(2,1)} %param.20) | copy-start | bytes 1572868
  320.7 104.2 %reduce-scatter.9.cloned.1.call-start = ((), (), s32[]{:S(2)}) async-start(), calls=%async_computation.11 | async-start | bytes 4718592
  332.0 164.4 %reduce-scatter.7.cloned.1.call-start = ((), (), s32[]{:S(2)}) async-start(), calls=%async_computation.10 | async-start | bytes 2359296
  427.1 73.4 %copy-start.1 = (bf16[1024,1024]{1,0:T(8,128)(2,1)S(1)}, bf16[1024,1024]{1,0:T(8,128)(2,1)}, u32[]{:S(2)}) copy-start(bf16[1024,1024]{1,0:T(8,128)(2,1)} %param.25) | copy-start | bytes 6291460
  (24 other events, 44.4 us)
Sparse Core Ops, SparseCore 0:
  11.9 16.9 sort.11.cloned.1.call-done
  141.5 32.0 all-reduce.5
  183.2 36.1 all-reduce.9
  320.8 37.3 all-reduce.7
  (1 shorter events, 0.0 us)
Sparse Core Ops, SparseCore 1:
  13.8 43.1 all-gather.5
  225.7 40.8 all-gather.7
  332.0 92.8 reduce-scatter.8
  428.8 67.4 reduce-scatter.6

commit v2 on v1

v2 whole, which is shorter than its diff:
```python
import functools
import math

import jax
import jax.numpy as jnp
import numpy as np
from jax import lax
from jax.experimental import pallas as pl
from jax.experimental.pallas import tpu as pltpu
from jax.sharding import PartitionSpec as P

W = 512
eps = 1e-06
exact_span = 16
far_distance = 128
highest = lax.Precision.HIGHEST
f32 = jnp.float32
bf16 = jnp.bfloat16
NEG = -1e30
MIB = 2**20


def bucket_table(key_span, bucket_total):
    found = []
    for distance in range(key_span):
        if distance < exact_span:
            found.append(distance)
        else:
            scaled = math.log(distance / exact_span) / math.log(far_distance / exact_span)
            found.append(
                min(bucket_total - 1, exact_span + math.floor(scaled * (bucket_total - exact_span)))
            )
    return np.asarray(found)


def diagonal_buckets(block_len, bucket_total):
    span = W + block_len
    table = bucket_table(W, bucket_total)
    hot = np.zeros((bucket_total, span), np.float32)
    for u in range(1, W + 1):
        hot[table[W - u], u] = 1.0
    outside = np.where(hot.sum(0) > 0, 0.0, NEG).astype(np.float32)
    return hot, outside


def nt(a, b):
    return lax.dot_general(a, b, (((1,), (1,)), ((), ())), preferred_element_type=f32)


def nn(a, b):
    return lax.dot_general(a, b, (((1,), (0,)), ((), ())), preferred_element_type=f32)


def tn(a, b):
    return lax.dot_general(a, b, (((0,), (0,)), ((), ())), preferred_element_type=f32)


def gather_kernel(codes_ref, table_ref, out_ref, wide, buf, *, rows, chunk, chunks, unroll, group):
    step = pl.program_id(0)
    part = 32

    @pl.when(step < chunks)
    def _():
        def widen(q, carry):
            x = table_ref[pl.ds(q * part, part)].astype(f32)
            base = step * chunk + q * part
            for r in range(part):
                wide[pl.ds(4 * (base + r), 2), :] = x[r, :, 0:128]
                wide[pl.ds(4 * (base + r) + 2, 2), :] = x[r, :, 128:256]
            return carry

        lax.fori_loop(0, chunk // part, widen, 0)

    @pl.when(step >= chunks)
    def _():
        head = (step - chunks) % 2

        def copy_rows(i, carry):
            base = i * unroll
            for g in range(0, unroll, group):
                found = [
                    wide[pl.ds(codes_ref[0, 0, 0, base + g + u] * 4 + head, 2, 2), :]
                    for u in range(group)
                ]
                for u in range(group):
                    buf[pl.ds(2 * (base + g + u), 2), :] = found[u]
            return carry

        lax.fori_loop(0, rows // unroll, copy_rows, 0)
        out_ref[0, 0, :, 0:128] = buf[pl.ds(0, rows, 2), :].astype(bf16)
        out_ref[0, 0, :, 128:256] = buf[pl.ds(1, rows, 2), :].astype(bf16)


def gather_rows(slots, table):
    parts, heads, rows = slots.shape
    total = table.shape[0]
    chunk = min(1024, total)
    chunks = total // chunk
    unroll = min(64, rows)

    def place(i):
        at = jnp.maximum(i - chunks, 0)
        return (at // 2, at % 2, 0, 0)

    return pl.pallas_call(
        functools.partial(
            gather_kernel, rows=rows, chunk=chunk, chunks=chunks, unroll=unroll, group=unroll // 2
        ),
        out_shape=jax.ShapeDtypeStruct((parts, heads, rows, 256), bf16),
        grid=(chunks + parts * heads,),
        in_specs=[
            pl.BlockSpec((1, 1, 1, rows), place, memory_space=pltpu.SMEM),
            pl.BlockSpec((chunk, 2, 256), lambda i: (jnp.minimum(i, chunks - 1), 0, 0)),
        ],
        out_specs=pl.BlockSpec((1, 1, rows, 256), place),
        scratch_shapes=[pltpu.VMEM((4 * total, 128), f32), pltpu.VMEM((2 * rows, 128), f32)],
        compiler_params=pltpu.CompilerParams(vmem_limit_bytes=40 * MIB),
        cost_estimate=pl.CostEstimate(flops=0, bytes_accessed=100 * MIB, transcendentals=0),
        name="gather_rows",
    )(slots.reshape(parts, heads, 1, rows), table)


MESH = pl.DeviceIdType.MESH


def greet(**counts):
    barrier = pltpu.get_barrier_semaphore()
    for axis, count in counts.items():
        me = lax.axis_index(axis)

        def call(d, carry, axis=axis, count=count, me=me):
            peer = lax.rem(me + d, count)
            pl.semaphore_signal(barrier, inc=1, device_id={axis: peer}, device_id_type=MESH)
            return carry

        lax.fori_loop(1, count, call, 0)
    pl.semaphore_wait(barrier, sum(counts.values()) - len(counts))


def send(src, dst, send_sem, recv_sem, axis, peer):
    return pltpu.make_async_remote_copy(
        src_ref=src,
        dst_ref=dst,
        send_sem=send_sem,
        recv_sem=recv_sem,
        device_id={axis: peer},
        device_id_type=MESH,
    )


def doc_starts(lengths_ref, first, count):
    place = first + lax.broadcasted_iota(jnp.int32, (count, 1), 0)
    start = jnp.zeros((count, 1), jnp.int32)
    end = jnp.int32(0)
    for c in range(lengths_ref.shape[0]):
        end = end + lengths_ref[c]
        start = jnp.where(end <= place, end, start)
    return start


def head_cols(h):
    return slice(h * 128, h * 128 + 128)


def row_form(columns, count):
    lane = lax.broadcasted_iota(jnp.int32, (count, 128), 1)
    wide = jnp.zeros((count, 128), f32)
    for i, column in enumerate(columns):
        wide = jnp.where(lane == i, column, wide)
    return wide


def attend_kernel(
    lengths_ref,
    gate_ref,
    q_ref,
    k_ref,
    v_ref,
    bias_ref,
    q_all_ref,
    tok_ref,
    rows_hbm,
    mixed_ref,
    recalled_ref,
    local_ref,
    logs_ref,
    p_ref,
    pair_ref,
    rows,
    out_send,
    out_recv,
    log_send,
    log_recv,
    rows_sem,
    out_ss,
    out_rs,
    log_ss,
    log_rs,
    pair_ss,
    pair_rs,
    *,
    parts,
    scale,
):
    count, span = q_ref.shape[0], pair_ref.shape[1]
    hops = W // count
    per = tok_ref.shape[2]

    def fetch(d, j):
        return pltpu.make_async_copy(rows_hbm.at[j], rows.at[d], rows_sem.at[d])

    me = lax.axis_index("seq")

    def fetch_start(d, carry):
        fetch(d, lax.rem(me + d, parts)).start()
        return carry

    lax.fori_loop(1, parts, fetch_start, 0)
    fetch(0, me).start()
    pair_ref[0, W:, :] = k_ref[...]
    pair_ref[1, W:, :] = v_ref[...]
    greet(seq=parts)

    def hand_on(hop):
        return send(
            pair_ref.at[:, pl.ds(W, count)],
            pair_ref.at[:, pl.ds(W - hop * count, count)],
            pair_ss.at[hop - 1],
            pair_rs.at[hop - 1],
            "seq",
            lax.rem(me + hop, parts),
        )

    for hop in range(1, hops + 1):
        hand_on(hop).start()

    ids = lax.broadcasted_iota(jnp.int32, (count, per), 0)

    def owner_part(d, j, out, logs):
        fetch(d, j).wait()
        found = []
        for h in range(2):
            cols = head_cols(h)
            keep = tok_ref[j, h : h + 1, :] == ids
            s = jnp.where(keep, nt(q_all_ref[j, :, cols], rows[d, h, :, 0:128]) * scale, NEG)
            top = jnp.max(s, axis=1, keepdims=True)
            p = jnp.where(keep, jnp.exp(s - top), 0.0)
            total = jnp.sum(p, axis=1, keepdims=True)
            some = total > 0.0
            safe = jnp.where(some, total, 1.0)
            out[d, h] = (nn(p.astype(bf16), rows[d, h, :, 128:256]) / safe).astype(bf16)
            found.append(jnp.where(some, top + jnp.log(safe), NEG))
        logs[d] = row_form(found, count).T[0:8]

    def send_out(d):
        peer = lax.rem(me + d, parts)
        return send(out_send.at[d], out_recv.at[d], out_ss.at[d], out_rs.at[d], "seq", peer)

    def send_log(d):
        peer = lax.rem(me + d, parts)
        return send(log_send.at[d], log_recv.at[d], log_ss.at[d], log_rs.at[d], "seq", peer)

    def serve(d, carry):
        owner_part(d, lax.rem(me + d, parts), out_send, log_send)
        send_log(d).start()
        send_out(d).start()
        return carry

    lax.fori_loop(1, parts, serve, 0)
    owner_part(0, me, out_recv, log_recv)

    for hop in range(1, hops + 1):
        hand_on(hop).wait()
    first = me * count
    start = doc_starts(lengths_ref, first, count)
    key_place = first - W + lax.broadcasted_iota(jnp.int32, (count, span), 1)
    seen = key_place >= start
    for h in range(2):
        cols = head_cols(h)
        bias = pltpu.roll(
            jnp.broadcast_to(bias_ref[h : h + 1, :], (count, span)), 0, 1, stride=1, stride_axis=0
        )
        s = nt(q_ref[:, cols], pair_ref[0, :, cols]) * scale + bias
        s = jnp.where(seen, s, NEG)
        raised = jnp.exp(s - jnp.max(s, axis=1, keepdims=True))
        p = raised / jnp.sum(raised, axis=1, keepdims=True)
        p_ref[h] = p
        local_ref[:, cols] = nn(p.astype(bf16), pair_ref[1, :, cols])

    def wait_log(d, carry):
        send_log(d).wait()
        return carry

    lax.fori_loop(1, parts, wait_log, 0)

    def top_of(d, top):
        return jnp.maximum(top, log_recv[d])

    top = lax.fori_loop(1, parts, top_of, log_recv[0])

    def add_to(d, total):
        return total + jnp.exp(log_recv[d] - top)

    total = lax.fori_loop(1, parts, add_to, jnp.exp(log_recv[0] - top))
    logs = top + jnp.log(total)
    logs_ref[...] = logs

    def merge(d):
        share = jnp.exp(log_recv[d] - logs).T
        for h in range(2):
            cols = head_cols(h)
            recalled_ref[:, cols] += share[:, h : h + 1] * out_recv[d, h].astype(f32)

    recalled_ref[...] = jnp.zeros_like(recalled_ref)
    merge(0)

    def merge_next(d, carry):
        send_out(d).wait()
        merge(d)
        return carry

    lax.fori_loop(1, parts, merge_next, 0)
    for h in range(2):
        cols = head_cols(h)
        gate = gate_ref[h]
        mixed = gate * recalled_ref[:, cols] + (1.0 - gate) * local_ref[:, cols]
        mixed_ref[:, cols] = mixed.astype(bf16)


def attend(lengths, gate, q, k, v, bias, q_all, tok, rows):
    parts, count, width = q_all.shape
    span, hops = W + count, W // count
    smem = pl.BlockSpec(memory_space=pltpu.SMEM)
    vmem = pl.BlockSpec(memory_space=pltpu.VMEM)
    dma = pltpu.SemaphoreType.DMA
    return pl.pallas_call(
        functools.partial(attend_kernel, parts=parts, scale=128**-0.5),
        out_shape=(
            jax.ShapeDtypeStruct((count, width), bf16),
            jax.ShapeDtypeStruct((count, width), f32),
            jax.ShapeDtypeStruct((count, width), f32),
            jax.ShapeDtypeStruct((8, count), f32),
            jax.ShapeDtypeStruct((2, count, span), f32),
            jax.ShapeDtypeStruct((2, span, width), bf16),
        ),
        in_specs=[smem, smem] + [vmem] * 6 + [pl.BlockSpec(memory_space=pl.ANY)],
        out_specs=(vmem,) * 6,
        scratch_shapes=[
            pltpu.VMEM(rows.shape, bf16),
            pltpu.VMEM((parts, 2, count, 128), bf16),
            pltpu.VMEM((parts, 2, count, 128), bf16),
            pltpu.VMEM((parts, 8, count), f32),
            pltpu.VMEM((parts, 8, count), f32),
        ]
        + [dma((parts,))] * 5
        + [dma((hops,))] * 2,
        compiler_params=pltpu.CompilerParams(
            vmem_limit_bytes=56 * MIB, collective_id=1, has_side_effects=True
        ),
        cost_estimate=pl.CostEstimate(
            flops=3 * 10**9, bytes_accessed=100 * MIB, transcendentals=5 * 10**6
        ),
        name="attend",
    )(lengths, gate, q, k, v, bias, q_all, tok, rows)


class ScatterSum:
    def __init__(self, grads, sems, parts):
        self.grads, self.sems = grads, sems
        self.quarter = parts // 4
        self.own = grads[0][0].shape[0] // parts
        me = lax.axis_index("seq")
        self.x, self.b, self.a = lax.rem(me, 2), lax.rem(me // 2, 2), me // 4

    def place(self, da, side, x):
        b = self.b if side == 1 else 1 - self.b
        return 4 * lax.rem(self.a + da, self.quarter) + 2 * b + x

    def rows_of(self, place):
        return pl.ds(pl.multiple_of(place * self.own, self.own), self.own)

    def send_x(self, k, da, side):
        ss, rs = self.sems[0:2]
        return send(
            self.grads[k][0].at[self.rows_of(self.place(da, side, 1 - self.x))],
            self.grads[k][1].at[side, da],
            ss.at[k, side, da],
            rs.at[k, side, da],
            "seq",
            self.place(0, 1, 1 - self.x),
        )

    def send_pair(self, k, da):
        ss, rs = self.sems[2:4]
        grads, peer = self.grads[k], self.place(0, 0, self.x)
        return send(grads[2].at[da], grads[3].at[da], ss.at[k, da], rs.at[k, da], "seq", peer)

    def send_far(self, k, da):
        ss, rs = self.sems[4:6]
        grads, peer = self.grads[k], self.place(da, 1, self.x)
        return send(grads[4].at[da], grads[5].at[da], ss.at[k, da], rs.at[k, da], "seq", peer)

    def loop(self, first, last, step):
        def body(da, carry):
            for k in range(len(self.grads)):
                step(k, da)
            return carry

        lax.fori_loop(first, last, body, 0)

    def span(self, far):
        return (1, self.quarter) if far else (0, 1)

    def start(self, far, side):
        self.loop(*self.span(far), lambda k, da: self.send_x(k, da, side).start())

    def column(self, k, da, side):
        self.send_x(k, da, side).wait()
        mine = self.grads[k][0][self.rows_of(self.place(da, side, self.x)), :]
        return mine.astype(f32) + self.grads[k][1][side, da].astype(f32)

    def pair(self, far):
        def step(k, da):
            self.grads[k][2][da] = self.column(k, da, 0).astype(bf16)
            self.send_pair(k, da).start()

        self.loop(*self.span(far), step)

    def both(self, k, da):
        found = self.column(k, da, 1)
        self.send_pair(k, da).wait()
        return found + self.grads[k][3][da].astype(f32)

    def far(self):
        def step(k, da):
            self.grads[k][4][da] = self.both(k, da).astype(bf16)
            self.send_far(k, da).start()

        self.loop(*self.span(True), step)

    def settle(self, outs):
        for k, out in enumerate(outs):
            out[...] = self.both(k, 0)

        def step(k, da):
            self.send_far(k, da).wait()
            outs[k][...] += self.grads[k][5][da].astype(f32)

        self.loop(*self.span(True), step)

    @staticmethod
    def scratch(arrays, parts):
        quarter = parts // 4
        slots = []
        for a in arrays:
            piece = (a.shape[0] // parts, a.shape[1])
            slots.append(pltpu.VMEM((2, quarter) + piece, bf16))
            slots += [pltpu.VMEM((quarter,) + piece, bf16)] * 4
        dma = pltpu.SemaphoreType.DMA
        count = len(arrays)
        return slots, [dma((count, 2, quarter))] * 2 + [dma((count, quarter))] * 4


def attend_back_kernel(
    gate_ref,
    sum_ref,
    cot_ref,
    gain_ref,
    middle_ref,
    weight_ref,
    q_ref,
    recalled_ref,
    local_ref,
    logs_ref,
    p_ref,
    pair_ref,
    q_all_ref,
    tok_ref,
    up_ref,
    down_ref,
    rows_hbm,
    branch_ref,
    grad_middle_ref,
    line_ref,
    d_ref,
    pos_ref,
    gate_out_ref,
    up_out_ref,
    down_out_ref,
    sum_recv,
    rows,
    g_own,
    g_all,
    st_own,
    st_all,
    dq_xs,
    dq_xr,
    dq_zs,
    dq_zr,
    pair_send,
    pair_recv,
    dq_sum,
    pair_sum,
    up_a,
    up_b,
    up_c,
    up_d,
    up_e,
    down_a,
    down_b,
    down_c,
    down_d,
    down_e,
    down_sum,
    sum_ss,
    sum_rs,
    full_ss,
    full_rs,
    rows_sem,
    g_ss,
    g_rs,
    st_ss,
    st_rs,
    dx_ss,
    dx_rs,
    dz_ss,
    dz_rs,
    pair_ss,
    pair_rs,
    sem_a,
    sem_b,
    sem_c,
    sem_d,
    sem_e,
    sem_f,
    *,
    parts,
    peers,
    scale,
):
    count, span = q_ref.shape[0], pair_ref.shape[1]
    width = q_ref.shape[1]
    hops = W // count
    per = tok_ref.shape[2]
    half = parts // 2
    me, head = lax.axis_index("seq"), lax.axis_index("head")
    x, z = lax.rem(me, 2), me // 2
    partner = me + 1 - 2 * x

    def reader(c, dz):
        at = lax.rem(z + half - dz, half)
        return 2 * at + (x if c == 0 else 1 - x)

    def fetch(c, dz):
        return pltpu.make_async_copy(
            rows_hbm.at[reader(c, dz)], rows.at[c, dz], rows_sem.at[c, dz]
        )

    def fetch_start(dz, carry):
        fetch(0, dz).start()
        fetch(1, dz).start()
        return carry

    lax.fori_loop(0, half, fetch_start, 0)
    greet(seq=parts, head=peers)

    share = count // peers

    def share_of(peer):
        return pl.ds(pl.multiple_of(peer * share, share), share)

    def send_sum(d):
        peer = lax.rem(head + d, peers)
        return send(
            sum_ref.at[share_of(peer)], sum_recv.at[d], sum_ss.at[d], sum_rs.at[d], "head", peer
        )

    mine = share_of(head)

    def send_full(d):
        peer = lax.rem(head + d, peers)
        return send(
            branch_ref.at[mine], branch_ref.at[mine], full_ss.at[d], full_rs.at[d], "head", peer
        )

    for d in range(1, peers):
        send_sum(d).start()
    scatter = ScatterSum(
        ((up_ref, up_a, up_b, up_c, up_d, up_e), (down_ref, down_a, down_b, down_c, down_d, down_e)),
        (sem_a, sem_b, sem_c, sem_d, sem_e, sem_f),
        parts,
    )
    scatter.start(True, 0)
    scatter.start(True, 1)
    middle = middle_ref[...]
    row_scale = lax.rsqrt(row_mean(middle * middle) + eps)
    hat = middle * row_scale
    grad_normed = sum_ref[mine, :].astype(f32)
    for d in range(1, peers):
        send_sum(d).wait()
        grad_normed = grad_normed + sum_recv[d].astype(f32)
    scaled = grad_normed * gain_ref[...]
    grad_middle = cot_ref[mine, :].astype(f32) + row_scale * (scaled - hat * row_mean(scaled * hat))
    branch_ref[mine, :] = grad_middle.astype(bf16)
    for d in range(1, peers):
        send_full(d).start()
    grad_middle_ref[...] = grad_middle
    line_ref[...] = col_sum(grad_normed * hat)
    scatter.pair(True)
    for d in range(1, peers):
        send_full(d).wait()
    g_own[...] = nt(branch_ref[...], weight_ref[...]).astype(bf16)

    deltas = []
    for h in range(2):
        cols = head_cols(h)
        g = g_own[:, cols].astype(f32)
        gate_out_ref[h : h + 1, :] = col_sum(g * (recalled_ref[:, cols] - local_ref[:, cols]))
        both = jnp.sum(g * recalled_ref[:, cols], axis=1, keepdims=True)
        deltas.append(both * gate_ref[h])
    turned = row_form([jnp.zeros_like(deltas[0])] * 2 + deltas, count).T[0:8]
    row = lax.broadcasted_iota(jnp.int32, (8, count), 0)
    st_own[...] = jnp.where(row < 2, logs_ref[...], turned)

    def ask_z(dz):
        peer = 2 * lax.rem(z + dz, half) + x
        return (
            send(st_own, st_all.at[0, dz], st_ss.at[0, dz], st_rs.at[0, dz], "seq", peer),
            send(g_own, g_all.at[0, dz], g_ss.at[0, dz], g_rs.at[0, dz], "seq", peer),
        )

    def ask_x(dz, own=False):
        st, g = (st_own, g_own) if own else (st_all.at[0, dz], g_all.at[0, dz])
        return (
            send(st, st_all.at[1, dz], st_ss.at[1, dz], st_rs.at[1, dz], "seq", partner),
            send(g, g_all.at[1, dz], g_ss.at[1, dz], g_rs.at[1, dz], "seq", partner),
        )

    def ask(dz, carry):
        for copy in ask_z(dz):
            copy.start()
        return carry

    for copy in ask_x(0, own=True):
        copy.start()
    lax.fori_loop(1, half, ask, 0)

    for h in range(2):
        cols = head_cols(h)
        rest = 1.0 - gate_ref[h]
        p = p_ref[h]
        e = nt(g_own[:, cols], pair_ref[1, :, cols]) * rest
        delta = jnp.sum(p * e, axis=1, keepdims=True)
        ds = (p * (e - delta)).astype(bf16)
        dq_sum[:, cols] = nn(ds, pair_ref[0, :, cols]) * scale
        dk = tn(ds, q_ref[:, cols]) * scale
        dv = tn(p.astype(bf16), g_own[:, cols]) * rest
        pair_sum[0, :, cols] = dk[W:]
        pair_sum[1, :, cols] = dv[W:]
        pair_send[0, :, cols] = dk[:W].astype(bf16)
        pair_send[1, :, cols] = dv[:W].astype(bf16)
        low = ds.astype(f32)
        acc = low[0:8]
        for a in range(1, count // 8):
            acc = acc + pltpu.roll(low[8 * a : 8 * a + 8], (span - 8 * a) % span, 1)
        line = acc[0:1]
        for b in range(1, 8):
            line = line + pltpu.roll(acc[b : b + 1], span - b, 1)
        pos_ref[h : h + 1, :] = line

    def hand_back(hop):
        return send(
            pair_send.at[:, pl.ds(W - hop * count, count)],
            pair_recv.at[hop - 1],
            pair_ss.at[hop - 1],
            pair_rs.at[hop - 1],
            "seq",
            lax.rem(me + parts - hop, parts),
        )

    for hop in range(1, hops + 1):
        hand_back(hop).start()

    ids = lax.broadcasted_iota(jnp.int32, (count, per), 0)

    def owner_part(c, dz, g_at, st_at):
        fetch(c, dz).wait()
        j = reader(c, dz)
        stats = st_at[...].T
        found = []
        for h in range(2):
            cols = head_cols(h)
            keep = tok_ref[j, h : h + 1, :] == ids
            s = nt(q_all_ref[j, :, cols], rows[c, dz, h, :, 0:128]) * scale
            p = jnp.exp(jnp.where(keep, s - stats[:, h : h + 1], NEG))
            e = nt(g_at[:, cols], rows[c, dz, h, :, 128:256]) * gate_ref[h]
            ds = (p * (e - stats[:, 2 + h : 3 + h])).astype(bf16)
            found.append(nn(ds, rows[c, dz, h, :, 0:128]) * scale)
        return found

    def give_x(dz):
        return send(dq_xs.at[dz], dq_xr.at[dz], dx_ss.at[dz], dx_rs.at[dz], "seq", partner)

    def give_z(dz):
        peer = reader(0, dz)
        return send(dq_zs.at[dz], dq_zr.at[dz], dz_ss.at[dz], dz_rs.at[dz], "seq", peer)

    own = owner_part(0, 0, g_own, st_own)
    for h in range(2):
        dq_sum[:, head_cols(h)] += own[h]

    def column(dz, carry):
        for copy in ask_z(dz):
            copy.wait()
        for copy in ask_x(dz):
            copy.start()
        found = owner_part(0, dz, g_all.at[0, dz], st_all.at[0, dz])
        for h in range(2):
            dq_zs[dz, h] = found[h].astype(bf16)
        return carry

    lax.fori_loop(1, half, column, 0)
    scatter.start(False, 0)
    scatter.far()

    def neighbour(dz, copies):
        for copy in copies:
            copy.wait()
        found = owner_part(1, dz, g_all.at[1, dz], st_all.at[1, dz])
        for h in range(2):
            dq_xs[dz, h] = found[h].astype(bf16)
        give_x(dz).start()

    def neighbour_step(dz, carry):
        neighbour(dz, ask_x(dz))
        return carry

    lax.fori_loop(1, half, neighbour_step, 0)
    neighbour(0, ask_x(0, own=True))
    scatter.start(False, 1)

    def column_back(dz, carry):
        give_x(dz).wait()
        for h in range(2):
            both = dq_zs[dz, h].astype(f32) + dq_xr[dz, h].astype(f32)
            dq_zs[dz, h] = both.astype(bf16)
        give_z(dz).start()
        return carry

    lax.fori_loop(1, half, column_back, 0)
    scatter.pair(False)
    give_x(0).wait()
    for h in range(2):
        dq_sum[:, head_cols(h)] += dq_xr[0, h].astype(f32)
    for hop in range(1, hops + 1):
        hand_back(hop).wait()
        pair_sum[...] += pair_recv[hop - 1].astype(f32)
    d_ref[:, width : 2 * width] = pair_sum[0].astype(bf16)
    d_ref[:, 2 * width :] = pair_sum[1].astype(bf16)

    def merge(dz, carry):
        give_z(dz).wait()
        for h in range(2):
            dq_sum[:, head_cols(h)] += dq_zr[dz, h].astype(f32)
        return carry

    lax.fori_loop(1, half, merge, 0)
    d_ref[:, :width] = dq_sum[...].astype(bf16)
    scatter.settle((up_out_ref, down_sum))
    down_out_ref[...] = down_sum[...].T


def attend_back(
    gate, sums, cot, gain, middle, weight, q, recalled, local, logs, p, pair, q_all, tok, up, down, rows, peers
):
    parts, count, width = q_all.shape
    span, hops, half = W + count, W // count, parts // 2
    model = sums.shape[1]
    share, own = count // peers, up.shape[0] // parts
    smem = pl.BlockSpec(memory_space=pltpu.SMEM)
    vmem = pl.BlockSpec(memory_space=pltpu.VMEM)
    dma = pltpu.SemaphoreType.DMA
    slots, sems = ScatterSum.scratch((up, down), parts)
    return pl.pallas_call(
        functools.partial(attend_back_kernel, parts=parts, peers=peers, scale=128**-0.5),
        out_shape=(
            jax.ShapeDtypeStruct((count, model), bf16),
            jax.ShapeDtypeStruct((share, model), f32),
            jax.ShapeDtypeStruct((1, model), f32),
            jax.ShapeDtypeStruct((count, 3 * width), bf16),
            jax.ShapeDtypeStruct((2, span), f32),
            jax.ShapeDtypeStruct((2, 128), f32),
            jax.ShapeDtypeStruct((own, up.shape[1]), f32),
            jax.ShapeDtypeStruct((down.shape[1], own), f32),
        ),
        in_specs=[smem] + [vmem] * 15 + [pl.BlockSpec(memory_space=pl.ANY)],
        out_specs=(vmem,) * 8,
        scratch_shapes=[
            pltpu.VMEM((peers, share, model), bf16),
            pltpu.VMEM((2, half) + rows.shape[1:], bf16),
            pltpu.VMEM((count, width), bf16),
            pltpu.VMEM((2, half, count, width), bf16),
            pltpu.VMEM((8, count), f32),
            pltpu.VMEM((2, half, 8, count), f32),
        ]
        + [pltpu.VMEM((half, 2, count, 128), bf16)] * 4
        + [
            pltpu.VMEM((2, W, width), bf16),
            pltpu.VMEM((hops, 2, count, width), bf16),
            pltpu.VMEM((count, width), f32),
            pltpu.VMEM((2, count, width), f32),
        ]
        + slots
        + [pltpu.VMEM((own, down.shape[1]), f32)]
        + [dma((peers,))] * 4
        + [dma((2, half))] * 5
        + [dma((half,))] * 4
        + [dma((hops,))] * 2
        + sems,
        compiler_params=pltpu.CompilerParams(
            vmem_limit_bytes=(44 if parts <= 8 else 62) * MIB, collective_id=2, has_side_effects=True
        ),
        cost_estimate=pl.CostEstimate(
            flops=4 * 10**9, bytes_accessed=150 * MIB, transcendentals=5 * 10**6
        ),
        name="attend_back",
    )(gate, sums, cot, gain, middle, weight, q, recalled, local, logs, p, pair, q_all, tok, up, down, rows)


def close_kernel(*refs, body, n_sum, n_aux, n_full, n_own, peers):
    sums = refs[:n_sum]
    aux = refs[n_sum : n_sum + n_aux]
    at = n_sum + n_aux
    full, own = refs[at : at + n_full], refs[at + n_full : at + n_full + n_own]
    at += n_full + n_own
    recv = refs[at : at + n_sum]
    ss, rs, full_ss, full_rs = refs[at + n_sum :]
    count = sums[0].shape[0]
    share = count // peers
    me = lax.axis_index("head")
    greet(head=peers)

    def rows_of(peer):
        return pl.ds(pl.multiple_of(peer * share, share), share)

    def send_sum(i, d):
        peer = lax.rem(me + d, peers)
        return send(
            sums[i].at[rows_of(peer)], recv[i].at[d], ss.at[i, d], rs.at[i, d], "head", peer
        )

    def send_full(i, d):
        return send(
            full[i].at[rows_of(me)],
            full[i].at[rows_of(me)],
            full_ss.at[i, d],
            full_rs.at[i, d],
            "head",
            lax.rem(me + d, peers),
        )

    for i in range(n_sum):
        for d in range(1, peers):
            send_sum(i, d).start()
    mine = rows_of(me)

    def total(i):
        found = sums[i][mine, :].astype(f32)
        for d in range(1, peers):
            send_sum(i, d).wait()
            found = found + recv[i][d].astype(f32)
        return found

    def spread(i, value):
        full[i][mine, :] = value.astype(full[i].dtype)
        for d in range(1, peers):
            send_full(i, d).start()

    body(mine, total, spread, aux, own)
    for i in range(n_full):
        for d in range(1, peers):
            send_full(i, d).wait()


def close(name, collective_id, body, sums, aux, full, own, peers):
    count, width = sums[0].shape
    vmem = pl.BlockSpec(memory_space=pltpu.VMEM)
    dma = pltpu.SemaphoreType.DMA
    return pl.pallas_call(
        functools.partial(
            close_kernel,
            body=body,
            n_sum=len(sums),
            n_aux=len(aux),
            n_full=len(full),
            n_own=len(own),
            peers=peers,
        ),
        out_shape=tuple(full) + tuple(own),
        in_specs=[vmem] * (len(sums) + len(aux)),
        out_specs=(vmem,) * (len(full) + len(own)),
        scratch_shapes=[pltpu.VMEM((peers, count // peers, width), bf16) for _ in sums]
        + [dma((len(sums), peers))] * 2
        + [dma((len(full), peers))] * 2,
        compiler_params=pltpu.CompilerParams(
            vmem_limit_bytes=40 * MIB, collective_id=collective_id, has_side_effects=True
        ),
        cost_estimate=pl.CostEstimate(flops=10**6, bytes_accessed=30 * MIB, transcendentals=0),
        name=name,
    )(*sums, *aux)


def row_mean(x):
    return jnp.mean(x, axis=1, keepdims=True)


def col_sum(x):
    return jnp.sum(x, axis=0, keepdims=True)


def close_attn(mine, total, spread, aux, own):
    inputs_ref, gain_ref = aux
    middle_ref, small_ref = own
    branch = total(0)
    middle = inputs_ref[mine, :].astype(f32) + branch
    hat = middle * lax.rsqrt(row_mean(middle * middle) + eps)
    spread(0, hat * gain_ref[...])
    middle_ref[...] = middle
    small_ref[...] = col_sum(branch * branch)


def folded(line):
    return jnp.concatenate([line[:, 128 * i : 128 * i + 128] for i in range(8)], axis=0)


def fold_sum(line):
    return col_sum(folded(line))


def finish_kernel(
    back_ref,
    feed_ref,
    in_ref,
    gain_ref,
    grad_middle_ref,
    middle_ref,
    gain_line_ref,
    attn_line_ref,
    extra_ref,
    grad_a,
    grad_b,
    input_grad_ref,
    layer_ref,
    out_a,
    out_b,
    small_ref,
    back_recv,
    feed_recv,
    in_a,
    in_b,
    in_c,
    in_d,
    in_e,
    res_a,
    res_b,
    res_c,
    res_d,
    res_e,
    small_head,
    small_seq,
    small_send,
    sum_ss,
    sum_rs,
    full_ss,
    full_rs,
    sh_ss,
    sh_rs,
    sq_ss,
    sq_rs,
    sem_a,
    sem_b,
    sem_c,
    sem_d,
    sem_e,
    sem_f,
    *,
    parts,
    peers,
):
    count = back_ref.shape[0]
    share = count // peers
    me, head = lax.axis_index("seq"), lax.axis_index("head")
    greet(seq=parts, head=peers)

    def share_of(peer):
        return pl.ds(pl.multiple_of(peer * share, share), share)

    def send_sum(i, d):
        peer = lax.rem(head + d, peers)
        src, recv = ((back_ref, back_recv), (feed_ref, feed_recv))[i]
        return send(
            src.at[share_of(peer)], recv.at[d], sum_ss.at[i, d], sum_rs.at[i, d], "head", peer
        )

    for i in range(2):
        for d in range(1, peers):
            send_sum(i, d).start()

    scatter = ScatterSum(
        ((grad_a, in_a, in_b, in_c, in_d, in_e), (grad_b, res_a, res_b, res_c, res_d, res_e)),
        (sem_a, sem_b, sem_c, sem_d, sem_e, sem_f),
        parts,
    )
    for far in (True, False):
        for side in range(2):
            scatter.start(far, side)

    mine = share_of(head)

    def total(i):
        src, recv = ((back_ref, back_recv), (feed_ref, feed_recv))[i]
        found = src[mine, :].astype(f32)
        for d in range(1, peers):
            send_sum(i, d).wait()
            found = found + recv[d].astype(f32)
        return found

    def send_full(i, d):
        full = (input_grad_ref, layer_ref)[i]
        return send(
            full.at[mine],
            full.at[mine],
            full_ss.at[i, d],
            full_rs.at[i, d],
            "head",
            lax.rem(head + d, peers),
        )

    tokens = in_ref[mine, :].astype(f32)
    scale = lax.rsqrt(row_mean(tokens * tokens) + eps)
    hat = tokens * scale
    grad_normed = total(0)
    g = grad_normed * gain_ref[...]
    back = grad_middle_ref[...] + scale * (g - hat * row_mean(g * hat))
    input_grad_ref[mine, :] = back.astype(bf16)
    for d in range(1, peers):
        send_full(0, d).start()
    scatter.pair(True)
    small_send[0:8] = folded(col_sum(grad_normed * hat))
    small_send[8:16] = folded(gain_line_ref[...])
    branch = total(1)
    layer = middle_ref[...] + branch
    layer_ref[mine, :] = layer.astype(bf16)
    for d in range(1, peers):
        send_full(1, d).start()
    small_send[16:24] = extra_ref[...]
    small_send[16:17] = fold_sum(col_sum(layer * layer))
    small_send[17:18] = fold_sum(attn_line_ref[...])
    small_send[18:19] = fold_sum(col_sum(branch * branch))

    def send_head(d):
        peer = lax.rem(head + d, peers)
        return send(small_send, small_head.at[d], sh_ss.at[d], sh_rs.at[d], "head", peer)

    for d in range(1, peers):
        send_head(d).start()

    scatter.far()

    kept = lax.broadcasted_iota(jnp.int32, (24, 128), 0) < 19
    found = small_send[...]
    for d in range(1, peers):
        send_head(d).wait()
        found = found + jnp.where(kept, small_head[d], 0.0)
    small_seq[0] = found

    def send_seq(d):
        peer = lax.rem(me + d, parts)
        return send(small_seq.at[0], small_seq.at[d], sq_ss.at[d], sq_rs.at[d], "seq", peer)

    def start_seq(d, carry):
        send_seq(d).start()
        return carry

    lax.fori_loop(1, parts, start_seq, 0)

    scatter.pair(False)
    scatter.settle((out_a, out_b))
    small_ref[...] = small_seq[0]

    def add_seq(d, carry):
        send_seq(d).wait()
        small_ref[...] += small_seq[d]
        return carry

    lax.fori_loop(1, parts, add_seq, 0)
    for i in range(2):
        for d in range(1, peers):
            send_full(i, d).wait()


def finish(back, feed, x, gain, grad_middle, middle, gain_line, attn_line, extra, grad_a, grad_b, parts, peers):
    count, width = back.shape
    share, own = count // peers, grad_a.shape[0] // parts
    slots, sems = ScatterSum.scratch((grad_a, grad_b), parts)
    wide_a, wide_b = grad_a.shape[1], grad_b.shape[1]
    vmem = pl.BlockSpec(memory_space=pltpu.VMEM)
    dma = pltpu.SemaphoreType.DMA
    return pl.pallas_call(
        functools.partial(finish_kernel, parts=parts, peers=peers),
        out_shape=(
            jax.ShapeDtypeStruct((count, width), bf16),
            jax.ShapeDtypeStruct((count, width), bf16),
            jax.ShapeDtypeStruct((own, wide_a), f32),
            jax.ShapeDtypeStruct((own, wide_b), f32),
            jax.ShapeDtypeStruct((24, 128), f32),
        ),
        in_specs=[vmem] * 11,
        out_specs=(vmem,) * 5,
        scratch_shapes=[pltpu.VMEM((peers, share, width), bf16)] * 2
        + slots
        + [
            pltpu.VMEM((peers, 24, 128), f32),
            pltpu.VMEM((parts, 24, 128), f32),
            pltpu.VMEM((24, 128), f32),
        ]
        + [dma((2, peers))] * 4
        + [dma((peers,))] * 2
        + [dma((parts,))] * 2
        + sems,
        compiler_params=pltpu.CompilerParams(
            vmem_limit_bytes=40 * MIB, collective_id=5, has_side_effects=True
        ),
        cost_estimate=pl.CostEstimate(flops=10**7, bytes_accessed=100 * MIB, transcendentals=0),
        name="finish",
    )(back, feed, x, gain, grad_middle, middle, gain_line, attn_line, extra, grad_a, grad_b)


def norm_stats(values):
    row_scale = lax.rsqrt(jnp.mean(values * values, axis=-1, keepdims=True) + eps)
    return (values * row_scale, row_scale)


def exchange(value):
    return lax.all_to_all(value, "seq", split_axis=0, concat_axis=0, tiled=True)


def per_device(
    inputs,
    cotangent,
    query_weight,
    key_weight,
    value_weight,
    output_weight,
    up_weight,
    down_weight,
    first_gain,
    second_gain,
    position_bias,
    gate_bias,
    memory_table,
    retrieved,
    lengths,
):
    _, block_len, model_width = inputs.shape
    bucket_total = position_bias.shape[1]
    seq_count = lax.axis_size("seq")
    slot_count = memory_table.shape[0]

    wanted = jnp.transpose(retrieved[0], (1, 0, 2))
    token = jnp.arange(block_len, dtype=jnp.int32)[None, :, None]
    codes = (wanted // slot_count) * (block_len * slot_count) + token * slot_count + wanted % slot_count
    codes = lax.sort(codes.reshape(2, -1), dimension=1, is_stable=False)
    codes = jnp.transpose(codes.reshape(2, seq_count, -1), (1, 0, 2))
    codes = exchange(codes)
    slots = codes % slot_count
    tok = (codes // slot_count) % block_len
    rows = gather_rows(slots, memory_table)

    hot, outside = diagonal_buckets(block_len, bucket_total)
    bias_row = jnp.dot(position_bias, hot, precision=highest) + outside[None]

    x, cot = inputs[0], cotangent[0]
    peers = lax.axis_size("head")
    gain_one, gain_two = first_gain[None], second_gain[None]
    gate_flat = jax.nn.sigmoid(gate_bias)
    hat_one, _ = norm_stats(x.astype(f32))
    normed_one = (hat_one * first_gain).astype(bf16)
    queries = nn(normed_one, query_weight).astype(bf16)
    keys = nn(normed_one, key_weight).astype(bf16)
    values = nn(normed_one, value_weight).astype(bf16)
    q_all = lax.all_gather(queries, "seq", axis=0)

    mixed, recalled, local_out, logs, window_weights, pair = attend(
        lengths[0], gate_flat, queries, keys, values, bias_row, q_all, tok, rows
    )

    def whole(dtype):
        return jax.ShapeDtypeStruct((block_len, model_width), dtype)

    def lines(count):
        return jax.ShapeDtypeStruct((count, model_width), f32)

    chunk = lines(block_len // peers)
    normed_two, middle, attn_line = close(
        "close_attn",
        3,
        close_attn,
        [nn(mixed, output_weight).astype(bf16)],
        [x, gain_two],
        [whole(bf16)],
        [chunk, lines(1)],
        peers,
    )
    upward = nn(normed_two, up_weight)
    gelu_value, gelu_back = jax.vjp(jax.nn.gelu, upward)
    hidden = gelu_value.astype(bf16)
    grad_upward = gelu_back(nt(cot, down_weight))[0].astype(bf16)
    grad_branch, grad_middle, gain_line, grad_heads, pos_rows, gate_rows, up_grad, down_grad = attend_back(
        gate_flat,
        nt(grad_upward, up_weight).astype(bf16),
        cot,
        gain_two,
        middle,
        output_weight,
        queries,
        recalled,
        local_out,
        logs,
        window_weights,
        pair,
        q_all,
        tok,
        tn(normed_two, grad_upward).astype(bf16),
        tn(cot, hidden).astype(bf16),
        rows,
        peers,
    )
    feed = nn(hidden, down_weight).astype(bf16)
    gate_part = jnp.sum(gate_rows, axis=1) * gate_flat * (1.0 - gate_flat)
    position_part = jnp.dot(pos_rows, hot.T, precision=highest)
    extra = jnp.zeros((8, 128), f32)
    extra = extra.at[3:5, :bucket_total].set(position_part).at[5, :2].set(gate_part)
    back = (
        nt(grad_heads[:, :256], query_weight)
        + nt(grad_heads[:, 256:512], key_weight)
        + nt(grad_heads[:, 512:], value_weight)
    )
    input_grad, layer_out, grads_in, grads_out, small = finish(
        back.astype(bf16),
        feed,
        x,
        gain_one,
        grad_middle,
        middle,
        gain_line,
        attn_line,
        extra,
        tn(normed_one, grad_heads).astype(bf16),
        tn(grad_branch, mixed).astype(bf16),
        seq_count,
        peers,
    )
    entry_count = float(block_len * model_width * seq_count)
    share = model_width // seq_count
    gains = small[:16].reshape(2, model_width)
    own_gains = lax.dynamic_slice_in_dim(gains, lax.axis_index("seq") * share, share, 1)
    return (
        layer_out[None],
        input_grad.astype(f32)[None],
        grads_in[:, 0:256],
        grads_in[:, 256:512],
        grads_in[:, 512:768],
        grads_out.T,
        up_grad,
        down_grad,
        own_gains[0],
        own_gains[1],
        small[19:21, :bucket_total],
        small[21, :2],
        jnp.sqrt(jnp.sum(small[16:19], axis=1) / entry_count),
    )


def solution(mesh):
    in_specs = (
        P(None, "seq", None),
        P(None, "seq", None),
        P(None, "head"),
        P(None, "head"),
        P(None, "head"),
        P("head", None),
        P(None, "head"),
        P("head", None),
        P(),
        P(),
        P("head", None),
        P("head"),
        P("seq", "head", None),
        P(None, "seq", "head", None),
        P(),
    )
    out_specs = (
        P(None, "seq", None),
        P(None, "seq", None),
        P("seq", "head"),
        P("seq", "head"),
        P("seq", "head"),
        P("head", "seq"),
        P("seq", "head"),
        P("head", "seq"),
        P("seq"),
        P("seq"),
        P("head", None),
        P("head"),
        P(),
    )
    return jax.shard_map(
        per_device, mesh=mesh, in_specs=in_specs, out_specs=out_specs, check_vma=False
    )
```

time: 510 us -> 312 us (0.61)
  waiting for transfers between devices: 226 us -> 6.39 us
  Pallas kernels: 63.5 us -> 218 us
  blocking collectives: 69 us -> 0 us
  starting transfers between devices: 30 us -> 7.3 us
  local copies, waits for them, and re-layouts: 53.7 us -> 32.4 us
  other arithmetic: 24.9 us -> 7.22 us
    pallas_call x4, Pallas kernels: 29 us -> 184 us  [the longest x1 93.7 us: attend_back(): pl.pallas_call(functools.partial(attend_back_kernel, parts=parts, peers=p...]
    unnamed x9 -> x1, waiting for transfers between devices: 89.5 us -> 0.02 us
    psum x3 -> x0, waiting for transfers between devices: 83.1 us -> none  [head_sum(): return lax.psum(value.astype(bf16), 'head').astype(f32)]
    psum x1 -> x0, blocking collectives: 38.2 us -> none  [per_device(): lax.psum((position_part, gate_part, square_parts, jnp.stack((first_gain_p...]
    all_gather x1 -> x0, blocking collectives: 30.8 us -> none  [per_device(): stats_all = lax.all_gather(stats, 'seq', axis=0)]
    all_to_all x4 -> x1, waiting for transfers between devices: 26.5 us -> 6.37 us  [exchange(): return lax.all_to_all(value, 'seq', split_axis=0, concat_axis=0, tiled=True)]
    unnamed x89 -> x103, local copies, waits for them, and re-layouts: 34.8 us -> 16.7 us
    ppermute x4 -> x0, waiting for transfers between devices: 18 us -> none  [from_behind(): lax.ppermute(value, axis, [(source, source + steps) for source in range(f...]
  transfers between devices with their start and end apart: 15 -> 2, of which waited for: 10 -> 1; matrix products, arithmetic and copies ran while one was open for 8% -> 2% of each run, Pallas kernels for 10% -> 11%
where the time goes in v2:
time: 312 us; the launch traced here: 311 us
  Pallas kernels  218 us (70%)
  local copies, waits for them, and re-layouts  32.4 us (10%)
  matrix products  23.3 us (7%)
  between operations  16 us (5%)
  starting transfers between devices  7.3 us (2%)
  other arithmetic  7.22 us (2%)
  waiting for transfers between devices  6.39 us (2%)
    pallas_call x1, Pallas kernels, attend_back(): pl.pallas_call(functools.partial(attend_back_kernel, parts=parts, peers=p...  93.7 us
    pallas_call x1, Pallas kernels, finish(): pl.pallas_call(functools.partial(finish_kernel, parts=parts, peers=peers)...  40.1 us
    pallas_call x1, Pallas kernels, attend(): pl.pallas_call(functools.partial(attend_kernel, parts=parts, scale=128 **...  35.3 us
    pallas_call x1, Pallas kernels, gather_rows(): pl.pallas_call(functools.partial(gather_kernel, rows=rows, chunk=chunk, c...  34.5 us
    unnamed x103, local copies, waits for them, and re-layouts  16.7 us
    pallas_call x1, Pallas kernels, close(): pl.pallas_call(functools.partial(close_kernel, body=body, n_sum=len(sums)...  14.6 us
    sort x2, local copies, waits for them, and re-layouts, per_device(): codes = lax.sort(codes.reshape(2, -1), dimension=1, is_stable=False)  11.5 us
    dot_general x6, matrix products, nn(): lax.dot_general(a, b, (((1,), (0,)), ((), ())), preferred_element_type=f32)  9 us
  transfers between devices with their start and end apart: 2, of which 1 were waited for; matrix products, arithmetic and copies ran while one was open for 2% of the time, Pallas kernels for 11%

profile of v2, /device:TPU:0, one launch (start us, length us, event | category | flops | bytes accessed | tf_op | source)
XLA Modules:
  0.0 310.8 jit_solution(1849983953234874199)
XLA Ops:
  8.1 1.1 fusion.18
  9.3 0.8 reshape.114
  10.2 1.3 fusion.2
  11.5 2.2 convolution_convert_fusion.8.q_ref
  14.6 2.1 convolution_convert_fusion.7.k_ref
  16.6 1.0 convolution_convert_fusion.6.v_ref
  17.6 11.5 %sort.9.cloned.1.call-done = s32[2,8192]{1,0:T(2,128)} async-done(((s32[2,8192]{1,0:T(2,128)}), s32[2,8192]{1,0:T(2,128)}) %sort.9.cloned.1.call-update) | async-done | bytes 65552 | tf_op jit(solution)/shard_map/sort | solution.py:1173
  29.1 7.3 %all-to-all-start = ((s32[8,2,1024]{2,1,0:T(2,128)}), s32[8,2,1024]{2,1,0:T(2,128)S(1)}, u32[]{:S(2)}, u32[]{:S(2)}) async-start(s32[8,2,1024]{2,1,0:T(2,128)} %bitcast.95), calls=%async_computation | async-start | bytes 131072 | tf_op jit(solution)/shard_map/all_to_all | solution.py:1145
  36.9 6.4 %all-to-all-done = s32[8,2,1024]{2,1,0:T(2,128)S(1)} async-done(((s32[8,2,1024]{2,1,0:T(2,128)}), s32[8,2,1024]{2,1,0:T(2,128)S(1)}, u32[]{:S(2)}, u32[]{:S(2)}) %all-to-all-start) | async-done | bytes 65568 | tf_op jit(solution)/shard_map/all_to_all | solution.py:1145
  43.3 0.9 fusion.19
  44.3 34.5 %gather_rows.1.rows_hbm = bf16[8,2,1024,256]{3,2,1,0:T(8,128)(2,1)S(1)} custom-call(s32[8,2,1,1024]{3,2,1,0:T(1,128)S(1)} %copy.35.codes_ref, bf16[8192,2,256]{2,1,0:T(2,128)(2,1)} %table_ref.1), custom_call_target="tpu_custom_call" | custom-call | bytes 104857600 | tf_op jit(solution)/shard_map/gather_rows/pallas_call | solution.py:105
  78.9 3.3 %copy-done.1 = bf16[8,2,1024,256]{3,2,1,0:T(8,128)(2,1)} copy-done((bf16[8,2,1024,256]{3,2,1,0:T(8,128)(2,1)}, bf16[8,2,1024,256]{3,2,1,0:T(8,128)(2,1)S(1)}, u32[]{:S(2)}) %copy-start.1) | copy-done | bytes 8388632
  82.2 35.3 %attend.1 = (bf16[256,256]{1,0:T(8,128)(2,1)}, f32[256,256]{1,0:T(8,128)}, f32[256,256]{1,0:T(8,128)}, f32[8,256]{1,0:T(8,128)}, f32[2,256,768]{2,1,0:T(8,128)}, /*index=5*/bf16[2,768,256]{2,1,0:T(8,128)(2,1)}) custom-call(s32[4]{0:T(128)} %bitcast.96, f32[2]{0:T(128)} %add_divide_fusion.gate_ref, bf16[256,256]{1,0:T(8,128)(2,1)} %convolution_convert_fusion.8.q_ref, ...), custom_call_target="tpu_custom_call" | custom-call | flops 3000000000 | bytes 104857600 | tf_op jit(solution)/shard_map/attend/pallas_call | solution.py:336
  117.5 1.4 convolution_convert_fusion.3.refs_0_
  118.9 14.6 %close_attn.1 = (bf16[256,1024]{1,0:T(8,128)(2,1)S(1)}, f32[64,1024]{1,0:T(8,128)S(1)}, f32[1,1024]{1,0:T(1,128)S(1)}) custom-call(bf16[256,1024]{1,0:T(8,128)(2,1)S(1)} %convolution_convert_fusion.3.refs_0_, bf16[256,1024]{1,0:T(8,128)(2,1)S(1)} %bitcast.85, f32[1,1024]{1,0:T(1,128)S(1)} %bitcast.93), custom_call_target="tpu_custom_call" | custom-call | flops 1000000 | bytes 31457280 | tf_op jit(solution)/shard_map/close_attn/pallas_call | solution.py:889
  134.3 1.6 convolution_convert_fusion.4.feed_ref
  135.9 1.2 fusion.11
  137.1 2.2 convert_bitcast_fusion.down_ref
  142.0 93.7 %attend_back.1 = (bf16[256,1024]{1,0:T(8,128)(2,1)S(1)}, f32[64,1024]{1,0:T(8,128)S(1)}, f32[1,1024]{1,0:T(1,128)S(1)}, bf16[256,768]{1,0:T(8,128)(2,1)S(1)}, f3...) custom-call(f32[2]{0:T(128)S(1)} %copy-done.35, ...), custom_call_target="tpu_custom_call" | custom-call | flops 4000000000 | bytes 157286400 | tf_op jit(solution)/shard_map/attend_back/pallas_call | solution.py:784
  236.3 1.5 fusion.14
  237.8 1.9 convolution_convert_fusion.1.grad_a
  240.4 1.3 fusion.37
  241.7 2.2 convolution_convert_fusion.2.grad_b
  244.0 1.4 convolution_add_fusion.1
  246.5 1.4 copy-done.3
  247.9 1.0 copy-done.5
  248.9 0.9 copy-done.8
  249.9 1.0 copy-done.21
  250.9 0.9 copy-done.26
  251.9 40.1 %finish.1 = (bf16[256,1024]{1,0:T(8,128)(2,1)S(1)}, bf16[256,1024]{1,0:T(8,128)(2,1)S(1)}, f32[128,768]{1,0:T(8,128)S(1)}, f32[128,256]{1,0:T(8,128)S(1)}, f32[24,128]{1,0:T(8,128)S(1)}) custom-call(bf16[256,1024]{1,0:T(8,128)(2,1)S(1)} %fusion.back_ref, bf16[256,1024]{1,0:T(8,128)(2,1)S(1)} %copy-done.21, bf16[256,1024]{1,0:T(8,128)(2,1)S(1)} %bitcast.86, ...), custom_call_target="tpu_custom_call" | custom-call | flops 10000000 | bytes 104857600 | tf_op jit(solution)/shard_map/finish/pallas_call | solution.py:1109
  296.5 1.7 copy.37
  298.9 2.1 bitcast_convert_fusion
  (123 shorter events, 15.0 us)
Async XLA Ops:
  8.0 126.3 %copy-start = (bf16[1024,1024]{1,0:T(8,128)(2,1)S(1)}, bf16[1024,1024]{1,0:T(8,128)(2,1)}, u32[]{:S(2)}) copy-start(bf16[1024,1024]{1,0:T(8,128)(2,1)} %param.29) | copy-start | bytes 6291460
  8.0 5.7 %copy-start.45 = (f32[768]{0:T(1024)S(1)}, f32[768]{0:T(1024)}, u32[]{:S(2)}) copy-start(f32[768]{0:T(1024)} %constant.164) | copy-start | bytes 9220
  8.0 5.7 %copy-start.42 = (f32[32,768]{1,0:T(8,128)S(1)}, f32[32,768]{1,0:T(8,128)}, u32[]{:S(2)}) copy-start(f32[32,768]{1,0:T(8,128)} %constant.155.clone) | copy-start | bytes 294916
  8.1 6.5 %copy-start.2 = (bf16[1,256,1024]{2,1,0:T(8,128)(2,1)S(1)}, bf16[1,256,1024]{2,1,0:T(8,128)(2,1)}, u32[]{:S(2)}) copy-start(bf16[1,256,1024]{2,1,0:T(8,128)(2,1)} %param.22) | copy-start | bytes 1572868
  8.1 6.5 %copy-start.28 = (f32[1024]{0:T(1024)S(1)}, f32[1024]{0:T(1024)}, u32[]{:S(2)}) copy-start(f32[1024]{0:T(1024)} %param.30) | copy-start | bytes 12292
  8.1 5.7 %copy-start.46 = (f32[2,32]{1,0:T(2,128)S(1)}, f32[2,32]{1,0:T(2,128)}, u32[]{:S(2)}) copy-start(f32[2,32]{1,0:T(2,128)} %param.32) | copy-start | bytes 772
  8.1 21.1 %sort.9.cloned.1.call-start = ((), (), s32[]{:S(2)}) async-start(), calls=%async_computation.2 | async-start | bytes 196640 | tf_op jit(solution)/shard_map/sort | solution.py:1173
  10.1 6.5 %copy-start.38 = (bf16[1024,256]{1,0:T(8,128)(2,1)S(1)}, bf16[1024,256]{1,0:T(8,128)(2,1)}, u32[]{:S(2)}) copy-start(bf16[1024,256]{1,0:T(8,128)(2,1)} %param.26) | copy-start | bytes 1572868
  10.2 72.0 %all-gather.3.cloned.1.call-start = ((), (), s32[]{:S(2)}) async-start(), calls=%async_computation.1 | async-start | bytes 1179648 | tf_op jit(solution)/shard_map/all_gather | solution.py:1192
  11.5 6.2 %copy-start.43 = (f32[256]{0:T(256)}, f32[256]{0:T(256)S(1)}, u32[]{:S(2)}) copy-start(f32[256]{0:T(256)S(1)} %add_rsqrt_fusion) | copy-start | bytes 3076
  13.7 22.7 %copy-start.47 = (f32[2]{0:T(128)S(1)}, f32[2]{0:T(128)}, u32[]{:S(2)}) copy-start(f32[2]{0:T(128)} %param.33) | copy-start | bytes 28
  29.1 14.2 %all-to-all-start = ((s32[8,2,1024]{2,1,0:T(2,128)}), s32[8,2,1024]{2,1,0:T(2,128)S(1)}, u32[]{:S(2)}, u32[]{:S(2)}) async-start(s32[8,2,1024]{2,1,0:T(2,128)} %bitcast.95), calls=%async_computation | async-start | bytes 131072 | tf_op jit(solution)/shard_map/all_to_all | solution.py:1145
  78.9 3.3 %copy-start.1 = (bf16[8,2,1024,256]{3,2,1,0:T(8,128)(2,1)}, bf16[8,2,1024,256]{3,2,1,0:T(8,128)(2,1)S(1)}, u32[]{:S(2)}) copy-start(bf16[8,2,1024,256]{3,2,1,0:T(8,128)(2,1)S(1)} %gather_rows.1.rows_hbm) | copy-start | bytes 25165828
  82.2 35.3 %copy-start.4 = (bf16[256,1024]{1,0:T(8,128)(2,1)S(1)}, bf16[256,1024]{1,0:T(8,128)(2,1)}, u32[]{:S(2)}) copy-start(bf16[256,1024]{1,0:T(8,128)(2,1)} %weight_ref.1) | copy-start | bytes 1572868
  82.2 36.7 %copy-start.29 = (f32[1024]{0:T(1024)S(1)}, f32[1024]{0:T(1024)}, u32[]{:S(2)}) copy-start(f32[1024]{0:T(1024)} %param.31) | copy-start | bytes 12292
  117.5 16.1 %copy-start.37 = (bf16[1024,1024]{1,0:T(8,128)(2,1)S(1)}, bf16[1024,1024]{1,0:T(8,128)(2,1)}, u32[]{:S(2)}) copy-start(bf16[1024,1024]{1,0:T(8,128)(2,1)} %param.28) | copy-start | bytes 6291460
  133.5 7.4 %copy-start.7 = (f32[64,1024]{1,0:T(8,128)}, f32[64,1024]{1,0:T(8,128)S(1)}, u32[]{:S(2)}) copy-start(f32[64,1024]{1,0:T(8,128)S(1)} %get-tuple-element.61.middle_ref) | copy-start | bytes 786436
  141.9 94.3 %copy-start.41 = (bf16[1024,256]{1,0:T(8,128)(2,1)S(1)}, bf16[1024,256]{1,0:T(8,128)(2,1)}, u32[]{:S(2)}) copy-start(bf16[1024,256]{1,0:T(8,128)(2,1)} %param.24) | copy-start | bytes 1572868
  141.9 95.8 %copy-start.44 = (f32[256]{0:T(256)S(1)}, f32[256]{0:T(256)}, u32[]{:S(2)}) copy-start(f32[256]{0:T(256)} %copy-done.43) | copy-start | bytes 3076
  236.2 3.5 %copy-start.14 = (f32[1024,128]{1,0:T(8,128)}, f32[1024,128]{1,0:T(8,128)S(1)}, u32[]{:S(2)}) copy-start(f32[1024,128]{1,0:T(8,128)S(1)} %get-tuple-element.134) | copy-start | bytes 1572868
  236.2 3.5 %copy-start.16 = (f32[128,1024]{1,0:T(8,128)}, f32[128,1024]{1,0:T(8,128)S(1)}, u32[]{:S(2)}) copy-start(f32[128,1024]{1,0:T(8,128)S(1)} %get-tuple-element.133) | copy-start | bytes 1572868
  236.2 3.5 %copy-start.20 = (bf16[256,1024]{1,0:T(8,128)(2,1)}, bf16[256,1024]{1,0:T(8,128)(2,1)S(1)}, u32[]{:S(2)}) copy-start(bf16[256,1024]{1,0:T(8,128)(2,1)S(1)} %get-tuple-element.73) | copy-start | bytes 1572868
  236.2 3.5 %copy-start.25 = (f32[64,1024]{1,0:T(8,128)}, f32[64,1024]{1,0:T(8,128)S(1)}, u32[]{:S(2)}) copy-start(f32[64,1024]{1,0:T(8,128)S(1)} %get-tuple-element.68.grad_middle_ref) | copy-start | bytes 786436
  236.2 3.5 %copy-start.31 = (f32[1,1024]{1,0:T(1,128)}, f32[1,1024]{1,0:T(1,128)S(1)}, u32[]{:S(2)}) copy-start(f32[1,1024]{1,0:T(1,128)S(1)} %get-tuple-element.69.gain_line_ref) | copy-start | bytes 12292
  236.2 3.5 %copy-start.34 = (f32[2,128]{1,0:T(2,128)S(1)}, f32[2,128]{1,0:T(2,128)}, u32[]{:S(2)}) copy-start(f32[2,128]{1,0:T(2,128)} %copy-done.33) | copy-start | bytes 3076
  236.2 3.6 %copy-start.48 = (f32[2]{0:T(128)S(1)}, f32[2]{0:T(128)}, u32[]{:S(2)}) copy-start(f32[2]{0:T(128)} %param.33) | copy-start | bytes 28
  236.3 5.5 %copy-start.40 = (bf16[256,256]{1,0:T(8,128)(2,1)S(1)}, bf16[256,256]{1,0:T(8,128)(2,1)}, u32[]{:S(2)}) copy-start(bf16[256,256]{1,0:T(8,128)(2,1)} %get-tuple-element.59) | copy-start | bytes 393220
  239.8 4.1 %copy-start.36 = (f32[256,1024]{1,0:T(8,128)S(1)}, f32[256,1024]{1,0:T(8,128)}, u32[]{:S(2)}) copy-start(f32[256,1024]{1,0:T(8,128)} %fusion.14) | copy-start | bytes 3145732
  240.4 5.0 %copy-start.39 = (bf16[1024,256]{1,0:T(8,128)(2,1)S(1)}, bf16[1024,256]{1,0:T(8,128)(2,1)}, u32[]{:S(2)}) copy-start(bf16[1024,256]{1,0:T(8,128)(2,1)} %param.26) | copy-start | bytes 1572868
  294.2 7.6 %copy-start.17 = (f32[128,1024]{1,0:T(8,128)S(1)}, f32[128,1024]{1,0:T(8,128)}, u32[]{:S(2)}) copy-start(f32[128,1024]{1,0:T(8,128)} %copy-done.16) | copy-start | bytes 1572868
  294.2 6.8 %copy-start.19 = (bf16[256,1024]{1,0:T(8,128)(2,1)S(1)}, bf16[256,1024]{1,0:T(8,128)(2,1)}, u32[]{:S(2)}) copy-start(bf16[256,1024]{1,0:T(8,128)(2,1)} %copy-done.18) | copy-start | bytes 1572868
  298.1 4.5 %copy-start.15 = (f32[1024,128]{1,0:T(8,128)S(1)}, f32[1024,128]{1,0:T(8,128)}, u32[]{:S(2)}) copy-start(f32[1024,128]{1,0:T(8,128)} %copy-done.14) | copy-start | bytes 1572868
  (20 other events, 27.8 us)
Sparse Core Ops, SparseCore 0:
  11.9 16.9 sort.11.cloned.1.call-done
  (1 shorter events, 0.0 us)
Sparse Core Ops, SparseCore 1:
  13.8 43.1 all-gather.2

commit v3 on v2

--- a/solution.py
+++ b/solution.py
@@ -55,69 +55,83 @@
     return lax.dot_general(a, b, (((0,), (0,)), ((), ())), preferred_element_type=f32)
 
 
-def gather_kernel(codes_ref, table_ref, out_ref, wide, buf, *, rows, chunk, chunks, unroll, group):
-    step = pl.program_id(0)
-    part = 32
-
-    @pl.when(step < chunks)
-    def _():
-        def widen(q, carry):
-            x = table_ref[pl.ds(q * part, part)].astype(f32)
-            base = step * chunk + q * part
+def widen_kernel(table_hbm, wide_ref, buf, sem, *, chunk, part):
+    chunks = table_hbm.shape[0] // chunk
+
+    def fetch(i):
+        return pltpu.make_async_copy(
+            table_hbm.at[pl.ds(i * chunk, chunk)], buf.at[i % 2], sem.at[i % 2]
+        )
+
+    fetch(0).start()
+    for i in range(chunks):
+        fetch(i).wait()
+        if i + 1 < chunks:
+            fetch(i + 1).start()
+
+        def widen(q, carry, i=i):
+            x = buf[i % 2, pl.ds(q * part, part)].astype(f32)
+            base = i * chunk + q * part
             for r in range(part):
-                wide[pl.ds(4 * (base + r), 2), :] = x[r, :, 0:128]
-                wide[pl.ds(4 * (base + r) + 2, 2), :] = x[r, :, 128:256]
+                wide_ref[pl.ds(4 * (base + r), 2), :] = x[r, :, 0:128]
+                wide_ref[pl.ds(4 * (base + r) + 2, 2), :] = x[r, :, 128:256]
             return carry
 
         lax.fori_loop(0, chunk // part, widen, 0)
 
-    @pl.when(step >= chunks)
-    def _():
-        head = (step - chunks) % 2
-
-        def copy_rows(i, carry):
-            base = i * unroll
+
+def widen(table):
+    total = table.shape[0]
+    chunk = min(1024, total)
+    return pl.pallas_call(
+        functools.partial(widen_kernel, chunk=chunk, part=32),
+        out_shape=jax.ShapeDtypeStruct((4 * total, 128), f32),
+        in_specs=[pl.BlockSpec(memory_space=pl.ANY)],
+        out_specs=pl.BlockSpec(memory_space=pltpu.VMEM),
+        scratch_shapes=[pltpu.VMEM((2, chunk, 2, 256), bf16), pltpu.SemaphoreType.DMA((2,))],
+        compiler_params=pltpu.CompilerParams(vmem_limit_bytes=24 * MIB),
+        cost_estimate=pl.CostEstimate(flops=0, bytes_accessed=40 * MIB, transcendentals=0),
+        name="widen",
+    )(table)
+
+
+def gather_kernel(at_ref, wide_ref, out_ref, buf, *, unroll, group):
+    groups, rows = out_ref.shape[0], out_ref.shape[1]
+
+    def one(i, carry):
+        def copy_rows(q, carry):
+            base = q * unroll
             for g in range(0, unroll, group):
                 found = [
-                    wide[pl.ds(codes_ref[0, 0, 0, base + g + u] * 4 + head, 2, 2), :]
-                    for u in range(group)
+                    wide_ref[pl.ds(at_ref[i * rows + base + g + u], 2, 2), :] for u in range(group)
                 ]
                 for u in range(group):
                     buf[pl.ds(2 * (base + g + u), 2), :] = found[u]
             return carry
 
         lax.fori_loop(0, rows // unroll, copy_rows, 0)
-        out_ref[0, 0, :, 0:128] = buf[pl.ds(0, rows, 2), :].astype(bf16)
-        out_ref[0, 0, :, 128:256] = buf[pl.ds(1, rows, 2), :].astype(bf16)
-
-
-def gather_rows(slots, table):
-    parts, heads, rows = slots.shape
-    total = table.shape[0]
-    chunk = min(1024, total)
-    chunks = total // chunk
+        out_ref[i, :, 0:128] = buf[pl.ds(0, rows, 2), :].astype(bf16)
+        out_ref[i, :, 128:256] = buf[pl.ds(1, rows, 2), :].astype(bf16)
+        return carry
+
+    lax.fori_loop(0, groups, one, 0)
+
+
+def gather_rows(places, wide):
+    parts, heads, rows = places.shape
     unroll = min(64, rows)
-
-    def place(i):
-        at = jnp.maximum(i - chunks, 0)
-        return (at // 2, at % 2, 0, 0)
-
-    return pl.pallas_call(
-        functools.partial(
-            gather_kernel, rows=rows, chunk=chunk, chunks=chunks, unroll=unroll, group=unroll // 2
-        ),
-        out_shape=jax.ShapeDtypeStruct((parts, heads, rows, 256), bf16),
-        grid=(chunks + parts * heads,),
-        in_specs=[
-            pl.BlockSpec((1, 1, 1, rows), place, memory_space=pltpu.SMEM),
-            pl.BlockSpec((chunk, 2, 256), lambda i: (jnp.minimum(i, chunks - 1), 0, 0)),
-        ],
-        out_specs=pl.BlockSpec((1, 1, rows, 256), place),
-        scratch_shapes=[pltpu.VMEM((4 * total, 128), f32), pltpu.VMEM((2 * rows, 128), f32)],
-        compiler_params=pltpu.CompilerParams(vmem_limit_bytes=40 * MIB),
+    vmem = pl.BlockSpec(memory_space=pltpu.VMEM)
+    found = pl.pallas_call(
+        functools.partial(gather_kernel, unroll=unroll, group=unroll // 2),
+        out_shape=jax.ShapeDtypeStruct((parts * heads, rows, 256), bf16),
+        in_specs=[pl.BlockSpec(memory_space=pltpu.SMEM), vmem],
+        out_specs=vmem,
+        scratch_shapes=[pltpu.VMEM((2 * rows, 128), f32)],
+        compiler_params=pltpu.CompilerParams(vmem_limit_bytes=32 * MIB),
         cost_estimate=pl.CostEstimate(flops=0, bytes_accessed=100 * MIB, transcendentals=0),
         name="gather_rows",
-    )(slots.reshape(parts, heads, 1, rows), table)
+    )(places.reshape(-1), wide)
+    return found.reshape(parts, heads, rows, 256)
 
 
 MESH = pl.DeviceIdType.MESH
@@ -168,6 +182,137 @@
     for i, column in enumerate(columns):
         wide = jnp.where(lane == i, column, wide)
     return wide
+
+
+def request_kernel(codes_ref, place_ref, tok_ref, got, own_sem, ss, rs, *, parts, slots, tokens):
+    rows = codes_ref.shape[1] // parts
+    me = lax.axis_index("seq")
+
+    def part(owner):
+        return codes_ref.at[:, pl.ds(pl.multiple_of(owner * rows, 128), rows)]
+
+    keep = pltpu.make_async_copy(part(me), got.at[0], own_sem)
+    keep.start()
+    greet(seq=parts)
+
+    def ask(d):
+        peer = lax.rem(me + d, parts)
+        return send(part(peer), got.at[d], ss.at[d], rs.at[d], "seq", peer)
+
+    def start(d, carry):
+        ask(d).start()
+        return carry
+
+    lax.fori_loop(1, parts, start, 0)
+    shift = slots.bit_length() - 1
+    head = lax.broadcasted_iota(jnp.int32, (2, rows), 0)
+
+    def read(d, j):
+        code = got[d]
+        place_ref[j] = (code & (slots - 1)) * 4 + head
+        tok_ref[j] = (code >> shift) & (tokens - 1)
+
+    keep.wait()
+    read(0, me)
+
+    def arrive(d, carry):
+        ask(d).wait()
+        read(d, lax.rem(me + parts - d, parts))
+        return carry
+
+    lax.fori_loop(1, parts, arrive, 0)
+
+
+def request(codes, parts, slots, tokens):
+    rows = codes.shape[1] // parts
+    vmem = pl.BlockSpec(memory_space=pltpu.VMEM)
+    dma = pltpu.SemaphoreType.DMA
+    shape = (parts, 2, rows)
+    return pl.pallas_call(
+        functools.partial(request_kernel, parts=parts, slots=slots, tokens=tokens),
+        out_shape=(jax.ShapeDtypeStruct(shape, jnp.int32),) * 2,
+        in_specs=[vmem],
+        out_specs=(vmem,) * 2,
+        scratch_shapes=[pltpu.VMEM(shape, jnp.int32), dma, dma((parts,)), dma((parts,))],
+        compiler_params=pltpu.CompilerParams(
+            vmem_limit_bytes=8 * MIB, collective_id=6, has_side_effects=True
+        ),
+        name="request",
+    )(codes)
+
+
+class HeadSum:
+    def __init__(self, src, scratch, sems, full=None, full_sems=None):
+        self.src, self.full = src, full
+        self.core_recv, self.side_send, self.side_recv = scratch
+        self.core_ss, self.core_rs, self.side_ss, self.side_rs = sems
+        self.full_sems = full_sems
+        head = lax.axis_index("head")
+        self.y, self.c = head // 2, lax.rem(head, 2)
+        self.share = src.shape[0] // 4
+        self.core = 2 * self.y + 1 - self.c
+        self.side = 2 * (1 - self.y) + self.c
+        self.mine = self.rows_of(head)
+
+    def rows_of(self, place):
+        return pl.ds(pl.multiple_of(place * self.share, self.share), self.share)
+
+    def to_core(self, i):
+        y = self.y if i == 0 else 1 - self.y
+        src = self.src.at[self.rows_of(2 * y + 1 - self.c)]
+        return send(src, self.core_recv.at[i], self.core_ss.at[i], self.core_rs.at[i], "head", self.core)
+
+    def to_side(self):
+        return send(self.side_send, self.side_recv, self.side_ss, self.side_rs, "head", self.side)
+
+    def start(self):
+        self.to_core(1).start()
+        self.to_core(0).start()
+
+    def relay(self):
+        self.to_core(1).wait()
+        other = self.src[self.rows_of(self.side), :].astype(f32)
+        self.side_send[...] = (other + self.core_recv[1].astype(f32)).astype(bf16)
+        self.to_side().start()
+
+    def total(self):
+        self.to_core(0).wait()
+        found = self.src[self.mine, :].astype(f32) + self.core_recv[0].astype(f32)
+        self.to_side().wait()
+        return found + self.side_recv[...].astype(f32)
+
+    def back(self, i):
+        rows = self.rows_of(self.side) if i == 2 else self.mine
+        peer = self.side if i == 1 else self.core
+        ss, rs = self.full_sems
+        return send(self.full.at[rows], self.full.at[rows], ss.at[i], rs.at[i], "head", peer)
+
+    def spread(self, value):
+        self.full[self.mine, :] = value.astype(self.full.dtype)
+        self.back(1).start()
+        self.back(0).start()
+
+    def forward(self):
+        self.back(1).wait()
+        self.back(2).start()
+
+    def settle(self):
+        self.back(0).wait()
+        self.back(2).wait()
+
+    @staticmethod
+    def scratch(count, width):
+        piece = (count // 4, width)
+        return [pltpu.VMEM((2,) + piece, bf16), pltpu.VMEM(piece, bf16), pltpu.VMEM(piece, bf16)]
+
+    @staticmethod
+    def sems():
+        dma = pltpu.SemaphoreType.DMA
+        return [dma((2,)), dma((2,)), dma, dma]
+
+    @staticmethod
+    def full_scratch():
+        return [pltpu.SemaphoreType.DMA((3,))] * 2
 
 
 def attend_kernel(
@@ -179,23 +324,29 @@
     bias_ref,
     q_all_ref,
     tok_ref,
-    rows_hbm,
+    rows_ref,
     mixed_ref,
     recalled_ref,
     local_ref,
     logs_ref,
     p_ref,
     pair_ref,
-    rows,
-    out_send,
-    out_recv,
-    log_send,
-    log_recv,
-    rows_sem,
-    out_ss,
-    out_rs,
-    log_ss,
-    log_rs,
+    out_xs,
+    out_xr,
+    out_zs,
+    out_zr,
+    log_xs,
+    log_xr,
+    log_zs,
+    log_zr,
+    ox_ss,
+    ox_rs,
+    oz_ss,
+    oz_rs,
+    lx_ss,
+    lx_rs,
+    lz_ss,
+    lz_rs,
     pair_ss,
     pair_rs,
     *,
@@ -205,18 +356,15 @@
     count, span = q_ref.shape[0], pair_ref.shape[1]
     hops = W // count
     per = tok_ref.shape[2]
-
-    def fetch(d, j):
-        return pltpu.make_async_copy(rows_hbm.at[j], rows.at[d], rows_sem.at[d])
-
+    half = parts // 2
     me = lax.axis_index("seq")
-
-    def fetch_start(d, carry):
-        fetch(d, lax.rem(me + d, parts)).start()
-        return carry
-
-    lax.fori_loop(1, parts, fetch_start, 0)
-    fetch(0, me).start()
+    x, z = lax.rem(me, 2), me // 2
+    partner = me + 1 - 2 * x
+
+    def reader(c, dz):
+        at = lax.rem(z + half - dz, half)
+        return 2 * at + (x if c == 0 else 1 - x)
+
     pair_ref[0, W:, :] = k_ref[...]
     pair_ref[1, W:, :] = v_ref[...]
     greet(seq=parts)
@@ -236,38 +384,82 @@
 
     ids = lax.broadcasted_iota(jnp.int32, (count, per), 0)
 
-    def owner_part(d, j, out, logs):
-        fetch(d, j).wait()
-        found = []
+    def owner_part(j):
+        outs, logs = [], []
         for h in range(2):
             cols = head_cols(h)
             keep = tok_ref[j, h : h + 1, :] == ids
-            s = jnp.where(keep, nt(q_all_ref[j, :, cols], rows[d, h, :, 0:128]) * scale, NEG)
+            s = jnp.where(keep, nt(q_all_ref[j, :, cols], rows_ref[j, h, :, 0:128]), NEG)
             top = jnp.max(s, axis=1, keepdims=True)
-            p = jnp.where(keep, jnp.exp(s - top), 0.0)
+            p = jnp.where(keep, jnp.exp((s - top) * scale), 0.0)
             total = jnp.sum(p, axis=1, keepdims=True)
             some = total > 0.0
             safe = jnp.where(some, total, 1.0)
-            out[d, h] = (nn(p.astype(bf16), rows[d, h, :, 128:256]) / safe).astype(bf16)
-            found.append(jnp.where(some, top + jnp.log(safe), NEG))
-        logs[d] = row_form(found, count).T[0:8]
-
-    def send_out(d):
-        peer = lax.rem(me + d, parts)
-        return send(out_send.at[d], out_recv.at[d], out_ss.at[d], out_rs.at[d], "seq", peer)
-
-    def send_log(d):
-        peer = lax.rem(me + d, parts)
-        return send(log_send.at[d], log_recv.at[d], log_ss.at[d], log_rs.at[d], "seq", peer)
-
-    def serve(d, carry):
-        owner_part(d, lax.rem(me + d, parts), out_send, log_send)
-        send_log(d).start()
-        send_out(d).start()
+            outs.append(nn(p.astype(bf16), rows_ref[j, h, :, 128:256]) / safe)
+            logs.append(jnp.where(some, top * scale + jnp.log(safe), NEG))
+        return outs, logs
+
+    def give_x(dz):
+        return (
+            send(log_xs.at[dz], log_xr.at[dz], lx_ss.at[dz], lx_rs.at[dz], "seq", partner),
+            send(out_xs.at[dz], out_xr.at[dz], ox_ss.at[dz], ox_rs.at[dz], "seq", partner),
+        )
+
+    def log_z(dz):
+        return send(
+            log_zs.at[dz], log_zr.at[dz], lz_ss.at[dz], lz_rs.at[dz], "seq", reader(0, dz)
+        )
+
+    def out_z(dz):
+        return send(
+            out_zs.at[dz], out_zr.at[dz], oz_ss.at[dz], oz_rs.at[dz], "seq", reader(0, dz)
+        )
+
+    def neighbour(dz):
+        outs, logs = owner_part(reader(1, dz))
+        for h in range(2):
+            out_xs[dz, h] = outs[h].astype(bf16)
+        log_xs[dz] = row_form(logs, count).T[0:8]
+        for copy in give_x(dz):
+            copy.start()
+
+    def join(outs, logs, dz):
+        for copy in give_x(dz):
+            copy.wait()
+        other = log_xr[dz].T
+        joined = []
+        for h in range(2):
+            theirs = other[:, h : h + 1]
+            top = jnp.maximum(logs[h], theirs)
+            a, b = jnp.exp(logs[h] - top), jnp.exp(theirs - top)
+            total = a + b
+            outs[h] = outs[h] * (a / total) + out_xr[dz, h].astype(f32) * (b / total)
+            joined.append(top + jnp.log(total))
+        return outs, joined
+
+    def neighbour_step(dz, carry):
+        neighbour(dz)
         return carry
 
-    lax.fori_loop(1, parts, serve, 0)
-    owner_part(0, me, out_recv, log_recv)
+    lax.fori_loop(1, half, neighbour_step, 0)
+    neighbour(0)
+
+    def column_step(dz, carry):
+        outs, logs = owner_part(reader(0, dz))
+        outs, logs = join(outs, logs, dz)
+        for h in range(2):
+            out_zs[dz, h] = outs[h].astype(bf16)
+        log_zs[dz] = row_form(logs, count).T[0:8]
+        log_z(dz).start()
+        out_z(dz).start()
+        return carry
+
+    lax.fori_loop(1, half, column_step, 0)
+    outs, logs = owner_part(me)
+    outs, logs = join(outs, logs, 0)
+    log_zr[0] = row_form(logs, count).T[0:8]
+    for h in range(2):
+        recalled_ref[:, head_cols(h)] = outs[h]
 
     for hop in range(1, hops + 1):
         hand_on(hop).wait()
@@ -287,39 +479,29 @@
         p_ref[h] = p
         local_ref[:, cols] = nn(p.astype(bf16), pair_ref[1, :, cols])
 
-    def wait_log(d, carry):
-        send_log(d).wait()
+    def wait_log(dz, top):
+        log_z(dz).wait()
+        return jnp.maximum(top, log_zr[dz])
+
+    top = lax.fori_loop(1, half, wait_log, log_zr[0])
+
+    def add_to(dz, total):
+        return total + jnp.exp(log_zr[dz] - top)
+
+    logs = top + jnp.log(lax.fori_loop(0, half, add_to, jnp.zeros_like(top)))
+    logs_ref[...] = logs
+    share = jnp.exp(log_zr[0] - logs).T
+    for h in range(2):
+        recalled_ref[:, head_cols(h)] *= share[:, h : h + 1]
+
+    def merge(dz, carry):
+        share = jnp.exp(log_zr[dz] - logs).T
+        out_z(dz).wait()
+        for h in range(2):
+            recalled_ref[:, head_cols(h)] += share[:, h : h + 1] * out_zr[dz, h].astype(f32)
         return carry
 
-    lax.fori_loop(1, parts, wait_log, 0)
-
-    def top_of(d, top):
-        return jnp.maximum(top, log_recv[d])
-
-    top = lax.fori_loop(1, parts, top_of, log_recv[0])
-
-    def add_to(d, total):
-        return total + jnp.exp(log_recv[d] - top)
-
-    total = lax.fori_loop(1, parts, add_to, jnp.exp(log_recv[0] - top))
-    logs = top + jnp.log(total)
-    logs_ref[...] = logs
-
-    def merge(d):
-        share = jnp.exp(log_recv[d] - logs).T
-        for h in range(2):
-            cols = head_cols(h)
-            recalled_ref[:, cols] += share[:, h : h + 1] * out_recv[d, h].astype(f32)
-
-    recalled_ref[...] = jnp.zeros_like(recalled_ref)
-    merge(0)
-
-    def merge_next(d, carry):
-        send_out(d).wait()
-        merge(d)
-        return carry
-
-    lax.fori_loop(1, parts, merge_next, 0)
+    lax.fori_loop(1, half, merge, 0)
     for h in range(2):
         cols = head_cols(h)
         gate = gate_ref[h]
@@ -329,7 +511,7 @@
 
 def attend(lengths, gate, q, k, v, bias, q_all, tok, rows):
     parts, count, width = q_all.shape
-    span, hops = W + count, W // count
+    span, hops, half = W + count, W // count, parts // 2
     smem = pl.BlockSpec(memory_space=pltpu.SMEM)
     vmem = pl.BlockSpec(memory_space=pltpu.VMEM)
     dma = pltpu.SemaphoreType.DMA
@@ -343,19 +525,14 @@
             jax.ShapeDtypeStruct((2, count, span), f32),
             jax.ShapeDtypeStruct((2, span, width), bf16),
         ),
-        in_specs=[smem, smem] + [vmem] * 6 + [pl.BlockSpec(memory_space=pl.ANY)],
+        in_specs=[smem, smem] + [vmem] * 7,
         out_specs=(vmem,) * 6,
-        scratch_shapes=[
-            pltpu.VMEM(rows.shape, bf16),
-            pltpu.VMEM((parts, 2, count, 128), bf16),
-            pltpu.VMEM((parts, 2, count, 128), bf16),
-            pltpu.VMEM((parts, 8, count), f32),
-            pltpu.VMEM((parts, 8, count), f32),
-        ]
-        + [dma((parts,))] * 5
+        scratch_shapes=[pltpu.VMEM((half, 2, count, 128), bf16)] * 4
+        + [pltpu.VMEM((half, 8, count), f32)] * 4
+        + [dma((half,))] * 8
         + [dma((hops,))] * 2,
         compiler_params=pltpu.CompilerParams(
-            vmem_limit_bytes=56 * MIB, collective_id=1, has_side_effects=True
+            vmem_limit_bytes=(28 if parts <= 8 else 56) * MIB, collective_id=1, has_side_effects=True
         ),
         cost_estimate=pl.CostEstimate(
             flops=3 * 10**9, bytes_accessed=100 * MIB, transcendentals=5 * 10**6
@@ -478,7 +655,7 @@
     tok_ref,
     up_ref,
     down_ref,
-    rows_hbm,
+    rows_ref,
     branch_ref,
     grad_middle_ref,
     line_ref,
@@ -487,8 +664,9 @@
     gate_out_ref,
     up_out_ref,
     down_out_ref,
-    sum_recv,
-    rows,
+    core_recv,
+    side_send,
+    side_recv,
     g_own,
     g_all,
     st_own,
@@ -512,11 +690,12 @@
     down_d,
     down_e,
     down_sum,
-    sum_ss,
-    sum_rs,
+    core_ss,
+    core_rs,
+    side_ss,
+    side_rs,
     full_ss,
     full_rs,
-    rows_sem,
     g_ss,
     g_rs,
     st_ss,
@@ -543,7 +722,7 @@
     hops = W // count
     per = tok_ref.shape[2]
     half = parts // 2
-    me, head = lax.axis_index("seq"), lax.axis_index("head")
+    me = lax.axis_index("seq")
     x, z = lax.rem(me, 2), me // 2
     partner = me + 1 - 2 * x
 
@@ -551,40 +730,16 @@
         at = lax.rem(z + half - dz, half)
         return 2 * at + (x if c == 0 else 1 - x)
 
-    def fetch(c, dz):
-        return pltpu.make_async_copy(
-            rows_hbm.at[reader(c, dz)], rows.at[c, dz], rows_sem.at[c, dz]
-        )
-
-    def fetch_start(dz, carry):
-        fetch(0, dz).start()
-        fetch(1, dz).start()
-        return carry
-
-    lax.fori_loop(0, half, fetch_start, 0)
     greet(seq=parts, head=peers)
 
-    share = count // peers
-
-    def share_of(peer):
-        return pl.ds(pl.multiple_of(peer * share, share), share)
-
-    def send_sum(d):
-        peer = lax.rem(head + d, peers)
-        return send(
-            sum_ref.at[share_of(peer)], sum_recv.at[d], sum_ss.at[d], sum_rs.at[d], "head", peer
-        )
-
-    mine = share_of(head)
-
-    def send_full(d):
-        peer = lax.rem(head + d, peers)
-        return send(
-            branch_ref.at[mine], branch_ref.at[mine], full_ss.at[d], full_rs.at[d], "head", peer
-        )
-
-    for d in range(1, peers):
-        send_sum(d).start()
+    sums = HeadSum(
+        sum_ref,
+        (core_recv, side_send, side_recv),
+        (core_ss, core_rs, side_ss, side_rs),
+        branch_ref,
+        (full_ss, full_rs),
+    )
+    sums.start()
     scatter = ScatterSum(
         ((up_ref, up_a, up_b, up_c, up_d, up_e), (down_ref, down_a, down_b, down_c, down_d, down_e)),
         (sem_a, sem_b, sem_c, sem_d, sem_e, sem_f),
@@ -595,20 +750,18 @@
     middle = middle_ref[...]
     row_scale = lax.rsqrt(row_mean(middle * middle) + eps)
     hat = middle * row_scale
-    grad_normed = sum_ref[mine, :].astype(f32)
-    for d in range(1, peers):
-        send_sum(d).wait()
-        grad_normed = grad_normed + sum_recv[d].astype(f32)
+    sums.relay()
+    grad_normed = sums.total()
     scaled = grad_normed * gain_ref[...]
-    grad_middle = cot_ref[mine, :].astype(f32) + row_scale * (scaled - hat * row_mean(scaled * hat))
-    branch_ref[mine, :] = grad_middle.astype(bf16)
-    for d in range(1, peers):
-        send_full(d).start()
+    grad_middle = cot_ref[sums.mine, :].astype(f32) + row_scale * (
+        scaled - hat * row_mean(scaled * hat)
+    )
+    sums.spread(grad_middle)
     grad_middle_ref[...] = grad_middle
     line_ref[...] = col_sum(grad_normed * hat)
     scatter.pair(True)
-    for d in range(1, peers):
-        send_full(d).wait()
+    sums.forward()
+    sums.settle()
     g_own[...] = nt(branch_ref[...], weight_ref[...]).astype(bf16)
 
     deltas = []
@@ -684,18 +837,17 @@
     ids = lax.broadcasted_iota(jnp.int32, (count, per), 0)
 
     def owner_part(c, dz, g_at, st_at):
-        fetch(c, dz).wait()
         j = reader(c, dz)
         stats = st_at[...].T
         found = []
         for h in range(2):
             cols = head_cols(h)
             keep = tok_ref[j, h : h + 1, :] == ids
-            s = nt(q_all_ref[j, :, cols], rows[c, dz, h, :, 0:128]) * scale
+            s = nt(q_all_ref[j, :, cols], rows_ref[j, h, :, 0:128]) * scale
             p = jnp.exp(jnp.where(keep, s - stats[:, h : h + 1], NEG))
-            e = nt(g_at[:, cols], rows[c, dz, h, :, 128:256]) * gate_ref[h]
+            e = nt(g_at[:, cols], rows_ref[j, h, :, 128:256]) * gate_ref[h]
             ds = (p * (e - stats[:, 2 + h : 3 + h])).astype(bf16)
-            found.append(nn(ds, rows[c, dz, h, :, 0:128]) * scale)
+            found.append(nn(ds, rows_ref[j, h, :, 0:128]) * scale)
         return found
 
     def give_x(dz):
@@ -793,11 +945,10 @@
             jax.ShapeDtypeStruct((own, up.shape[1]), f32),
             jax.ShapeDtypeStruct((down.shape[1], own), f32),
         ),
-        in_specs=[smem] + [vmem] * 15 + [pl.BlockSpec(memory_space=pl.ANY)],
+        in_specs=[smem] + [vmem] * 16,
         out_specs=(vmem,) * 8,
-        scratch_shapes=[
-            pltpu.VMEM((peers, share, model), bf16),
-            pltpu.VMEM((2, half) + rows.shape[1:], bf16),
+        scratch_shapes=HeadSum.scratch(count, model)
+        + [
             pltpu.VMEM((count, width), bf16),
             pltpu.VMEM((2, half, count, width), bf16),
             pltpu.VMEM((8, count), f32),
@@ -812,13 +963,14 @@
         ]
         + slots
         + [pltpu.VMEM((own, down.shape[1]), f32)]
-        + [dma((peers,))] * 4
-        + [dma((2, half))] * 5
+        + HeadSum.sems()
+        + HeadSum.full_scratch()
+        + [dma((2, half))] * 4
         + [dma((half,))] * 4
         + [dma((hops,))] * 2
         + sems,
         compiler_params=pltpu.CompilerParams(
-            vmem_limit_bytes=(44 if parts <= 8 else 62) * MIB, collective_id=2, has_side_effects=True
+            vmem_limit_bytes=(36 if parts <= 8 else 62) * MIB, collective_id=2, has_side_effects=True
         ),
         cost_estimate=pl.CostEstimate(
             flops=4 * 10**9, bytes_accessed=150 * MIB, transcendentals=5 * 10**6
@@ -827,87 +979,42 @@
     )(gate, sums, cot, gain, middle, weight, q, recalled, local, logs, p, pair, q_all, tok, up, down, rows)
 
 
-def close_kernel(*refs, body, n_sum, n_aux, n_full, n_own, peers):
-    sums = refs[:n_sum]
-    aux = refs[n_sum : n_sum + n_aux]
-    at = n_sum + n_aux
-    full, own = refs[at : at + n_full], refs[at + n_full : at + n_full + n_own]
-    at += n_full + n_own
-    recv = refs[at : at + n_sum]
-    ss, rs, full_ss, full_rs = refs[at + n_sum :]
-    count = sums[0].shape[0]
-    share = count // peers
-    me = lax.axis_index("head")
-    greet(head=peers)
-
-    def rows_of(peer):
-        return pl.ds(pl.multiple_of(peer * share, share), share)
-
-    def send_sum(i, d):
-        peer = lax.rem(me + d, peers)
-        return send(
-            sums[i].at[rows_of(peer)], recv[i].at[d], ss.at[i, d], rs.at[i, d], "head", peer
-        )
-
-    def send_full(i, d):
-        return send(
-            full[i].at[rows_of(me)],
-            full[i].at[rows_of(me)],
-            full_ss.at[i, d],
-            full_rs.at[i, d],
-            "head",
-            lax.rem(me + d, peers),
-        )
-
-    for i in range(n_sum):
-        for d in range(1, peers):
-            send_sum(i, d).start()
-    mine = rows_of(me)
-
-    def total(i):
-        found = sums[i][mine, :].astype(f32)
-        for d in range(1, peers):
-            send_sum(i, d).wait()
-            found = found + recv[i][d].astype(f32)
-        return found
-
-    def spread(i, value):
-        full[i][mine, :] = value.astype(full[i].dtype)
-        for d in range(1, peers):
-            send_full(i, d).start()
-
-    body(mine, total, spread, aux, own)
-    for i in range(n_full):
-        for d in range(1, peers):
-            send_full(i, d).wait()
-
-
-def close(name, collective_id, body, sums, aux, full, own, peers):
-    count, width = sums[0].shape
+def close_attn_kernel(
+    sum_ref, in_ref, gain_ref, full_ref, middle_ref, line_ref, a, b, c, ss_a, rs_a, ss_b, rs_b, ss_f, rs_f
+):
+    greet(head=4)
+    sums = HeadSum(sum_ref, (a, b, c), (ss_a, rs_a, ss_b, rs_b), full_ref, (ss_f, rs_f))
+    sums.start()
+    sums.relay()
+    branch = sums.total()
+    middle = in_ref[sums.mine, :].astype(f32) + branch
+    hat = middle * lax.rsqrt(row_mean(middle * middle) + eps)
+    sums.spread(hat * gain_ref[...])
+    middle_ref[...] = middle
+    line_ref[...] = col_sum(branch * branch)
+    sums.forward()
+    sums.settle()
+
+
+def close_attn(sums, x, gain):
+    count, width = sums.shape
     vmem = pl.BlockSpec(memory_space=pltpu.VMEM)
-    dma = pltpu.SemaphoreType.DMA
     return pl.pallas_call(
-        functools.partial(
-            close_kernel,
-            body=body,
-            n_sum=len(sums),
-            n_aux=len(aux),
-            n_full=len(full),
-            n_own=len(own),
-            peers=peers,
+        close_attn_kernel,
+        out_shape=(
+            jax.ShapeDtypeStruct((count, width), bf16),
+            jax.ShapeDtypeStruct((count // 4, width), f32),
+            jax.ShapeDtypeStruct((1, width), f32),
         ),
-        out_shape=tuple(full) + tuple(own),
-        in_specs=[vmem] * (len(sums) + len(aux)),
-        out_specs=(vmem,) * (len(full) + len(own)),
-        scratch_shapes=[pltpu.VMEM((peers, count // peers, width), bf16) for _ in sums]
-        + [dma((len(sums), peers))] * 2
-        + [dma((len(full), peers))] * 2,
+        in_specs=[vmem] * 3,
+        out_specs=(vmem,) * 3,
+        scratch_shapes=HeadSum.scratch(count, width) + HeadSum.sems() + HeadSum.full_scratch(),
         compiler_params=pltpu.CompilerParams(
-            vmem_limit_bytes=40 * MIB, collective_id=collective_id, has_side_effects=True
+            vmem_limit_bytes=16 * MIB, collective_id=3, has_side_effects=True
         ),
         cost_estimate=pl.CostEstimate(flops=10**6, bytes_accessed=30 * MIB, transcendentals=0),
-        name=name,
-    )(*sums, *aux)
+        name="close_attn",
+    )(sums, x, gain)
 
 
 def row_mean(x):
@@ -916,17 +1023,6 @@
 
 def col_sum(x):
     return jnp.sum(x, axis=0, keepdims=True)
-
-
-def close_attn(mine, total, spread, aux, own):
-    inputs_ref, gain_ref = aux
-    middle_ref, small_ref = own
-    branch = total(0)
-    middle = inputs_ref[mine, :].astype(f32) + branch
-    hat = middle * lax.rsqrt(row_mean(middle * middle) + eps)
-    spread(0, hat * gain_ref[...])
-    middle_ref[...] = middle
-    small_ref[...] = col_sum(branch * branch)
 
 
 def folded(line):
@@ -954,8 +1050,12 @@
     out_a,
     out_b,
     small_ref,
-    back_recv,
-    feed_recv,
+    back_a,
+    back_b,
+    back_c,
+    feed_a,
+    feed_b,
+    feed_c,
     in_a,
     in_b,
     in_c,
@@ -969,10 +1069,18 @@
     small_head,
     small_seq,
     small_send,
-    sum_ss,
-    sum_rs,
-    full_ss,
-    full_rs,
+    bs_a,
+    bs_b,
+    bs_c,
+    bs_d,
+    fs_a,
+    fs_b,
+    fs_c,
+    fs_d,
+    bf_ss,
+    bf_rs,
+    ff_ss,
+    ff_rs,
     sh_ss,
     sh_rs,
     sq_ss,
@@ -988,24 +1096,16 @@
     peers,
 ):
     count = back_ref.shape[0]
-    share = count // peers
     me, head = lax.axis_index("seq"), lax.axis_index("head")
     greet(seq=parts, head=peers)
-
-    def share_of(peer):
-        return pl.ds(pl.multiple_of(peer * share, share), share)
-
-    def send_sum(i, d):
-        peer = lax.rem(head + d, peers)
-        src, recv = ((back_ref, back_recv), (feed_ref, feed_recv))[i]
-        return send(
-            src.at[share_of(peer)], recv.at[d], sum_ss.at[i, d], sum_rs.at[i, d], "head", peer
-        )
-
-    for i in range(2):
-        for d in range(1, peers):
-            send_sum(i, d).start()
-
+    backs = HeadSum(
+        back_ref, (back_a, back_b, back_c), (bs_a, bs_b, bs_c, bs_d), input_grad_ref, (bf_ss, bf_rs)
+    )
+    feeds = HeadSum(
+        feed_ref, (feed_a, feed_b, feed_c), (fs_a, fs_b, fs_c, fs_d), layer_ref, (ff_ss, ff_rs)
+    )
+    backs.start()
+    feeds.start()
     scatter = ScatterSum(
         ((grad_a, in_a, in_b, in_c, in_d, in_e), (grad_b, res_a, res_b, res_c, res_d, res_e)),
         (sem_a, sem_b, sem_c, sem_d, sem_e, sem_f),
@@ -1015,44 +1115,20 @@
         for side in range(2):
             scatter.start(far, side)
 
-    mine = share_of(head)
-
-    def total(i):
-        src, recv = ((back_ref, back_recv), (feed_ref, feed_recv))[i]
-        found = src[mine, :].astype(f32)
-        for d in range(1, peers):
-            send_sum(i, d).wait()
-            found = found + recv[d].astype(f32)
-        return found
-
-    def send_full(i, d):
-        full = (input_grad_ref, layer_ref)[i]
-        return send(
-            full.at[mine],
-            full.at[mine],
-            full_ss.at[i, d],
-            full_rs.at[i, d],
-            "head",
-            lax.rem(head + d, peers),
-        )
-
-    tokens = in_ref[mine, :].astype(f32)
+    backs.relay()
+    feeds.relay()
+    tokens = in_ref[backs.mine, :].astype(f32)
     scale = lax.rsqrt(row_mean(tokens * tokens) + eps)
     hat = tokens * scale
-    grad_normed = total(0)
+    grad_normed = backs.total()
     g = grad_normed * gain_ref[...]
-    back = grad_middle_ref[...] + scale * (g - hat * row_mean(g * hat))
-    input_grad_ref[mine, :] = back.astype(bf16)
-    for d in range(1, peers):
-        send_full(0, d).start()
+    backs.spread(grad_middle_ref[...] + scale * (g - hat * row_mean(g * hat)))
+    branch = feeds.total()
+    layer = middle_ref[...] + branch
+    feeds.spread(layer)
     scatter.pair(True)
     small_send[0:8] = folded(col_sum(grad_normed * hat))
     small_send[8:16] = folded(gain_line_ref[...])
-    branch = total(1)
-    layer = middle_ref[...] + branch
-    layer_ref[mine, :] = layer.astype(bf16)
-    for d in range(1, peers):
-        send_full(1, d).start()
     small_send[16:24] = extra_ref[...]
     small_send[16:17] = fold_sum(col_sum(layer * layer))
     small_send[17:18] = fold_sum(attn_line_ref[...])
@@ -1066,6 +1142,8 @@
         send_head(d).start()
 
     scatter.far()
+    backs.forward()
+    feeds.forward()
 
     kept = lax.broadcasted_iota(jnp.int32, (24, 128), 0) < 19
     found = small_send[...]
@@ -1094,14 +1172,13 @@
         return carry
 
     lax.fori_loop(1, parts, add_seq, 0)
-    for i in range(2):
-        for d in range(1, peers):
-            send_full(i, d).wait()
+    backs.settle()
+    feeds.settle()
 
 
 def finish(back, feed, x, gain, grad_middle, middle, gain_line, attn_line, extra, grad_a, grad_b, parts, peers):
     count, width = back.shape
-    share, own = count // peers, grad_a.shape[0] // parts
+    own = grad_a.shape[0] // parts
     slots, sems = ScatterSum.scratch((grad_a, grad_b), parts)
     wide_a, wide_b = grad_a.shape[1], grad_b.shape[1]
     vmem = pl.BlockSpec(memory_space=pltpu.VMEM)
@@ -1117,14 +1194,15 @@
         ),
         in_specs=[vmem] * 11,
         out_specs=(vmem,) * 5,
-        scratch_shapes=[pltpu.VMEM((peers, share, width), bf16)] * 2
+        scratch_shapes=HeadSum.scratch(count, width) * 2
         + slots
         + [
             pltpu.VMEM((peers, 24, 128), f32),
             pltpu.VMEM((parts, 24, 128), f32),
             pltpu.VMEM((24, 128), f32),
         ]
-        + [dma((2, peers))] * 4
+        + HeadSum.sems() * 2
+        + HeadSum.full_scratch() * 2
         + [dma((peers,))] * 2
         + [dma((parts,))] * 2
         + sems,
@@ -1139,10 +1217,6 @@
 def norm_stats(values):
     row_scale = lax.rsqrt(jnp.mean(values * values, axis=-1, keepdims=True) + eps)
     return (values * row_scale, row_scale)
-
-
-def exchange(value):
-    return lax.all_to_all(value, "seq", split_axis=0, concat_axis=0, tiled=True)
 
 
 def per_device(
@@ -1171,11 +1245,8 @@
     token = jnp.arange(block_len, dtype=jnp.int32)[None, :, None]
     codes = (wanted // slot_count) * (block_len * slot_count) + token * slot_count + wanted % slot_count
     codes = lax.sort(codes.reshape(2, -1), dimension=1, is_stable=False)
-    codes = jnp.transpose(codes.reshape(2, seq_count, -1), (1, 0, 2))
-    codes = exchange(codes)
-    slots = codes % slot_count
-    tok = (codes // slot_count) % block_len
-    rows = gather_rows(slots, memory_table)
+    places, tok = request(codes, seq_count, slot_count, block_len)
+    rows = gather_rows(places, widen(memory_table))
 
     hot, outside = diagonal_buckets(block_len, bucket_total)
     bias_row = jnp.dot(position_bias, hot, precision=highest) + outside[None]
@@ -1195,23 +1266,7 @@
         lengths[0], gate_flat, queries, keys, values, bias_row, q_all, tok, rows
     )
 
-    def whole(dtype):
-        return jax.ShapeDtypeStruct((block_len, model_width), dtype)
-
-    def lines(count):
-        return jax.ShapeDtypeStruct((count, model_width), f32)
-
-    chunk = lines(block_len // peers)
-    normed_two, middle, attn_line = close(
-        "close_attn",
-        3,
-        close_attn,
-        [nn(mixed, output_weight).astype(bf16)],
-        [x, gain_two],
-        [whole(bf16)],
-        [chunk, lines(1)],
-        peers,
-    )
+    normed_two, middle, attn_line = close_attn(nn(mixed, output_weight).astype(bf16), x, gain_two)
     upward = nn(normed_two, up_weight)
     gelu_value, gelu_back = jax.vjp(jax.nn.gelu, upward)
     hidden = gelu_value.astype(bf16)

time: 312 us -> 278 us (0.89)
  Pallas kernels: 218 us -> 205 us
  starting transfers between devices: 7.3 us -> 0.04 us
  waiting for transfers between devices: 6.39 us -> 0.02 us
  matrix products: 23.3 us -> 18.2 us
    unnamed x103 -> x82, local copies, waits for them, and re-layouts: 16.7 us -> 29 us
    sort x2, local copies, waits for them, and re-layouts: 11.5 us -> 0.06 us  [per_device(): codes = lax.sort(codes.reshape(2, -1), dimension=1, is_stable=False)]
    all_to_all x1 -> x0, starting transfers between devices: 7.25 us -> none  [exchange(): return lax.all_to_all(value, 'seq', split_axis=0, concat_axis=0, tiled=True)]
    pallas_call x1, Pallas kernels: 40.1 us -> 33.2 us  [finish(): pl.pallas_call(functools.partial(finish_kernel, parts=parts, peers=peers)...]
    all_to_all x1 -> x0, waiting for transfers between devices: 6.37 us -> none  [exchange(): return lax.all_to_all(value, 'seq', split_axis=0, concat_axis=0, tiled=True)]
    pallas_call x1, Pallas kernels: 35.3 us -> 29 us  [attend(): pl.pallas_call(functools.partial(attend_kernel, parts=parts, scale=128 **...]
    pallas_call x1, Pallas kernels: 93.7 us -> 90.1 us  [attend_back(): pl.pallas_call(functools.partial(attend_back_kernel, parts=parts, peers=p...]
    pallas_call x2 -> x4, Pallas kernels: 49.2 us -> 52.7 us  [the longest x1 24 us: gather_rows(): pl.pallas_call(functools.partial(gather_kernel, unroll=unroll, group=unro...]
  transfers between devices with their start and end apart: 2 -> 1, of which waited for: 1 -> 0; matrix products, arithmetic and copies ran while one was open for 2% -> 1% of each run, Pallas kernels for 11% -> 14%
where the time goes in v3:
time: 278 us; the launch traced here: 277 us
  Pallas kernels  205 us (74%)
  local copies, waits for them, and re-layouts  33.1 us (12%)
  matrix products  18.2 us (7%)
  between operations  16 us (6%)
  other arithmetic  4.65 us (2%)
    pallas_call x1, Pallas kernels, attend_back(): pl.pallas_call(functools.partial(attend_back_kernel, parts=parts, peers=p...  90.1 us
    pallas_call x1, Pallas kernels, finish(): pl.pallas_call(functools.partial(finish_kernel, parts=parts, peers=peers)...  33.2 us
    pallas_call x1, Pallas kernels, attend(): pl.pallas_call(functools.partial(attend_kernel, parts=parts, scale=128 **...  29 us
    unnamed x82, local copies, waits for them, and re-layouts  29 us
    pallas_call x1, Pallas kernels, gather_rows(): pl.pallas_call(functools.partial(gather_kernel, unroll=unroll, group=unro...  24 us
    pallas_call x1, Pallas kernels, close_attn(): pl.pallas_call(close_attn_kernel, out_shape=(jax.ShapeDtypeStruct((count,...  13.3 us
    pallas_call x1, Pallas kernels, request(): pl.pallas_call(functools.partial(request_kernel, parts=parts, slots=slots...  8.7 us
    dot_general x6, matrix products, nn(): lax.dot_general(a, b, (((1,), (0,)), ((), ())), preferred_element_type=f32)  7.66 us
  transfers between devices with their start and end apart: 1, of which 0 were waited for; matrix products, arithmetic and copies ran while one was open for 1% of the time, Pallas kernels for 14%

profile of v3, /device:TPU:0, one launch (start us, length us, event | category | flops | bytes accessed | tf_op | source)
XLA Modules:
  0.0 277.0 jit_solution(12275146768572749627)
XLA Ops:
  8.1 1.0 fusion.18
  10.1 1.2 fusion.2
  11.4 2.2 convolution_convert_fusion.8.q_ref
  13.7 3.4 %copy-done.4 = bf16[8192,2,256]{2,1,0:T(2,128)(2,1)S(1)} copy-done((bf16[8192,2,256]{2,1,0:T(2,128)(2,1)S(1)}, bf16[8192,2,256]{2,1,0:T(2,128)(2,1)}, u32[]{:S(2)}) %copy-start.4) | copy-done | bytes 8388632
  17.1 6.6 %widen.1.wide_ref = f32[32768,128]{1,0:T(8,128)S(1)} custom-call(bf16[8192,2,256]{2,1,0:T(2,128)(2,1)S(1)} %copy-done.4), custom_call_target="tpu_custom_call" | custom-call | bytes 41943040 | tf_op jit(solution)/shard_map/widen/pallas_call | solution.py:86
  23.7 5.7 %copy-done.1 = f32[32768,128]{1,0:T(8,128)} copy-done((f32[32768,128]{1,0:T(8,128)}, f32[32768,128]{1,0:T(8,128)S(1)}, u32[]{:S(2)}) %copy-start.1) | copy-done | bytes 16777240
  29.7 1.4 convolution_convert_fusion.6.v_ref
  31.1 1.4 convolution_convert_fusion.7.k_ref
  32.6 0.8 copy-done.23
  33.4 8.7 %request.1 = (s32[8,2,1024]{2,1,0:T(2,128)S(1)}, s32[8,2,1024]{2,1,0:T(2,128)S(1)}) custom-call(s32[2,8192]{1,0:T(2,128)S(1)} %copy-done.23), custom_call_target="tpu_custom_call" | custom-call | tf_op jit(solution)/shard_map/request/pallas_call | solution.py:231
  42.1 24.0 %gather_rows.1 = bf16[16,1024,256]{2,1,0:T(8,128)(2,1)S(1)} custom-call(s32[16384]{0:T(1024)S(1)} %bitcast.91, f32[32768,128]{1,0:T(8,128)} %copy-done.1), custom_call_target="tpu_custom_call" | custom-call | bytes 104857600 | tf_op jit(solution)/shard_map/gather_rows/pallas_call | solution.py:124
  66.2 3.3 %copy-done.2 = bf16[16,1024,256]{2,1,0:T(8,128)(2,1)} copy-done((bf16[16,1024,256]{2,1,0:T(8,128)(2,1)}, bf16[16,1024,256]{2,1,0:T(8,128)(2,1)S(1)}, u32[]{:S(2)}) %copy-start.2) | copy-done | bytes 8388632
  69.4 3.4 %copy-done.3 = bf16[16,1024,256]{2,1,0:T(8,128)(2,1)S(1)} copy-done((bf16[16,1024,256]{2,1,0:T(8,128)(2,1)S(1)}, bf16[16,1024,256]{2,1,0:T(8,128)(2,1)}, u32[]{:S(2)}) %copy-start.3) | copy-done | bytes 8388632
  72.8 1.2 copy-done.11
  74.0 29.0 %attend.1 = (bf16[256,256]{1,0:T(8,128)(2,1)S(1)}, f32[256,256]{1,0:T(8,128)S(1)}, f32[256,256]{1,0:T(8,128)S(1)}, f32[8,256]{1,0:T(8,128)S(1)}, f32[2,256,768]{...) custom-call(s32[4]{0:T(128)S(1)} %bitcast.97, f32[2]{0:T(128)S(1)} %add_divide_fusion.gate_ref, ...), custom_call_target="tpu_custom_call" | custom-call | flops 3000000000 | bytes 104857600 | tf_op jit(solution)/shard_map/attend/pallas_call | solution.py:518
  103.4 13.3 %close_attn.1 = (bf16[256,1024]{1,0:T(8,128)(2,1)S(1)}, f32[64,1024]{1,0:T(8,128)S(1)}, f32[1,1024]{1,0:T(1,128)S(1)}) custom-call(bf16[256,1024]{1,0:T(8,128)(2,1)S(1)} %convolution_convert_fusion.3.sum_ref, bf16[256,1024]{1,0:T(8,128)(2,1)S(1)} %bitcast.85, f32[1,1024]{1,0:T(1,128)S(1)} %bitcast.95), custom_call_target="tpu_custom_call" | custom-call | flops 1000000 | bytes 31457280 | tf_op jit(solution)/shard_map/close_attn/pallas_call | solution.py:1002
  118.6 1.3 fusion.11
  121.3 0.9 convert_bitcast_fusion.down_ref
  122.6 90.1 %attend_back.1 = (bf16[256,1024]{1,0:T(8,128)(2,1)S(1)}, f32[64,1024]{1,0:T(8,128)S(1)}, f32[1,1024]{1,0:T(1,128)S(1)}, bf16[256,768]{1,0:T(8,128)(2,1)S(1)}, f3...) custom-call(f32[2]{0:T(128)S(1)} %add_divide_fusion.gate_ref, ...), custom_call_target="tpu_custom_call" | custom-call | flops 4000000000 | bytes 157286400 | tf_op jit(solution)/shard_map/attend_back/pallas_call | solution.py:936
  212.7 1.4 fusion.14
  214.1 1.9 convolution_convert_fusion.1.grad_a
  216.0 1.6 convolution_convert_fusion.4.feed_ref
  217.7 1.2 convolution_convert_fusion.2.grad_b
  219.8 1.7 convolution_add_fusion.1
  222.7 1.4 copy-done.6
  224.1 1.0 copy-done.8
  225.1 0.9 copy-done.10
  226.1 1.0 copy-done.20
  227.1 0.9 copy-done.22
  228.1 33.2 %finish.1 = (bf16[256,1024]{1,0:T(8,128)(2,1)S(1)}, bf16[256,1024]{1,0:T(8,128)(2,1)S(1)}, f32[128,768]{1,0:T(8,128)S(1)}, f32[128,256]{1,0:T(8,128)S(1)}, f32[24,128]{1,0:T(8,128)S(1)}) custom-call(bf16[256,1024]{1,0:T(8,128)(2,1)S(1)} %fusion.back_ref, bf16[256,1024]{1,0:T(8,128)(2,1)S(1)} %copy-done.20, bf16[256,1024]{1,0:T(8,128)(2,1)S(1)} %bitcast.86, ...), custom_call_target="tpu_custom_call" | custom-call | flops 10000000 | bytes 104857600 | tf_op jit(solution)/shard_map/finish/pallas_call | solution.py:1186
  262.5 1.1 bitcast_convert_fusion
  266.1 1.9 copy.42
  (100 shorter events, 12.7 us)
Async XLA Ops:
  8.0 108.7 %copy-start = (bf16[1024,1024]{1,0:T(8,128)(2,1)S(1)}, bf16[1024,1024]{1,0:T(8,128)(2,1)}, u32[]{:S(2)}) copy-start(bf16[1024,1024]{1,0:T(8,128)(2,1)} %param.28) | copy-start | bytes 6291460
  8.0 24.5 %sort.9.cloned.1.call-start = ((), (), s32[]{:S(2)}) async-start(), calls=%async_computation.1 | async-start | bytes 196640 | tf_op jit(solution)/shard_map/sort | solution.py:1247
  10.1 59.3 %all-gather.3.cloned.1.call-start = ((), (), s32[]{:S(2)}) async-start(), calls=%async_computation | async-start | bytes 1179648 | tf_op jit(solution)/shard_map/all_gather | solution.py:1263
  11.4 19.7 %copy-start.31 = (f32[256]{0:T(256)}, f32[256]{0:T(256)S(1)}, u32[]{:S(2)}) copy-start(f32[256]{0:T(256)S(1)} %add_rsqrt_fusion) | copy-start | bytes 3076
  13.6 3.4 %copy-start.4 = (bf16[8192,2,256]{2,1,0:T(2,128)(2,1)S(1)}, bf16[8192,2,256]{2,1,0:T(2,128)(2,1)}, u32[]{:S(2)}) copy-start(bf16[8192,2,256]{2,1,0:T(2,128)(2,1)} %table_hbm.1) | copy-start | bytes 25165828
  17.0 12.4 %copy-start.36 = (f32[2]{0:T(128)S(1)}, f32[2]{0:T(128)}, u32[]{:S(2)}) copy-start(f32[2]{0:T(128)} %param.33) | copy-start | bytes 28
  17.0 12.4 %copy-start.30 = (f32[32,768]{1,0:T(8,128)S(1)}, f32[32,768]{1,0:T(8,128)}, u32[]{:S(2)}) copy-start(f32[32,768]{1,0:T(8,128)} %constant.127.clone) | copy-start | bytes 294916
  17.0 12.4 %copy-start.33 = (f32[768]{0:T(1024)S(1)}, f32[768]{0:T(1024)}, u32[]{:S(2)}) copy-start(f32[768]{0:T(1024)} %constant.136) | copy-start | bytes 9220
  17.0 12.4 %copy-start.34 = (f32[2,32]{1,0:T(2,128)S(1)}, f32[2,32]{1,0:T(2,128)}, u32[]{:S(2)}) copy-start(f32[2,32]{1,0:T(2,128)} %param.32) | copy-start | bytes 772
  17.0 12.6 %copy-start.5 = (bf16[1,256,1024]{2,1,0:T(8,128)(2,1)S(1)}, bf16[1,256,1024]{2,1,0:T(8,128)(2,1)}, u32[]{:S(2)}) copy-start(bf16[1,256,1024]{2,1,0:T(8,128)(2,1)} %param.22) | copy-start | bytes 1572868
  17.1 12.6 %copy-start.24 = (f32[1024]{0:T(1024)S(1)}, f32[1024]{0:T(1024)}, u32[]{:S(2)}) copy-start(f32[1024]{0:T(1024)} %param.30) | copy-start | bytes 12292
  23.7 5.7 %copy-start.1 = (f32[32768,128]{1,0:T(8,128)}, f32[32768,128]{1,0:T(8,128)S(1)}, u32[]{:S(2)}) copy-start(f32[32768,128]{1,0:T(8,128)S(1)} %widen.1.wide_ref) | copy-start | bytes 50331652
  42.1 27.3 %copy-start.13 = (bf16[256,256]{1,0:T(8,128)(2,1)S(1)}, bf16[256,256]{1,0:T(8,128)(2,1)}, u32[]{:S(2)}) copy-start(bf16[256,256]{1,0:T(8,128)(2,1)} %convolution_convert_fusion.8.q_ref) | copy-start | bytes 393220
  42.1 27.3 %copy-start.26 = (s32[1,4]{1,0:T(1,128)S(1)}, s32[1,4]{1,0:T(1,128)}, u32[]{:S(2)}) copy-start(s32[1,4]{1,0:T(1,128)} %param.36) | copy-start | bytes 52
  66.1 3.3 %copy-start.2 = (bf16[16,1024,256]{2,1,0:T(8,128)(2,1)}, bf16[16,1024,256]{2,1,0:T(8,128)(2,1)S(1)}, u32[]{:S(2)}) copy-start(bf16[16,1024,256]{2,1,0:T(8,128)(2,1)S(1)} %gather_rows.1) | copy-start | bytes 25165828
  69.4 3.4 %copy-start.3 = (bf16[16,1024,256]{2,1,0:T(8,128)(2,1)S(1)}, bf16[16,1024,256]{2,1,0:T(8,128)(2,1)}, u32[]{:S(2)}) copy-start(bf16[16,1024,256]{2,1,0:T(8,128)(2,1)} %copy-done.2) | copy-start | bytes 25165828
  74.0 29.0 %copy-start.7 = (bf16[256,1024]{1,0:T(8,128)(2,1)S(1)}, bf16[256,1024]{1,0:T(8,128)(2,1)}, u32[]{:S(2)}) copy-start(bf16[256,1024]{1,0:T(8,128)(2,1)} %weight_ref.1) | copy-start | bytes 1572868
  74.0 29.3 %copy-start.25 = (f32[1024]{0:T(1024)S(1)}, f32[1024]{0:T(1024)}, u32[]{:S(2)}) copy-start(f32[1024]{0:T(1024)} %param.31) | copy-start | bytes 12292
  116.7 5.5 %copy-start.9 = (f32[64,1024]{1,0:T(8,128)}, f32[64,1024]{1,0:T(8,128)S(1)}, u32[]{:S(2)}) copy-start(f32[64,1024]{1,0:T(8,128)S(1)} %get-tuple-element.65.middle_ref) | copy-start | bytes 786436
  116.7 1.8 copy-start.35
  122.6 90.2 %copy-start.28 = (bf16[1024,256]{1,0:T(8,128)(2,1)S(1)}, bf16[1024,256]{1,0:T(8,128)(2,1)}, u32[]{:S(2)}) copy-start(bf16[1024,256]{1,0:T(8,128)(2,1)} %param.24) | copy-start | bytes 1572868
  122.6 91.5 %copy-start.32 = (f32[256]{0:T(256)S(1)}, f32[256]{0:T(256)}, u32[]{:S(2)}) copy-start(f32[256]{0:T(256)} %copy-done.31) | copy-start | bytes 3076
  212.7 3.3 %copy-start.15 = (f32[1024,128]{1,0:T(8,128)}, f32[1024,128]{1,0:T(8,128)S(1)}, u32[]{:S(2)}) copy-start(f32[1024,128]{1,0:T(8,128)S(1)} %get-tuple-element.136) | copy-start | bytes 1572868
  212.7 3.3 %copy-start.17 = (f32[128,1024]{1,0:T(8,128)}, f32[128,1024]{1,0:T(8,128)S(1)}, u32[]{:S(2)}) copy-start(f32[128,1024]{1,0:T(8,128)S(1)} %get-tuple-element.135) | copy-start | bytes 1572868
  212.7 3.3 %copy-start.21 = (f32[64,1024]{1,0:T(8,128)}, f32[64,1024]{1,0:T(8,128)S(1)}, u32[]{:S(2)}) copy-start(f32[64,1024]{1,0:T(8,128)S(1)} %get-tuple-element.72.grad_middle_ref) | copy-start | bytes 786436
  216.0 2.8 %copy-start.29 = (f32[768,32]{1,0:T(8,128)S(1)}, f32[768,32]{1,0:T(8,128)}, u32[]{:S(2)}) copy-start(f32[768,32]{1,0:T(8,128)} %constant.129.clone) | copy-start | bytes 294916
  216.0 3.2 %copy-start.37 = (f32[2]{0:T(128)S(1)}, f32[2]{0:T(128)}, u32[]{:S(2)}) copy-start(f32[2]{0:T(128)} %param.33) | copy-start | bytes 28
  219.3 2.3 copy-start.27
  222.7 1.4 copy-start.6
  261.2 2.3 copy-start.19
  261.3 6.7 %copy-start.18 = (f32[128,1024]{1,0:T(8,128)S(1)}, f32[128,1024]{1,0:T(8,128)}, u32[]{:S(2)}) copy-start(f32[128,1024]{1,0:T(8,128)} %copy-done.17) | copy-start | bytes 1572868
  262.5 6.3 %copy-start.16 = (f32[1024,128]{1,0:T(8,128)S(1)}, f32[1024,128]{1,0:T(8,128)}, u32[]{:S(2)}) copy-start(f32[1024,128]{1,0:T(8,128)} %copy-done.15) | copy-start | bytes 1572868
  (8 other events, 8.4 us)
Sparse Core Ops, SparseCore 0:
  11.9 16.9 sort.11.cloned.1.call-done
  (1 shorter events, 0.0 us)
Sparse Core Ops, SparseCore 1:
  13.7 43.1 all-gather.2

commit v4 on v3

v4 whole, which is shorter than its diff:
```python
import functools
import math
import types

import jax
import jax.numpy as jnp
import numpy as np
from jax import lax
from jax.experimental import pallas as pl
from jax.experimental.pallas import tpu as pltpu
from jax.sharding import PartitionSpec as P

W = 512
eps = 1e-06
exact_span = 16
far_distance = 128
highest = lax.Precision.HIGHEST
f32 = jnp.float32
bf16 = jnp.bfloat16
NEG = -1e30
MIB = 2**20


def bucket_table(key_span, bucket_total):
    found = []
    for distance in range(key_span):
        if distance < exact_span:
            found.append(distance)
        else:
            scaled = math.log(distance / exact_span) / math.log(far_distance / exact_span)
            found.append(
                min(bucket_total - 1, exact_span + math.floor(scaled * (bucket_total - exact_span)))
            )
    return np.asarray(found)


def diagonal_buckets(block_len, bucket_total):
    span = W + block_len
    table = bucket_table(W, bucket_total)
    hot = np.zeros((bucket_total, span), np.float32)
    for u in range(1, W + 1):
        hot[table[W - u], u] = 1.0
    outside = np.where(hot.sum(0) > 0, 0.0, NEG).astype(np.float32)
    return hot, outside


def nt(a, b):
    return lax.dot_general(a, b, (((1,), (1,)), ((), ())), preferred_element_type=f32)


def nn(a, b):
    return lax.dot_general(a, b, (((1,), (0,)), ((), ())), preferred_element_type=f32)


def tn(a, b):
    return lax.dot_general(a, b, (((0,), (0,)), ((), ())), preferred_element_type=f32)


def widen_kernel(table_hbm, wide_hbm, buf, out, sem, out_sem, *, chunk, part):
    chunks = table_hbm.shape[0] // chunk

    def fetch(i):
        return pltpu.make_async_copy(
            table_hbm.at[pl.ds(i * chunk, chunk)], buf.at[i % 2], sem.at[i % 2]
        )

    def store(i):
        return pltpu.make_async_copy(
            out.at[i % 2], wide_hbm.at[:, pl.ds(2 * i * chunk, 2 * chunk)], out_sem.at[i % 2]
        )

    fetch(0).start()
    for i in range(chunks):
        fetch(i).wait()
        if i + 1 < chunks:
            fetch(i + 1).start()
        if i > 1:
            store(i - 2).wait()

        def widen(q, carry, i=i):
            x = buf[i % 2, pl.ds(q * part, part)].astype(f32)
            for r in range(part):
                for h in range(2):
                    place = pl.ds(2 * (q * part + r), 1)
                    out[i % 2, h, place, :] = x[r, h : h + 1, 0:128]
                    place = pl.ds(2 * (q * part + r) + 1, 1)
                    out[i % 2, h, place, :] = x[r, h : h + 1, 128:256]
            return carry

        lax.fori_loop(0, chunk // part, widen, 0)
        store(i).start()
    for i in range(max(0, chunks - 2), chunks):
        store(i).wait()


def widen(table):
    total = table.shape[0]
    chunk = min(1024, total)
    hbm = pl.BlockSpec(memory_space=pltpu.HBM)
    dma = pltpu.SemaphoreType.DMA
    return pl.pallas_call(
        functools.partial(widen_kernel, chunk=chunk, part=32),
        out_shape=jax.ShapeDtypeStruct((2, 2 * total, 128), f32),
        in_specs=[hbm],
        out_specs=hbm,
        scratch_shapes=[
            pltpu.VMEM((2, chunk, 2, 256), bf16),
            pltpu.VMEM((2, 2, 2 * chunk, 128), f32),
            dma((2,)),
            dma((2,)),
        ],
        compiler_params=pltpu.CompilerParams(vmem_limit_bytes=58 * MIB),
        cost_estimate=pl.CostEstimate(flops=0, bytes_accessed=40 * MIB, transcendentals=0),
        name="widen",
    )(table)


def gather_kernel(at_ref, wide_hbm, out_hbm, wide, buf, low, wide_sem, out_sem, *, unroll, group):
    parts, rows = out_hbm.shape[0], out_hbm.shape[2]

    def fetch(h):
        return pltpu.make_async_copy(wide_hbm.at[h], wide.at[h], wide_sem.at[h])

    def store(j, h, slot):
        return pltpu.make_async_copy(low.at[slot], out_hbm.at[j, h], out_sem.at[slot])

    for h in range(2):
        fetch(h).start()
    for h in range(2):
        fetch(h).wait()

        def one(j, carry, h=h):
            slot = lax.rem(j, 2)
            first = (2 * j + h) * rows

            def copy_rows(q, carry):
                base = q * unroll
                for g in range(0, unroll, group):
                    found = [
                        wide[h, pl.ds(at_ref[first + base + g + u], 2), :] for u in range(group)
                    ]
                    for u in range(group):
                        buf[pl.ds(2 * (base + g + u), 2), :] = found[u]
                return carry

            lax.fori_loop(0, rows // unroll, copy_rows, 0)

            if h == 0:

                @pl.when(j > 1)
                def _():
                    store(j, h, slot).wait()

            else:
                store(j, h, slot).wait()

            low[slot, :, 0:128] = buf[pl.ds(0, rows, 2), :].astype(bf16)
            low[slot, :, 128:256] = buf[pl.ds(1, rows, 2), :].astype(bf16)
            store(j, h, slot).start()
            return carry

        lax.fori_loop(0, parts, one, 0)
    store(0, 1, 0).wait()
    store(1, 1, 1).wait()


def gather_rows(places, wide):
    parts, heads, rows = places.shape
    unroll = min(64, rows)
    hbm = pl.BlockSpec(memory_space=pltpu.HBM)
    dma = pltpu.SemaphoreType.DMA
    return pl.pallas_call(
        functools.partial(gather_kernel, unroll=unroll, group=unroll // 2),
        out_shape=jax.ShapeDtypeStruct((parts, heads, rows, 256), bf16),
        in_specs=[pl.BlockSpec(memory_space=pltpu.SMEM), hbm],
        out_specs=hbm,
        scratch_shapes=[
            pltpu.VMEM(wide.shape, f32),
            pltpu.VMEM((2 * rows, 128), f32),
            pltpu.VMEM((2, rows, 256), bf16),
            dma((2,)),
            dma((2,)),
        ],
        compiler_params=pltpu.CompilerParams(vmem_limit_bytes=58 * MIB),
        cost_estimate=pl.CostEstimate(flops=0, bytes_accessed=100 * MIB, transcendentals=0),
        name="gather_rows",
    )(places.reshape(-1), wide)


MESH = pl.DeviceIdType.MESH


def greet(**counts):
    barrier = pltpu.get_barrier_semaphore()
    for axis, count in counts.items():
        me = lax.axis_index(axis)

        def call(d, carry, axis=axis, count=count, me=me):
            peer = lax.rem(me + d, count)
            pl.semaphore_signal(barrier, inc=1, device_id={axis: peer}, device_id_type=MESH)
            return carry

        lax.fori_loop(1, count, call, 0)
    pl.semaphore_wait(barrier, sum(counts.values()) - len(counts))


def send(src, dst, send_sem, recv_sem, axis, peer):
    return pltpu.make_async_remote_copy(
        src_ref=src,
        dst_ref=dst,
        send_sem=send_sem,
        recv_sem=recv_sem,
        device_id={axis: peer},
        device_id_type=MESH,
    )


def doc_starts(lengths_ref, first, count):
    place = first + lax.broadcasted_iota(jnp.int32, (count, 1), 0)
    start = jnp.zeros((count, 1), jnp.int32)
    end = jnp.int32(0)
    for c in range(lengths_ref.shape[0]):
        end = end + lengths_ref[c]
        start = jnp.where(end <= place, end, start)
    return start


def head_cols(h):
    return slice(h * 128, h * 128 + 128)


def row_form(columns, count):
    lane = lax.broadcasted_iota(jnp.int32, (count, 128), 1)
    wide = jnp.zeros((count, 128), f32)
    for i, column in enumerate(columns):
        wide = jnp.where(lane == i, column, wide)
    return wide


def request_kernel(codes_ref, place_ref, tok_ref, got, own_sem, ss, rs, *, parts, slots, tokens):
    rows = codes_ref.shape[1] // parts
    me = lax.axis_index("seq")

    def part(owner):
        return codes_ref.at[:, pl.ds(pl.multiple_of(owner * rows, 128), rows)]

    keep = pltpu.make_async_copy(part(me), got.at[0], own_sem)
    keep.start()
    greet(seq=parts)

    def ask(d):
        peer = lax.rem(me + d, parts)
        return send(part(peer), got.at[d], ss.at[d], rs.at[d], "seq", peer)

    def start(d, carry):
        ask(d).start()
        return carry

    lax.fori_loop(1, parts, start, 0)
    shift = slots.bit_length() - 1

    def read(d, j):
        code = got[d]
        place_ref[j] = (code & (slots - 1)) * 2
        tok_ref[j] = (code >> shift) & (tokens - 1)

    keep.wait()
    read(0, me)

    def arrive(d, carry):
        ask(d).wait()
        read(d, lax.rem(me + parts - d, parts))
        return carry

    lax.fori_loop(1, parts, arrive, 0)


def request(codes, parts, slots, tokens):
    rows = codes.shape[1] // parts
    vmem = pl.BlockSpec(memory_space=pltpu.VMEM)
    dma = pltpu.SemaphoreType.DMA
    shape = (parts, 2, rows)
    return pl.pallas_call(
        functools.partial(request_kernel, parts=parts, slots=slots, tokens=tokens),
        out_shape=(jax.ShapeDtypeStruct(shape, jnp.int32),) * 2,
        in_specs=[vmem],
        out_specs=(vmem,) * 2,
        scratch_shapes=[pltpu.VMEM(shape, jnp.int32), dma, dma((parts,)), dma((parts,))],
        compiler_params=pltpu.CompilerParams(
            vmem_limit_bytes=8 * MIB, collective_id=6, has_side_effects=True
        ),
        name="request",
    )(codes)


class HeadSum:
    def __init__(self, src, scratch, sems, full=None, full_sems=None):
        self.src, self.full = src, full
        self.core_recv, self.side_send, self.side_recv = scratch
        self.core_ss, self.core_rs, self.side_ss, self.side_rs = sems
        self.full_sems = full_sems
        head = lax.axis_index("head")
        self.y, self.c = head // 2, lax.rem(head, 2)
        self.share = src.shape[0] // 4
        self.core = 2 * self.y + 1 - self.c
        self.side = 2 * (1 - self.y) + self.c
        self.mine = self.rows_of(head)

    def rows_of(self, place):
        return pl.ds(pl.multiple_of(place * self.share, self.share), self.share)

    def to_core(self, i):
        y = self.y if i == 0 else 1 - self.y
        src = self.src.at[self.rows_of(2 * y + 1 - self.c)]
        return send(src, self.core_recv.at[i], self.core_ss.at[i], self.core_rs.at[i], "head", self.core)

    def to_side(self):
        return send(self.side_send, self.side_recv, self.side_ss, self.side_rs, "head", self.side)

    def start(self):
        self.to_core(1).start()
        self.to_core(0).start()

    def relay(self):
        self.to_core(1).wait()
        other = self.src[self.rows_of(self.side), :].astype(f32)
        self.side_send[...] = (other + self.core_recv[1].astype(f32)).astype(bf16)
        self.to_side().start()

    def total(self):
        self.to_core(0).wait()
        found = self.src[self.mine, :].astype(f32) + self.core_recv[0].astype(f32)
        self.to_side().wait()
        return found + self.side_recv[...].astype(f32)

    def back(self, i):
        rows = self.rows_of(self.side) if i == 2 else self.mine
        peer = self.side if i == 1 else self.core
        ss, rs = self.full_sems
        return send(self.full.at[rows], self.full.at[rows], ss.at[i], rs.at[i], "head", peer)

    def spread(self, value):
        self.full[self.mine, :] = value.astype(self.full.dtype)
        self.back(1).start()
        self.back(0).start()

    def forward(self):
        self.back(1).wait()
        self.back(2).start()

    def settle(self):
        self.back(0).wait()
        self.back(2).wait()

    @staticmethod
    def scratch(count, width):
        piece = (count // 4, width)
        return [pltpu.VMEM((2,) + piece, bf16), pltpu.VMEM(piece, bf16), pltpu.VMEM(piece, bf16)]

    @staticmethod
    def sems():
        dma = pltpu.SemaphoreType.DMA
        return [dma((2,)), dma((2,)), dma, dma]

    @staticmethod
    def full_scratch():
        return [pltpu.SemaphoreType.DMA((3,))] * 2


class Held:
    def __init__(self, arrays, parts):
        self.arrays, self.parts = arrays, parts
        self.all = arrays[0][1].shape[0] == parts

    def fetch(self, i, j):
        hbm, place, sem = self.arrays[i]
        slot = j if self.all else 0
        return pltpu.make_async_copy(hbm.at[j], place.at[slot], sem.at[slot])

    def ahead(self):
        if self.all:

            def start(j, carry):
                for i in range(len(self.arrays)):
                    self.fetch(i, j).start()
                return carry

            lax.fori_loop(0, self.parts, start, 0)

    def get(self, j):
        for i in range(len(self.arrays)):
            if not self.all:
                self.fetch(i, j).start()
            self.fetch(i, j).wait()
        return [place.at[j if self.all else 0] for _, place, _ in self.arrays]

    @staticmethod
    def scratch(arrays, parts):
        slots = parts if parts <= 8 else 1
        places = [pltpu.VMEM((slots,) + a.shape[1:], a.dtype) for a in arrays]
        return places + [pltpu.SemaphoreType.DMA((slots,))] * len(arrays)


def attend_kernel(
    lengths_ref,
    gate_ref,
    q_ref,
    k_ref,
    v_ref,
    bias_ref,
    tok_ref,
    q_all_hbm,
    rows_hbm,
    mixed_ref,
    recalled_ref,
    local_ref,
    logs_ref,
    p_ref,
    pair_ref,
    out_xs,
    out_xr,
    out_zs,
    out_zr,
    log_xs,
    log_xr,
    log_zs,
    log_zr,
    q_all,
    rows,
    q_sem,
    rows_sem,
    ox_ss,
    ox_rs,
    oz_ss,
    oz_rs,
    lx_ss,
    lx_rs,
    lz_ss,
    lz_rs,
    pair_ss,
    pair_rs,
    *,
    parts,
    scale,
):
    count, span = q_ref.shape[0], pair_ref.shape[1]
    per = tok_ref.shape[2]
    half = parts // 2
    me = lax.axis_index("seq")
    x, z = lax.rem(me, 2), me // 2
    partner = me + 1 - 2 * x

    def reader(c, dz):
        at = lax.rem(z + half - dz, half)
        return 2 * at + (x if c == 0 else 1 - x)

    held = Held(((q_all_hbm, q_all, q_sem), (rows_hbm, rows, rows_sem)), parts)
    held.ahead()
    pair_ref[0, W:, :] = k_ref[...]
    pair_ref[1, W:, :] = v_ref[...]

    @pl.when(z == 0)
    def _():
        pair_ref[:, :count] = jnp.zeros_like(pair_ref[:, :count])

    @pl.when(me == 0)
    def _():
        pair_ref[:, count:W] = jnp.zeros_like(pair_ref[:, count:W])

    greet(seq=parts)

    def pair_rows(first):
        return pair_ref.at[:, pl.ds(first, count)]

    def hand_on(i, source, target, peer):
        return send(
            pair_rows(source), pair_rows(target), pair_ss.at[i], pair_rs.at[i], "seq", peer
        )

    next_one = hand_on(0, W, count, partner)
    next_two = hand_on(1, W, 0, me + 2)
    passed_on = hand_on(2, 0, count, partner)

    @pl.when(z < half - 1)
    def _():
        next_two.start()

    @pl.when(x == 0)
    def _():
        next_one.start()

    ids = lax.broadcasted_iota(jnp.int32, (count, per), 0)

    def owner_part(j):
        q_at, rows_at = held.get(j)
        outs, logs = [], []
        for h in range(2):
            cols = head_cols(h)
            keep = tok_ref[j, h : h + 1, :] == ids
            s = jnp.where(keep, nt(q_at[:, cols], rows_at[h, :, 0:128]), NEG)
            top = jnp.max(s, axis=1, keepdims=True)
            p = jnp.where(keep, jnp.exp((s - top) * scale), 0.0)
            total = jnp.sum(p, axis=1, keepdims=True)
            some = total > 0.0
            safe = jnp.where(some, total, 1.0)
            outs.append(nn(p.astype(bf16), rows_at[h, :, 128:256]) / safe)
            logs.append(jnp.where(some, top * scale + jnp.log(safe), NEG))
        return outs, logs

    def give_x(dz):
        return (
            send(log_xs.at[dz], log_xr.at[dz], lx_ss.at[dz], lx_rs.at[dz], "seq", partner),
            send(out_xs.at[dz], out_xr.at[dz], ox_ss.at[dz], ox_rs.at[dz], "seq", partner),
        )

    def log_z(dz):
        return send(
            log_zs.at[dz], log_zr.at[dz], lz_ss.at[dz], lz_rs.at[dz], "seq", reader(0, dz)
        )

    def out_z(dz):
        return send(
            out_zs.at[dz], out_zr.at[dz], oz_ss.at[dz], oz_rs.at[dz], "seq", reader(0, dz)
        )

    def neighbour(dz):
        outs, logs = owner_part(reader(1, dz))
        for h in range(2):
            out_xs[dz, h] = outs[h].astype(bf16)
        log_xs[dz] = row_form(logs, count).T[0:8]
        for copy in give_x(dz):
            copy.start()

    def join(outs, logs, dz):
        for copy in give_x(dz):
            copy.wait()
        other = log_xr[dz].T
        joined = []
        for h in range(2):
            theirs = other[:, h : h + 1]
            top = jnp.maximum(logs[h], theirs)
            a, b = jnp.exp(logs[h] - top), jnp.exp(theirs - top)
            total = a + b
            outs[h] = outs[h] * (a / total) + out_xr[dz, h].astype(f32) * (b / total)
            joined.append(top + jnp.log(total))
        return outs, joined

    def neighbour_step(dz, carry):
        neighbour(dz)
        return carry

    lax.fori_loop(1, half, neighbour_step, 0)
    neighbour(0)

    @pl.when(z > 0)
    def _():
        hand_on(1, W, 0, partner).wait_recv()

        @pl.when(x == 1)
        def _():
            passed_on.start()

    def column_step(dz, carry):
        outs, logs = owner_part(reader(0, dz))
        outs, logs = join(outs, logs, dz)
        for h in range(2):
            out_zs[dz, h] = outs[h].astype(bf16)
        log_zs[dz] = row_form(logs, count).T[0:8]
        log_z(dz).start()
        out_z(dz).start()
        return carry

    lax.fori_loop(1, half, column_step, 0)
    outs, logs = owner_part(me)
    outs, logs = join(outs, logs, 0)
    log_zr[0] = row_form(logs, count).T[0:8]
    for h in range(2):
        recalled_ref[:, head_cols(h)] = outs[h]

    @pl.when(x == 0)
    def _():
        next_one.wait_send()

        @pl.when(z > 0)
        def _():
            passed_on.wait_recv()

    @pl.when(x == 1)
    def _():
        next_one.wait_recv()

        @pl.when(z > 0)
        def _():
            passed_on.wait_send()

    @pl.when(z < half - 1)
    def _():
        next_two.wait_send()

    first = me * count
    start = doc_starts(lengths_ref, first, count)
    key_place = first - W + lax.broadcasted_iota(jnp.int32, (count, span), 1)
    seen = key_place >= start
    for h in range(2):
        cols = head_cols(h)
        bias = pltpu.roll(
            jnp.broadcast_to(bias_ref[h : h + 1, :], (count, span)), 0, 1, stride=1, stride_axis=0
        )
        s = nt(q_ref[:, cols], pair_ref[0, :, cols]) * scale + bias
        s = jnp.where(seen, s, NEG)
        raised = jnp.exp(s - jnp.max(s, axis=1, keepdims=True))
        p = raised / jnp.sum(raised, axis=1, keepdims=True)
        p_ref[h] = p
        local_ref[:, cols] = nn(p.astype(bf16), pair_ref[1, :, cols])

    def wait_log(dz, top):
        log_z(dz).wait()
        return jnp.maximum(top, log_zr[dz])

    top = lax.fori_loop(1, half, wait_log, log_zr[0])

    def add_to(dz, total):
        return total + jnp.exp(log_zr[dz] - top)

    logs = top + jnp.log(lax.fori_loop(0, half, add_to, jnp.zeros_like(top)))
    logs_ref[...] = logs
    share = jnp.exp(log_zr[0] - logs).T
    for h in range(2):
        recalled_ref[:, head_cols(h)] *= share[:, h : h + 1]

    def merge(dz, carry):
        share = jnp.exp(log_zr[dz] - logs).T
        out_z(dz).wait()
        for h in range(2):
            recalled_ref[:, head_cols(h)] += share[:, h : h + 1] * out_zr[dz, h].astype(f32)
        return carry

    lax.fori_loop(1, half, merge, 0)
    for h in range(2):
        cols = head_cols(h)
        gate = gate_ref[h]
        mixed = gate * recalled_ref[:, cols] + (1.0 - gate) * local_ref[:, cols]
        mixed_ref[:, cols] = mixed.astype(bf16)


def attend(lengths, gate, q, k, v, bias, q_all, tok, rows):
    parts, count, width = q_all.shape
    span, half = W + count, parts // 2
    smem = pl.BlockSpec(memory_space=pltpu.SMEM)
    vmem = pl.BlockSpec(memory_space=pltpu.VMEM)
    hbm = pl.BlockSpec(memory_space=pltpu.HBM)
    dma = pltpu.SemaphoreType.DMA
    return pl.pallas_call(
        functools.partial(attend_kernel, parts=parts, scale=128**-0.5),
        out_shape=(
            jax.ShapeDtypeStruct((count, width), bf16),
            jax.ShapeDtypeStruct((count, width), f32),
            jax.ShapeDtypeStruct((count, width), f32),
            jax.ShapeDtypeStruct((8, count), f32),
            jax.ShapeDtypeStruct((2, count, span), f32),
            jax.ShapeDtypeStruct((2, span, width), bf16),
        ),
        in_specs=[smem, smem] + [vmem] * 5 + [hbm] * 2,
        out_specs=(vmem,) * 6,
        scratch_shapes=[pltpu.VMEM((half, 2, count, 128), bf16)] * 4
        + [pltpu.VMEM((half, 8, count), f32)] * 4
        + Held.scratch((q_all, rows), parts)
        + [dma((half,))] * 8
        + [dma((3,))] * 2,
        compiler_params=pltpu.CompilerParams(
            vmem_limit_bytes=58 * MIB, collective_id=1, has_side_effects=True
        ),
        cost_estimate=pl.CostEstimate(
            flops=3 * 10**9, bytes_accessed=100 * MIB, transcendentals=5 * 10**6
        ),
        name="attend",
    )(lengths, gate, q, k, v, bias, tok, q_all, rows)


class ScatterSum:
    def __init__(self, grads, sems, parts):
        self.grads, self.sems = grads, sems
        self.quarter = parts // 4
        self.own = grads[0][0].shape[0] // parts
        me = lax.axis_index("seq")
        self.x, self.b, self.a = lax.rem(me, 2), lax.rem(me // 2, 2), me // 4

    def place(self, da, side, x):
        b = self.b if side == 1 else 1 - self.b
        return 4 * lax.rem(self.a + da, self.quarter) + 2 * b + x

    def rows_of(self, place):
        return pl.ds(pl.multiple_of(place * self.own, self.own), self.own)

    def send_x(self, k, da, side):
        ss, rs = self.sems[0:2]
        return send(
            self.grads[k][0].at[self.rows_of(self.place(da, side, 1 - self.x))],
            self.grads[k][1].at[side, da],
            ss.at[k, side, da],
            rs.at[k, side, da],
            "seq",
            self.place(0, 1, 1 - self.x),
        )

    def send_pair(self, k, da):
        ss, rs = self.sems[2:4]
        grads, peer = self.grads[k], self.place(0, 0, self.x)
        return send(grads[2].at[da], grads[3].at[da], ss.at[k, da], rs.at[k, da], "seq", peer)

    def send_far(self, k, da):
        ss, rs = self.sems[4:6]
        grads, peer = self.grads[k], self.place(da, 1, self.x)
        return send(grads[4].at[da], grads[5].at[da], ss.at[k, da], rs.at[k, da], "seq", peer)

    def loop(self, first, last, step):
        def body(da, carry):
            for k in range(len(self.grads)):
                step(k, da)
            return carry

        lax.fori_loop(first, last, body, 0)

    def span(self, far):
        return (1, self.quarter) if far else (0, 1)

    def start(self, far, side):
        self.loop(*self.span(far), lambda k, da: self.send_x(k, da, side).start())

    def start_one(self, k):
        for far in (True, False):
            for side in range(2):

                def body(da, carry, side=side):
                    self.send_x(k, da, side).start()
                    return carry

                lax.fori_loop(*self.span(far), body, 0)

    def column(self, k, da, side):
        self.send_x(k, da, side).wait()
        mine = self.grads[k][0][self.rows_of(self.place(da, side, self.x)), :]
        return mine.astype(f32) + self.grads[k][1][side, da].astype(f32)

    def pair(self, far):
        def step(k, da):
            self.grads[k][2][da] = self.column(k, da, 0).astype(bf16)
            self.send_pair(k, da).start()

        self.loop(*self.span(far), step)

    def both(self, k, da):
        found = self.column(k, da, 1)
        self.send_pair(k, da).wait()
        return found + self.grads[k][3][da].astype(f32)

    def far(self):
        def step(k, da):
            self.grads[k][4][da] = self.both(k, da).astype(bf16)
            self.send_far(k, da).start()

        self.loop(*self.span(True), step)

    def settle(self, outs):
        for k, out in enumerate(outs):
            out[...] = self.both(k, 0)

        def step(k, da):
            self.send_far(k, da).wait()
            outs[k][...] += self.grads[k][5][da].astype(f32)

        self.loop(*self.span(True), step)

    @staticmethod
    def scratch(shapes, parts):
        quarter = parts // 4
        slots = []
        for rows, columns in shapes:
            piece = (rows // parts, columns)
            slots.append(pltpu.VMEM((2, quarter) + piece, bf16))
            slots += [pltpu.VMEM((quarter,) + piece, bf16)] * 4
        dma = pltpu.SemaphoreType.DMA
        count = len(shapes)
        return slots, [dma((count, 2, quarter))] * 2 + [dma((count, quarter))] * 4


def close_attn_kernel(*refs, names, parts):
    r = types.SimpleNamespace(**dict(zip(names, refs, strict=True)))
    greet(seq=parts, head=4)
    sums = HeadSum(
        r.sum, (r.a, r.b, r.c), (r.ss_a, r.rs_a, r.ss_b, r.rs_b), r.full, (r.ss_full, r.rs_full)
    )
    sums.start()
    copies = []
    if hasattr(r, "cot_other"):
        crossed = (
            ("cot", "z", r.cot, r.cot_other),
            ("normed", "x", r.normed, r.normed_other),
        )
        for name, first, left, other in crossed:
            joined = JoinedSum([(left, other, left, left)], [None] * 4, parts, first)
            sems = getattr(r, f"{name}_ss"), getattr(r, f"{name}_rs")
            copies += joined.cross_blocks(0, sems)
        sems = (r.mixed_ss, r.mixed_rs)
        joined = JoinedSum([(r.normed, r.normed, r.mixed, r.mixed_other)], [None] * 4, parts, "x")
        copies += joined.cross(0, sems)
        for copy in copies:
            copy.start()
    sums.relay()
    branch = sums.total()
    middle = r.inputs[sums.mine, :].astype(f32) + branch
    hat = middle * lax.rsqrt(row_mean(middle * middle) + eps)
    sums.spread(hat * r.gain[...])
    r.middle[...] = middle
    r.line[...] = col_sum(branch * branch)
    sums.forward()
    sums.settle()
    for copy in copies:
        copy.wait()


def close_attn(inputs, parts):
    count, width = inputs["sum"].shape
    vmem = pl.BlockSpec(memory_space=pltpu.VMEM)
    dma = pltpu.SemaphoreType.DMA
    outputs = dict(
        full=jax.ShapeDtypeStruct((count, width), bf16),
        middle=jax.ShapeDtypeStruct((count // 4, width), f32),
        line=jax.ShapeDtypeStruct((1, width), f32),
    )
    scratch = dict(zip("abc", HeadSum.scratch(count, width), strict=True))
    scratch |= dict(zip(("ss_a", "rs_a", "ss_b", "rs_b"), HeadSum.sems(), strict=True))
    scratch |= dict(zip(("ss_full", "rs_full"), HeadSum.full_scratch(), strict=True))
    if width // parts % 128 == 0:
        for name in ("cot", "normed"):
            outputs[f"{name}_other"] = jax.ShapeDtypeStruct((count, width // 2), bf16)
            scratch |= {f"{name}_{end}": dma((parts // 2,)) for end in ("ss", "rs")}
        outputs["mixed_other"] = jax.ShapeDtypeStruct(inputs["mixed"].shape, bf16)
        scratch |= {f"mixed_{end}": dma((1,)) for end in ("ss", "rs")}
    found = pl.pallas_call(
        functools.partial(close_attn_kernel, names=(*inputs, *outputs, *scratch), parts=parts),
        out_shape=tuple(outputs.values()),
        in_specs=[vmem] * len(inputs),
        out_specs=(vmem,) * len(outputs),
        scratch_shapes=list(scratch.values()),
        compiler_params=pltpu.CompilerParams(
            vmem_limit_bytes=16 * MIB, collective_id=3, has_side_effects=True
        ),
        cost_estimate=pl.CostEstimate(flops=10**6, bytes_accessed=30 * MIB, transcendentals=0),
        name="close_attn",
    )(*inputs.values())
    return dict(zip(outputs, found, strict=True))


def row_mean(x):
    return jnp.mean(x, axis=1, keepdims=True)


def col_sum(x):
    return jnp.sum(x, axis=0, keepdims=True)


def folded(line):
    return jnp.concatenate([line[:, 128 * i : 128 * i + 128] for i in range(8)], axis=0)


def fold_sum(line):
    return col_sum(folded(line))


class JoinedSum(ScatterSum):
    def __init__(self, grads, sems, parts, first):
        super().__init__([(g[0], *g[4:]) for g in grads], sems, parts)
        self.own = grads[0][0].shape[1] // parts
        self.operands = [g[0:4] for g in grads]
        self.first = first

    def side_of(self, first, second):
        return 2 * first + second if self.first == "z" else 2 * second + first

    def mine(self):
        return (self.b, self.x) if self.first == "z" else (self.x, self.b)

    def place(self, da, side, flip=0):
        first, second = self.mine()
        first = 1 - first if flip else first
        second = second if side == 1 else 1 - second
        return 4 * lax.rem(self.a + da, self.quarter) + self.side_of(first, second)

    def partner(self):
        return self.place(0, 1, 1)

    def columns(self, place):
        return pl.ds(pl.multiple_of(place * self.own, self.own), self.own)

    def cross_blocks(self, k, sems):
        left, slots = self.operands[k][0:2]
        first, _ = self.mine()
        copies = []
        for block in range(2 * self.quarter):
            place = 4 * (block // 2) + self.side_of(1 - first, block % 2)
            copies.append(
                send(
                    left.at[:, self.columns(place)],
                    slots.at[:, pl.ds(block * self.own, self.own)],
                    sems[0].at[block],
                    sems[1].at[block],
                    "seq",
                    self.partner(),
                )
            )
        return copies

    def cross(self, k, sems):
        right, slots = self.operands[k][2:4]
        return [send(right, slots, sems[0].at[0], sems[1].at[0], "seq", self.partner())]

    def send_pair(self, k, da):
        ss, rs = self.sems[0:2]
        grads, peer = self.grads[k], self.place(0, 0)
        return send(grads[1].at[da], grads[2].at[da], ss.at[k, da], rs.at[k, da], "seq", peer)

    def send_far(self, k, da):
        ss, rs = self.sems[2:4]
        grads, peer = self.grads[k], self.place(da, 1)
        return send(grads[3].at[da], grads[4].at[da], ss.at[k, da], rs.at[k, da], "seq", peer)

    def column(self, k, da, side):
        left, left_other, right, right_other = self.operands[k]
        _, second = self.mine()
        second = second if side == 1 else 1 - second
        block = 2 * lax.rem(self.a + da, self.quarter) + second
        found = tn(left[:, self.columns(self.place(da, side))], right[...])
        return found + tn(left_other[:, self.columns(block)], right_other[...])

    def pair(self, far):
        def step(k, da):
            self.grads[k][1][da] = self.column(k, da, 0).astype(bf16)
            self.send_pair(k, da).start()

        self.loop(*self.span(far), step)

    def both(self, k, da):
        found = self.column(k, da, 1)
        self.send_pair(k, da).wait()
        return found + self.grads[k][2][da].astype(f32)

    def far(self):
        def step(k, da):
            self.grads[k][3][da] = self.both(k, da).astype(bf16)
            self.send_far(k, da).start()

        self.loop(*self.span(True), step)

    def settle(self, outs):
        for k, out in enumerate(outs):
            out[...] = self.both(k, 0)

        def step(k, da):
            self.send_far(k, da).wait()
            outs[k][...] += self.grads[k][4][da].astype(f32)

        self.loop(*self.span(True), step)

    @staticmethod
    def scratch(shapes, parts):
        quarter = parts // 4
        slots = []
        for rows, columns in shapes:
            slots += [pltpu.VMEM((quarter, rows // parts, columns), bf16)] * 4
        return slots, [pltpu.SemaphoreType.DMA((len(shapes), quarter))] * 4


class Product:
    def __init__(self, r, name, left, right, parts, first, left_other=None, right_other=None):
        self.left, self.right = left, right
        self.joined = left.shape[1] // parts % 128 == 0

        def own(part):
            return getattr(r, f"{name}_{part}")

        if self.joined:
            left_slots = own("left") if left_other is None else left_other
            right_slots = own("right") if right_other is None else right_other
            grads = (left, left_slots, right, right_slots, *(own(i) for i in range(4)))
            self.sum = JoinedSum([grads], [own(f"sem_{i}") for i in range(4)], parts, first)
            self.lefts, self.rights = [], []
            if left_other is None:
                self.lefts = self.sum.cross_blocks(0, (own("left_ss"), own("left_rs")))
            if right_other is None:
                self.rights = self.sum.cross(0, (own("right_ss"), own("right_rs")))
        else:
            self.whole = own("whole")
            grads = (self.whole, *(own(i) for i in range(5)))
            self.sum = ScatterSum([grads], [own(f"sem_{i}") for i in range(6)], parts)
        self.pair, self.far = self.sum.pair, self.sum.far

    def begin_left(self):
        if self.joined:
            for copy in self.lefts:
                copy.start()

    def begin(self):
        if self.joined:
            for copy in self.rights:
                copy.start()
        else:
            for b in range(self.left.shape[1] // 256):
                block = slice(256 * b, 256 * b + 256)
                self.whole[block, :] = tn(self.left[:, block], self.right[...]).astype(bf16)
            self.sum.start_one(0)

    def ready(self):
        if self.joined:
            for copy in self.lefts + self.rights:
                copy.wait()

    def settle(self, out):
        self.sum.settle((out,))

    @staticmethod
    def scratch(name, count, model, columns, parts, left=True, right=True):
        own, dma = model // parts, pltpu.SemaphoreType.DMA
        found = {}
        if own % 128 == 0:
            slots, sems = JoinedSum.scratch([(model, columns)], parts)
            if left:
                found["left"] = pltpu.VMEM((count, model // 2), bf16)
                found |= {f"left_{end}": dma((parts // 2,)) for end in ("ss", "rs")}
            if right:
                found["right"] = pltpu.VMEM((count, columns), bf16)
                found |= {f"right_{end}": dma((1,)) for end in ("ss", "rs")}
        else:
            slots, sems = ScatterSum.scratch([(model, columns)], parts)
            found["whole"] = pltpu.VMEM((model, columns), bf16)
        found |= {str(i): s for i, s in enumerate(slots)}
        found |= {f"sem_{i}": s for i, s in enumerate(sems)}
        return {f"{name}_{part}": spec for part, spec in found.items()}


def back_kernel(*refs, names, parts, peers, scale):
    r = types.SimpleNamespace(**dict(zip(names, refs, strict=True)))
    count, width = r.q.shape
    span, model = r.pair.shape[1], r.cot.shape[1]
    per = r.tok.shape[2]
    half = parts // 2
    me = lax.axis_index("seq")
    x, z = lax.rem(me, 2), me // 2
    partner = me + 1 - 2 * x

    def at(o, c):
        return 2 * o + (x if c == 0 else 1 - x)

    held = Held(((r.q_all_hbm, r.q_all, r.q_sem), (r.rows_hbm, r.rows, r.rows_sem)), parts)
    held.ahead()
    greet(seq=parts, head=peers)

    def head_sum(name, source, full):
        return HeadSum(
            source,
            [getattr(r, f"{name}_{i}") for i in range(3)],
            [getattr(r, f"{name}_sem_{i}") for i in range(4)],
            full,
            [getattr(r, f"{name}_full_{i}") for i in range(2)],
        )

    sums = head_sum("sum", r.sum, r.branch)
    feeds = head_sum("feed", r.feed_in, r.layer)
    cot_other = getattr(r, "cot_other", None)
    normed_other = getattr(r, "normed_other", None)
    mixed_other = getattr(r, "mixed_other", None)
    p_down = Product(r, "down", r.cot, r.hidden, parts, "z", left_other=cot_other)
    p_up = Product(r, "up", r.normed_two, r.grad_upward, parts, "x")
    p_o = Product(r, "o", r.branch, r.mixed, parts, "x", right_other=mixed_other)
    p_kv = Product(r, "kv", r.normed, r.d_kv, parts, "x", left_other=normed_other)
    p_q = Product(r, "q", r.normed, r.d_q, parts, "x", left_other=normed_other)

    sums.start()
    p_down.begin()
    p_up.begin_left()
    p_up.begin()
    feeds.start()
    middle = r.middle[...]
    row_scale = lax.rsqrt(row_mean(middle * middle) + eps)
    hat = middle * row_scale
    sums.relay()
    grad_normed = sums.total()
    scaled = grad_normed * r.gain_two[...]
    grad_middle = r.cot[sums.mine, :].astype(f32) + row_scale * (
        scaled - hat * row_mean(scaled * hat)
    )
    sums.spread(grad_middle)
    r.grad_middle[...] = grad_middle
    r.small_send[8:16] = folded(col_sum(grad_normed * hat))
    feeds.relay()
    sums.forward()
    sums.settle()
    g_own = nt(r.branch[...], r.w_o[...]).astype(bf16)
    r.g_all[0, z] = g_own

    deltas = []
    for h in range(2):
        cols = head_cols(h)
        g = g_own[:, cols].astype(f32)
        r.small_send[19 + h : 20 + h] = col_sum(g * (r.recalled[:, cols] - r.local[:, cols]))
        both = jnp.sum(g * r.recalled[:, cols], axis=1, keepdims=True)
        deltas.append(both * r.gate[h])
    turned = row_form([jnp.zeros_like(deltas[0])] * 2 + deltas, count).T[0:8]
    row = lax.broadcasted_iota(jnp.int32, (8, count), 0)
    r.st_all[0, z] = jnp.where(row < 2, r.logs[...], turned)

    def ask(c, o, way, peer):
        return (
            send(
                r.st_all.at[0, o], r.st_all.at[c, o], r.st_ss.at[way, o], r.st_rs.at[c, o], "seq", peer
            ),
            send(r.g_all.at[0, o], r.g_all.at[c, o], r.g_ss.at[way, o], r.g_rs.at[c, o], "seq", peer),
        )

    def start(copies):
        for copy in copies:
            copy.start()

    def up(o):
        return ask(0, o, 0, me + 2)

    def down(o):
        return ask(0, o, 1, me - 2)

    def across(o):
        return ask(1, o, 2, partner)

    def arrived(c, o):
        for copy in ask(c, o, 2, partner):
            copy.wait_recv()

    def sent(copies):
        for copy in copies:
            copy.wait_send()

    @pl.when(z < half - 1)
    def _():
        start(up(z))

    @pl.when(z > 0)
    def _():
        start(down(z))

    start(across(z))
    p_down.ready()
    p_down.pair(True)

    dq = []
    for h in range(2):
        cols = head_cols(h)
        rest = 1.0 - r.gate[h]
        g = r.g_all[0, z, :, cols]
        p = r.p[h]
        e = nt(g, r.pair[1, :, cols])
        delta = jnp.sum(p * e, axis=1, keepdims=True)
        ds = (p * ((e - delta) * rest)).astype(bf16)
        r.dq_sum[:, cols] = nn(ds, r.pair[0, :, cols]) * scale
        dk = tn(ds, r.q[:, cols]) * scale
        dv = tn(p.astype(bf16), g) * rest
        r.pair_sum[0, :, cols] = dk[W:]
        r.pair_sum[1, :, cols] = dv[W:]
        r.pair_send[0, :, cols] = dk[:W].astype(bf16)
        r.pair_send[1, :, cols] = dv[:W].astype(bf16)
        low = ds.astype(f32)
        acc = low[0:8]
        for a in range(1, count // 8):
            acc = acc + pltpu.roll(low[8 * a : 8 * a + 8], (span - 8 * a) % span, 1)
        line = acc[0:1]
        for b in range(1, 8):
            line = line + pltpu.roll(acc[b : b + 1], span - b, 1)
        lines = span // 128
        for i in range(lines):
            r.small_send[24 + h * lines + i : 25 + h * lines + i] = line[:, 128 * i : 128 * i + 128]

    halo_x = send(
        r.pair_send.at[:, pl.ds(count, count)], r.halo_x, r.halo_ss.at[0], r.halo_rs.at[0], "seq", partner
    )
    halo_z = send(r.halo_send, r.halo_z, r.halo_ss.at[1], r.halo_rs.at[1], "seq", me - 2)
    halo_x.start()

    ids = lax.broadcasted_iota(jnp.int32, (count, per), 0)

    def owner_part(c, o):
        j = at(o, c)
        q_at, rows_at = held.get(j)
        stats = r.st_all[c, o].T
        found = []
        for h in range(2):
            cols = head_cols(h)
            keep = r.tok[j, h : h + 1, :] == ids
            s = nt(q_at[:, cols], rows_at[h, :, 0:128]) * scale
            p = jnp.exp(jnp.where(keep, s - stats[:, h : h + 1], NEG))
            e = nt(r.g_all[c, o, :, cols], rows_at[h, :, 128:256]) * r.gate[h]
            ds = (p * (e - stats[:, 2 + h : 3 + h])).astype(bf16)
            found.append(nn(ds, rows_at[h, :, 0:128]) * scale)
        return found

    own = owner_part(0, z)
    for h in range(2):
        r.dq_sum[:, head_cols(h)] += own[h]

    halo_x.wait()
    passing = x.astype(f32)
    r.halo_send[...] = (
        r.pair_send[:, :count].astype(f32) + r.halo_x[...].astype(f32) * passing
    ).astype(bf16)
    r.pair_sum[...] += r.halo_x[...].astype(f32) * (1.0 - passing)

    @pl.when(z > 0)
    def _():
        halo_z.start()

    def give_x(o):
        return send(r.dq_xs.at[o], r.dq_xr.at[o], r.dx_ss.at[o], r.dx_rs.at[o], "seq", partner)

    def give_z(o):
        return send(r.dq_zs.at[o], r.dq_zr.at[z], r.dz_ss.at[o], r.dz_rs.at[z], "seq", at(o, 0))

    def got_z(o):
        return send(r.dq_zs.at[o], r.dq_zr.at[o], r.dz_ss.at[o], r.dz_rs.at[o], "seq", partner)

    def neighbour(o):
        arrived(1, o)
        found = owner_part(1, o)
        for h in range(2):
            r.dq_xs[o, h] = found[h].astype(bf16)
        give_x(o).start()

    def column(o):
        found = owner_part(0, o)
        for h in range(2):
            r.dq_zs[o, h] = found[h].astype(bf16)

    def near(body):
        def step(t, carry):
            @pl.when(z - t >= 0)
            def _():
                body(z - t, True)

            @pl.when(z + t < half)
            def _():
                body(z + t, False)

            return carry

        lax.fori_loop(1, half, step, 0)

    neighbour(z)

    def relay(o, below):
        arrived(0, o)
        start(across(o))
        if below:

            @pl.when(z < half - 1)
            def _():
                start(up(o))

        else:

            @pl.when(z > 0)
            def _():
                start(down(o))

    def relay_step(t, carry):
        @pl.when(z - t >= 0)
        def _():
            relay(z - t, True)

        @pl.when(z + t < half)
        def _():
            relay(z + t, False)

        @pl.when(z - t >= 0)
        def _():
            column(z - t)

        @pl.when(z + t < half)
        def _():
            column(z + t)

        return carry

    lax.fori_loop(1, half, relay_step, 0)
    p_up.ready()
    p_up.pair(True)
    feed_sum = feeds.total()
    layer = r.middle[...] + feed_sum
    feeds.spread(layer)
    r.small_send[16:17] = fold_sum(col_sum(layer * layer))
    r.small_send[17:18] = fold_sum(r.attn_line[...])
    r.small_send[18:19] = fold_sum(col_sum(feed_sum * feed_sum))
    near(lambda o, below: neighbour(o))
    p_down.pair(False)
    p_o.begin_left()
    p_o.begin()
    p_up.pair(False)

    @pl.when(z > 0)
    def _():
        halo_z.wait_send()

    @pl.when(z < half - 1)
    def _():
        send(r.halo_send, r.halo_z, r.halo_ss.at[1], r.halo_rs.at[1], "seq", partner).wait_recv()
        r.pair_sum[...] += r.halo_z[...].astype(f32)

    def join(o, below):
        give_x(o).wait()
        for h in range(2):
            both = r.dq_zs[o, h].astype(f32) + r.dq_xr[o, h].astype(f32)
            r.dq_zs[o, h] = both.astype(bf16)
        give_z(o).start()

    near(join)
    r.d_kv[:, :width] = r.pair_sum[0].astype(bf16)
    r.d_kv[:, width:] = r.pair_sum[1].astype(bf16)
    p_kv.begin()
    feeds.forward()
    p_down.far()
    p_up.far()
    give_x(z).wait()
    for h in range(2):
        r.dq_sum[:, head_cols(h)] += r.dq_xr[z, h].astype(f32)

    def merge(o, below):
        got_z(o).wait_recv()
        for h in range(2):
            r.dq_sum[:, head_cols(h)] += r.dq_zr[o, h].astype(f32)

    near(merge)

    r.d_q[...] = r.dq_sum[...].astype(bf16)
    p_q.begin()
    for b in range(model // 256):
        block = slice(256 * b, 256 * b + 256)
        r.back[:, block] = (
            nt(r.d_q[...], r.w_q[block, :])
            + nt(r.d_kv[:, :width], r.w_k[block, :])
            + nt(r.d_kv[:, width:], r.w_v[block, :])
        ).astype(bf16)
    backs = head_sum("back", r.back, r.input_grad)
    backs.start()
    backs.relay()
    p_o.ready()
    p_o.pair(True)
    p_kv.ready()
    p_kv.pair(True)
    tokens = r.inputs[backs.mine, :].astype(f32)
    in_scale = lax.rsqrt(row_mean(tokens * tokens) + eps)
    in_hat = tokens * in_scale
    back_sum = backs.total()
    g = back_sum * r.gain_one[...]
    backs.spread(r.grad_middle[...] + in_scale * (g - in_hat * row_mean(g * in_hat)))
    r.small_send[0:8] = folded(col_sum(back_sum * in_hat))
    r.small_send[21:24] = jnp.zeros((3, 128), f32)
    r.small_send[36:40] = jnp.zeros((4, 128), f32)

    def small_heads(d):
        peer = lax.rem(lax.axis_index("head") + d, peers)
        return send(r.small_send, r.small_head.at[d], r.sh_ss.at[d], r.sh_rs.at[d], "head", peer)

    for d in range(1, peers):
        small_heads(d).start()
    p_q.ready()
    p_q.pair(True)
    backs.forward()
    p_o.far()
    p_kv.far()

    kept = lax.broadcasted_iota(jnp.int32, r.small_send.shape, 0) < 19
    found = r.small_send[...]
    for d in range(1, peers):
        small_heads(d).wait()
        found = found + jnp.where(kept, r.small_head[d], 0.0)
    r.small_seq[0] = found

    def small_seqs(d):
        peer = lax.rem(me + d, parts)
        return send(r.small_seq.at[0], r.small_seq.at[d], r.sq_ss.at[d], r.sq_rs.at[d], "seq", peer)

    def small_start(d, carry):
        small_seqs(d).start()
        return carry

    lax.fori_loop(1, parts, small_start, 0)
    p_o.pair(False)
    p_kv.pair(False)
    p_q.far()
    p_q.pair(False)
    p_down.settle(r.down_sum)
    r.down_out[...] = r.down_sum[...].T
    p_up.settle(r.up_out)
    p_o.settle(r.o_sum)
    p_kv.settle(r.kv_sum)
    r.k_out[...] = r.kv_sum[:, :width]
    r.v_out[...] = r.kv_sum[:, width:]
    r.o_out[...] = r.o_sum[...].T
    p_q.settle(r.q_out)
    r.small[...] = r.small_seq[0]

    def small_add(d, carry):
        small_seqs(d).wait()
        r.small[...] += r.small_seq[d]
        return carry

    lax.fori_loop(1, parts, small_add, 0)
    feeds.settle()
    backs.settle()

    sent(across(z))

    @pl.when(z < half - 1)
    def _():
        sent(up(z))

    @pl.when(z > 0)
    def _():
        sent(down(z))

    def drain(o, below):
        sent(across(o))
        give_z(o).wait_send()
        if below:

            @pl.when(z < half - 1)
            def _():
                sent(up(o))

        else:

            @pl.when(z > 0)
            def _():
                sent(down(o))

    near(drain)


def back(inputs, parts, peers):
    count, width = inputs["q"].shape
    model, span = inputs["cot"].shape[1], W + count
    half, own = parts // 2, model // parts
    smem = pl.BlockSpec(memory_space=pltpu.SMEM)
    vmem = pl.BlockSpec(memory_space=pltpu.VMEM)
    hbm = pl.BlockSpec(memory_space=pltpu.HBM)
    dma = pltpu.SemaphoreType.DMA
    wide = inputs["hidden"].shape[1]
    outputs = dict(
        input_grad=((count, model), bf16),
        layer=((count, model), bf16),
        q_out=((own, width), f32),
        k_out=((own, width), f32),
        v_out=((own, width), f32),
        o_out=((width, own), f32),
        up_out=((own, wide), f32),
        down_out=((wide, own), f32),
        small=((40, 128), f32),
    )
    outputs = {name: jax.ShapeDtypeStruct(*spec) for name, spec in outputs.items()}
    held = Held.scratch((inputs["q_all_hbm"], inputs["rows_hbm"]), parts)
    scratch = dict(zip(("q_all", "rows", "q_sem", "rows_sem"), held, strict=True))
    for name, spec in dict(
        branch=((count, model), bf16),
        back=((count, model), bf16),
        grad_middle=((count // peers, model), f32),
        g_all=((2, half, count, width), bf16),
        st_all=((2, half, 8, count), f32),
        dq_xs=((half, 2, count, 128), bf16),
        dq_xr=((half, 2, count, 128), bf16),
        dq_zs=((half, 2, count, 128), bf16),
        dq_zr=((half, 2, count, 128), bf16),
        pair_send=((2, W, width), bf16),
        pair_sum=((2, count, width), f32),
        halo_x=((2, count, width), bf16),
        halo_send=((2, count, width), bf16),
        halo_z=((2, count, width), bf16),
        dq_sum=((count, width), f32),
        d_kv=((count, 2 * width), bf16),
        d_q=((count, width), bf16),
        kv_sum=((own, 2 * width), f32),
        o_sum=((own, width), f32),
        down_sum=((own, wide), f32),
        small_send=((40, 128), f32),
        small_head=((peers, 40, 128), f32),
        small_seq=((parts, 40, 128), f32),
    ).items():
        scratch[name] = pltpu.VMEM(*spec)
    for name, shape in dict(
        st_ss=(3, half),
        st_rs=(2, half),
        g_ss=(3, half),
        g_rs=(2, half),
        dx_ss=(half,),
        dx_rs=(half,),
        dz_ss=(half,),
        dz_rs=(half,),
        halo_ss=(2,),
        halo_rs=(2,),
        sh_ss=(peers,),
        sh_rs=(peers,),
        sq_ss=(parts,),
        sq_rs=(parts,),
    ).items():
        scratch[name] = dma(shape)
    for name in ("sum", "feed", "back"):
        scratch |= {f"{name}_{i}": s for i, s in enumerate(HeadSum.scratch(count, model))}
        scratch |= {f"{name}_sem_{i}": s for i, s in enumerate(HeadSum.sems())}
        scratch |= {f"{name}_full_{i}": s for i, s in enumerate(HeadSum.full_scratch())}
    for name, columns, left, right in (
        ("down", wide, False, True),
        ("up", wide, True, True),
        ("o", width, True, False),
        ("kv", 2 * width, False, True),
        ("q", width, False, True),
    ):
        scratch |= Product.scratch(name, count, model, columns, parts, left, right)
    spaces = dict(gate=smem, q_all_hbm=hbm, rows_hbm=hbm)
    found = pl.pallas_call(
        functools.partial(
            back_kernel,
            names=(*inputs, *outputs, *scratch),
            parts=parts,
            peers=peers,
            scale=128**-0.5,
        ),
        out_shape=tuple(outputs.values()),
        in_specs=[spaces.get(name, vmem) for name in inputs],
        out_specs=(vmem,) * len(outputs),
        scratch_shapes=list(scratch.values()),
        compiler_params=pltpu.CompilerParams(
            vmem_limit_bytes=(40 if parts <= 8 else 62) * MIB, collective_id=2, has_side_effects=True
        ),
        cost_estimate=pl.CostEstimate(
            flops=4 * 10**9, bytes_accessed=150 * MIB, transcendentals=5 * 10**6
        ),
        name="back",
    )(*inputs.values())
    return dict(zip(outputs, found, strict=True))


def norm_stats(values):
    row_scale = lax.rsqrt(jnp.mean(values * values, axis=-1, keepdims=True) + eps)
    return (values * row_scale, row_scale)


def per_device(
    inputs,
    cotangent,
    query_weight,
    key_weight,
    value_weight,
    output_weight,
    up_weight,
    down_weight,
    first_gain,
    second_gain,
    position_bias,
    gate_bias,
    memory_table,
    retrieved,
    lengths,
):
    _, block_len, model_width = inputs.shape
    bucket_total = position_bias.shape[1]
    seq_count = lax.axis_size("seq")
    slot_count = memory_table.shape[0]

    wanted = jnp.transpose(retrieved[0], (1, 0, 2))
    token = jnp.arange(block_len, dtype=jnp.int32)[None, :, None]
    codes = (wanted // slot_count) * (block_len * slot_count) + token * slot_count + wanted % slot_count
    codes = lax.sort(codes.reshape(2, -1), dimension=1, is_stable=False)
    places, tok = request(codes, seq_count, slot_count, block_len)
    rows = gather_rows(places, widen(memory_table))

    hot, outside = diagonal_buckets(block_len, bucket_total)
    bias_row = jnp.dot(position_bias, hot, precision=highest) + outside[None]

    x, cot = inputs[0], cotangent[0]
    peers = lax.axis_size("head")
    gain_one, gain_two = first_gain[None], second_gain[None]
    gate_flat = jax.nn.sigmoid(gate_bias)
    hat_one, _ = norm_stats(x.astype(f32))
    normed_one = (hat_one * first_gain).astype(bf16)
    queries = nn(normed_one, query_weight).astype(bf16)
    keys = nn(normed_one, key_weight).astype(bf16)
    values = nn(normed_one, value_weight).astype(bf16)
    q_all = lax.all_gather(queries, "seq", axis=0)

    mixed, recalled, local_out, logs, window_weights, pair = attend(
        lengths[0], gate_flat, queries, keys, values, bias_row, q_all, tok, rows
    )

    closed = close_attn(
        dict(
            sum=nn(mixed, output_weight).astype(bf16),
            inputs=x,
            gain=gain_two,
            cot=cot,
            normed=normed_one,
            mixed=mixed,
        ),
        seq_count,
    )
    normed_two, middle, attn_line = closed.pop("full"), closed.pop("middle"), closed.pop("line")
    others = closed
    upward = nn(normed_two, up_weight)
    gelu_value, gelu_back = jax.vjp(jax.nn.gelu, upward)
    hidden = gelu_value.astype(bf16)
    grad_upward = gelu_back(nt(cot, down_weight))[0].astype(bf16)
    done = back(
        dict(
            gate=gate_flat,
            sum=nt(grad_upward, up_weight).astype(bf16),
            feed_in=nn(hidden, down_weight).astype(bf16),
            hidden=hidden,
            grad_upward=grad_upward,
            normed_two=normed_two,
            **others,
            cot=cot,
            inputs=x,
            gain_one=gain_one,
            gain_two=gain_two,
            middle=middle,
            attn_line=attn_line,
            w_o=output_weight,
            w_q=query_weight,
            w_k=key_weight,
            w_v=value_weight,
            normed=normed_one,
            mixed=mixed,
            q=queries,
            recalled=recalled,
            local=local_out,
            logs=logs,
            p=window_weights,
            pair=pair,
            tok=tok,
            q_all_hbm=q_all,
            rows_hbm=rows,
        ),
        seq_count,
        peers,
    )
    small = done["small"]
    entry_count = float(block_len * model_width * seq_count)
    share = model_width // seq_count
    gains = small[:16].reshape(2, model_width)
    own_gains = lax.dynamic_slice_in_dim(gains, lax.axis_index("seq") * share, share, 1)
    position_grad = jnp.dot(small[24:36].reshape(2, -1), hot.T, precision=highest)
    gate_grad = jnp.sum(small[19:21], axis=1) * gate_flat * (1.0 - gate_flat)
    return (
        done["layer"][None],
        done["input_grad"].astype(f32)[None],
        done["q_out"],
        done["k_out"],
        done["v_out"],
        done["o_out"],
        done["up_out"],
        done["down_out"],
        own_gains[0],
        own_gains[1],
        position_grad,
        gate_grad,
        jnp.sqrt(jnp.sum(small[16:19], axis=1) / entry_count),
    )


def solution(mesh):
    in_specs = (
        P(None, "seq", None),
        P(None, "seq", None),
        P(None, "head"),
        P(None, "head"),
        P(None, "head"),
        P("head", None),
        P(None, "head"),
        P("head", None),
        P(),
        P(),
        P("head", None),
        P("head"),
        P("seq", "head", None),
        P(None, "seq", "head", None),
        P(),
    )
    out_specs = (
        P(None, "seq", None),
        P(None, "seq", None),
        P("seq", "head"),
        P("seq", "head"),
        P("seq", "head"),
        P("head", "seq"),
        P("seq", "head"),
        P("head", "seq"),
        P("seq"),
        P("seq"),
        P("head", None),
        P("head"),
        P(),
    )
    return jax.shard_map(
        per_device, mesh=mesh, in_specs=in_specs, out_specs=out_specs, check_vma=False
    )
```

time: 278 us -> 254 us (0.914)
  local copies, waits for them, and re-layouts: 33.1 us -> 15.4 us
  matrix products: 18.2 us -> 12.4 us
  Pallas kernels: 205 us -> 200 us
  other arithmetic: 4.65 us -> 8.94 us
    unnamed x82 -> x77, local copies, waits for them, and re-layouts: 29 us -> 12.6 us
    pallas_call x3 -> x2, Pallas kernels: 137 us -> 125 us  [the longest x1 110 us: back(): pl.pallas_call(functools.partial(back_kernel, names=(*inputs, *outputs, *...]
    pallas_call x1, Pallas kernels: 6.63 us -> 14.6 us  [widen(): pl.pallas_call(functools.partial(widen_kernel, chunk=chunk, part=32), out...]
    dot_general x5 -> x2, matrix products: 5.41 us -> 1.96 us  [nt(): lax.dot_general(a, b, (((1,), (1,)), ((), ())), preferred_element_type=f32)]
    dot_general x5 -> x1, matrix products: 4.98 us -> 1.86 us  [per_device(): jnp.dot(small[24:36].reshape(2, -1), hot.T, precision=highest)]
  transfers between devices with their start and end apart: 1 -> 1, of which waited for: 0 -> 0; matrix products, arithmetic and copies ran while one was open for 1% -> 2% of each run, Pallas kernels for 14% -> 18%
where the time goes in v4:
time: 254 us; the launch traced here: 252 us
  Pallas kernels  200 us (79%)
  between operations  16 us (6%)
  local copies, waits for them, and re-layouts  15.4 us (6%)
  matrix products  12.4 us (5%)
  other arithmetic  8.94 us (4%)
    pallas_call x1, Pallas kernels, back(): pl.pallas_call(functools.partial(back_kernel, names=(*inputs, *outputs, *...  110 us
    pallas_call x1, Pallas kernels, attend(): pl.pallas_call(functools.partial(attend_kernel, parts=parts, scale=128 **...  29.1 us
    pallas_call x1, Pallas kernels, gather_rows(): pl.pallas_call(functools.partial(gather_kernel, unroll=unroll, group=unro...  21.9 us
    pallas_call x1, Pallas kernels, close_attn(): pl.pallas_call(functools.partial(close_attn_kernel, names=(*inputs, *outp...  14.8 us
    pallas_call x1, Pallas kernels, widen(): pl.pallas_call(functools.partial(widen_kernel, chunk=chunk, part=32), out...  14.6 us
    unnamed x77, local copies, waits for them, and re-layouts  12.6 us
    pallas_call x1, Pallas kernels, request(): pl.pallas_call(functools.partial(request_kernel, parts=parts, slots=slots...  8.68 us
    dot_general x6, matrix products, nn(): lax.dot_general(a, b, (((1,), (0,)), ((), ())), preferred_element_type=f32)  7.79 us
  transfers between devices with their start and end apart: 1, of which 0 were waited for; matrix products, arithmetic and copies ran while one was open for 2% of the time, Pallas kernels for 18%

profile of v4, /device:TPU:0, one launch (start us, length us, event | category | flops | bytes accessed | tf_op | source)
XLA Modules:
  0.0 252.4 jit_solution(17889183394609753025)
XLA Ops:
  8.1 1.1 fusion.13
  9.3 0.8 reshape.52
  10.2 1.2 fusion.1
  11.4 1.2 fusion.3.refs_4_.refs_19_
  12.7 1.0 convolution_convert_fusion.5.q_ref.refs_21_
  13.7 14.6 %widen.1.wide_hbm = f32[2,16384,128]{2,1,0:T(8,128)} custom-call(bf16[8192,2,256]{2,1,0:T(2,128)(2,1)} %table_hbm.1), custom_call_target="tpu_custom_call" | custom-call | bytes 41943040 | tf_op jit(solution)/shard_map/widen/pallas_call | solution.py:101
  28.9 0.8 fusion.bias_ref
  29.6 2.0 convolution_convert_fusion.3.v_ref
  31.6 2.0 convolution_convert_fusion.4.k_ref
  33.6 0.8 copy-done.24
  34.5 8.7 %request.1 = (s32[8,2,1024]{2,1,0:T(2,128)S(1)}, s32[8,2,1024]{2,1,0:T(2,128)S(1)}) custom-call(s32[2,8192]{1,0:T(2,128)S(1)} %copy-done.24), custom_call_target="tpu_custom_call" | custom-call | tf_op jit(solution)/shard_map/request/pallas_call | solution.py:283
  44.4 21.9 %gather_rows.1.rows_hbm.refs_29_ = bf16[8,2,1024,256]{3,2,1,0:T(8,128)(2,1)} custom-call(s32[16384]{0:T(1024)} %bitcast.76, f32[2,16384,128]{2,1,0:T(8,128)} %widen.1.wide_hbm), custom_call_target="tpu_custom_call" | custom-call | bytes 104857600 | tf_op jit(solution)/shard_map/gather_rows/pallas_call | solution.py:172
  66.4 29.1 %attend.1 = (bf16[256,256]{1,0:T(8,128)(2,1)}, f32[256,256]{1,0:T(8,128)}, f32[256,256]{1,0:T(8,128)}, f32[8,256]{1,0:T(8,128)}, f32[2,256,768]{2,1,0:T(8,128)}, /*index=5*/bf16[2,768,256]{2,1,0:T(8,128)(2,1)}) custom-call(s32[4]{0:T(128)} %bitcast.77, f32[2]{0:T(128)} %add_divide_fusion.gate_ref.refs_0_, ...), custom_call_target="tpu_custom_call" | custom-call | flops 3000000000 | bytes 104857600 | tf_op jit(solution)/shard_map/attend/pallas_call | solution.py:653
  95.5 1.2 convolution_convert_fusion.refs_0_
  96.7 0.9 copy-done.9
  97.6 14.8 %close_attn.1 = (bf16[256,1024]{1,0:T(8,128)(2,1)S(1)}, f32[64,1024]{1,0:T(8,128)S(1)}, f32[1,1024]{1,0:T(1,128)S(1)}, bf16[256,512]{1,0:T(8,128)(2,1)S(1)}, bf1...) custom-call(bf16[256,1024]{1,0:T(8,128)(2,1)S(1)} %convolution_convert_fusion.refs_0_, ...), custom_call_target="tpu_custom_call" | custom-call | flops 1000000 | bytes 31457280 | tf_op jit(solution)/shard_map/close_attn/pallas_call | solution.py:840
  112.5 0.9 multiply_convert_fusion
  114.1 1.2 fusion.10.refs_4_
  115.4 0.7 convolution_convert_fusion.2.refs_1_
  116.2 0.7 convolution_convert_fusion.1.refs_2_
  118.2 110.5 %back.1 = (bf16[256,1024]{1,0:T(8,128)(2,1)S(1)}, bf16[256,1024]{1,0:T(8,128)(2,1)S(1)}, f32[128,256]{1,0:T(8,128)S(1)}, f32[128,256]{1,0:T(8,128)S(1)}, f32[128...) custom-call(f32[2]{0:T(128)S(1)} %copy-done.28, ...), custom_call_target="tpu_custom_call" | custom-call | flops 4000000000 | bytes 157286400 | tf_op jit(solution)/shard_map/back/pallas_call | solution.py:1523
  229.4 0.7 slice_reduce_fusion
  230.8 1.1 bitcast_convert_fusion
  232.5 0.7 constant_dynamic-slice_fusion
  233.7 1.2 multiply_sqrt_fusion
  234.9 1.2 subtract_multiply_fusion
  236.1 1.9 fusion.23
  237.9 1.9 copy.40
  239.8 1.6 copy.41
  241.4 0.7 copy.42
  243.3 0.8 copy.45
  244.1 0.8 copy.46
  (85 shorter events, 7.8 us)
Async XLA Ops:
  8.0 104.5 %copy-start = (bf16[1024,1024]{1,0:T(8,128)(2,1)S(1)}, bf16[1024,1024]{1,0:T(8,128)(2,1)}, u32[]{:S(2)}) copy-start(bf16[1024,1024]{1,0:T(8,128)(2,1)} %param.24) | copy-start | bytes 6291460
  8.0 4.7 %copy-start.3 = (bf16[1024,256]{1,0:T(8,128)(2,1)S(1)}, bf16[1024,256]{1,0:T(8,128)(2,1)}, u32[]{:S(2)}) copy-start(bf16[1024,256]{1,0:T(8,128)(2,1)} %refs_16_.1) | copy-start | bytes 1572868
  8.0 25.6 %sort.9.cloned.1.call-start = ((), (), s32[]{:S(2)}) async-start(), calls=%async_computation.1 | async-start | bytes 196640 | tf_op jit(solution)/shard_map/sort | solution.py:1576
  10.1 56.2 %all-gather.3.cloned.1.call-start = ((), (), s32[]{:S(2)}) async-start(), calls=%async_computation | async-start | bytes 1179648 | tf_op jit(solution)/shard_map/all_gather | solution.py:1592
  13.7 14.6 %copy-start.33 = (f32[2]{0:T(128)S(1)}, f32[2]{0:T(128)}, u32[]{:S(2)}) copy-start(f32[2]{0:T(128)} %param.29) | copy-start | bytes 28
  13.7 15.1 %copy-start.29 = (f32[32,768]{1,0:T(8,128)S(1)}, f32[32,768]{1,0:T(8,128)}, u32[]{:S(2)}) copy-start(f32[32,768]{1,0:T(8,128)} %constant.71.clone) | copy-start | bytes 294916
  13.7 15.1 %copy-start.30 = (f32[768]{0:T(1024)S(1)}, f32[768]{0:T(1024)}, u32[]{:S(2)}) copy-start(f32[768]{0:T(1024)} %constant.78) | copy-start | bytes 9220
  13.7 15.1 %copy-start.31 = (f32[2,32]{1,0:T(2,128)S(1)}, f32[2,32]{1,0:T(2,128)}, u32[]{:S(2)}) copy-start(f32[2,32]{1,0:T(2,128)} %param.28) | copy-start | bytes 772
  66.3 29.2 %copy-start.6 = (bf16[256,1024]{1,0:T(8,128)(2,1)S(1)}, bf16[256,1024]{1,0:T(8,128)(2,1)}, u32[]{:S(2)}) copy-start(bf16[256,1024]{1,0:T(8,128)(2,1)} %refs_15_.1) | copy-start | bytes 1572868
  66.3 30.4 %copy-start.1 = (bf16[1,256,1024]{2,1,0:T(8,128)(2,1)S(1)}, bf16[1,256,1024]{2,1,0:T(8,128)(2,1)}, u32[]{:S(2)}) copy-start(bf16[1,256,1024]{2,1,0:T(8,128)(2,1)} %param.18) | copy-start | bytes 1572868
  66.3 30.4 %copy-start.2 = (bf16[1,256,1024]{2,1,0:T(8,128)(2,1)S(1)}, bf16[1,256,1024]{2,1,0:T(8,128)(2,1)}, u32[]{:S(2)}) copy-start(bf16[1,256,1024]{2,1,0:T(8,128)(2,1)} %param.19) | copy-start | bytes 1572868
  66.3 30.4 %copy-start.26 = (f32[1024]{0:T(1024)S(1)}, f32[1024]{0:T(1024)}, u32[]{:S(2)}) copy-start(f32[1024]{0:T(1024)} %param.27) | copy-start | bytes 12292
  112.5 1.6 copy-start.32
  115.3 1.6 copy-start.12
  115.3 1.6 copy-start.13
  115.3 1.6 copy-start.19
  115.3 1.6 copy-start.20
  116.1 1.2 copy-start.4
  116.1 1.4 copy-start.5
  116.1 1.5 copy-start.7
  116.1 2.0 copy-start.8
  116.2 2.0 copy-start.10
  116.2 2.0 copy-start.11
  116.2 2.0 copy-start.23
  116.2 2.0 copy-start.25
  116.2 2.0 copy-start.27
  116.2 2.0 copy-start.28
  229.4 2.5 copy-start.14
  229.4 2.5 copy-start.16
  229.4 2.5 copy-start.18
  231.9 12.3 %copy-start.15 = (f32[1024,128]{1,0:T(8,128)S(1)}, f32[1024,128]{1,0:T(8,128)}, u32[]{:S(2)}) copy-start(f32[1024,128]{1,0:T(8,128)} %copy-done.14) | copy-start | bytes 1572868
  231.9 11.5 %copy-start.17 = (f32[128,1024]{1,0:T(8,128)S(1)}, f32[128,1024]{1,0:T(8,128)}, u32[]{:S(2)}) copy-start(f32[128,1024]{1,0:T(8,128)} %copy-done.16) | copy-start | bytes 1572868
  (4 other events, 3.0 us)
Sparse Core Ops, SparseCore 0:
  11.9 16.9 sort.11.cloned.1.call-done
  (1 shorter events, 0.0 us)
Sparse Core Ops, SparseCore 1:
  13.8 43.1 all-gather.2

commit v5 on v4

--- a/solution.py
+++ b/solution.py
@@ -387,11 +387,12 @@
 
             lax.fori_loop(0, self.parts, start, 0)
 
-    def get(self, j):
+    def get(self, j, again=False):
         for i in range(len(self.arrays)):
             if not self.all:
                 self.fetch(i, j).start()
-            self.fetch(i, j).wait()
+            if not (self.all and again):
+                self.fetch(i, j).wait()
         return [place.at[j if self.all else 0] for _, place, _ in self.arrays]
 
     @staticmethod
@@ -399,282 +400,6 @@
         slots = parts if parts <= 8 else 1
         places = [pltpu.VMEM((slots,) + a.shape[1:], a.dtype) for a in arrays]
         return places + [pltpu.SemaphoreType.DMA((slots,))] * len(arrays)
-
-
-def attend_kernel(
-    lengths_ref,
-    gate_ref,
-    q_ref,
-    k_ref,
-    v_ref,
-    bias_ref,
-    tok_ref,
-    q_all_hbm,
-    rows_hbm,
-    mixed_ref,
-    recalled_ref,
-    local_ref,
-    logs_ref,
-    p_ref,
-    pair_ref,
-    out_xs,
-    out_xr,
-    out_zs,
-    out_zr,
-    log_xs,
-    log_xr,
-    log_zs,
-    log_zr,
-    q_all,
-    rows,
-    q_sem,
-    rows_sem,
-    ox_ss,
-    ox_rs,
-    oz_ss,
-    oz_rs,
-    lx_ss,
-    lx_rs,
-    lz_ss,
-    lz_rs,
-    pair_ss,
-    pair_rs,
-    *,
-    parts,
-    scale,
-):
-    count, span = q_ref.shape[0], pair_ref.shape[1]
-    per = tok_ref.shape[2]
-    half = parts // 2
-    me = lax.axis_index("seq")
-    x, z = lax.rem(me, 2), me // 2
-    partner = me + 1 - 2 * x
-
-    def reader(c, dz):
-        at = lax.rem(z + half - dz, half)
-        return 2 * at + (x if c == 0 else 1 - x)
-
-    held = Held(((q_all_hbm, q_all, q_sem), (rows_hbm, rows, rows_sem)), parts)
-    held.ahead()
-    pair_ref[0, W:, :] = k_ref[...]
-    pair_ref[1, W:, :] = v_ref[...]
-
-    @pl.when(z == 0)
-    def _():
-        pair_ref[:, :count] = jnp.zeros_like(pair_ref[:, :count])
-
-    @pl.when(me == 0)
-    def _():
-        pair_ref[:, count:W] = jnp.zeros_like(pair_ref[:, count:W])
-
-    greet(seq=parts)
-
-    def pair_rows(first):
-        return pair_ref.at[:, pl.ds(first, count)]
-
-    def hand_on(i, source, target, peer):
-        return send(
-            pair_rows(source), pair_rows(target), pair_ss.at[i], pair_rs.at[i], "seq", peer
-        )
-
-    next_one = hand_on(0, W, count, partner)
-    next_two = hand_on(1, W, 0, me + 2)
-    passed_on = hand_on(2, 0, count, partner)
-
-    @pl.when(z < half - 1)
-    def _():
-        next_two.start()
-
-    @pl.when(x == 0)
-    def _():
-        next_one.start()
-
-    ids = lax.broadcasted_iota(jnp.int32, (count, per), 0)
-
-    def owner_part(j):
-        q_at, rows_at = held.get(j)
-        outs, logs = [], []
-        for h in range(2):
-            cols = head_cols(h)
-            keep = tok_ref[j, h : h + 1, :] == ids
-            s = jnp.where(keep, nt(q_at[:, cols], rows_at[h, :, 0:128]), NEG)
-            top = jnp.max(s, axis=1, keepdims=True)
-            p = jnp.where(keep, jnp.exp((s - top) * scale), 0.0)
-            total = jnp.sum(p, axis=1, keepdims=True)
-            some = total > 0.0
-            safe = jnp.where(some, total, 1.0)
-            outs.append(nn(p.astype(bf16), rows_at[h, :, 128:256]) / safe)
-            logs.append(jnp.where(some, top * scale + jnp.log(safe), NEG))
-        return outs, logs
-
-    def give_x(dz):
-        return (
-            send(log_xs.at[dz], log_xr.at[dz], lx_ss.at[dz], lx_rs.at[dz], "seq", partner),
-            send(out_xs.at[dz], out_xr.at[dz], ox_ss.at[dz], ox_rs.at[dz], "seq", partner),
-        )
-
-    def log_z(dz):
-        return send(
-            log_zs.at[dz], log_zr.at[dz], lz_ss.at[dz], lz_rs.at[dz], "seq", reader(0, dz)
-        )
-
-    def out_z(dz):
-        return send(
-            out_zs.at[dz], out_zr.at[dz], oz_ss.at[dz], oz_rs.at[dz], "seq", reader(0, dz)
-        )
-
-    def neighbour(dz):
-        outs, logs = owner_part(reader(1, dz))
-        for h in range(2):
-            out_xs[dz, h] = outs[h].astype(bf16)
-        log_xs[dz] = row_form(logs, count).T[0:8]
-        for copy in give_x(dz):
-            copy.start()
-
-    def join(outs, logs, dz):
-        for copy in give_x(dz):
-            copy.wait()
-        other = log_xr[dz].T
-        joined = []
-        for h in range(2):
-            theirs = other[:, h : h + 1]
-            top = jnp.maximum(logs[h], theirs)
-            a, b = jnp.exp(logs[h] - top), jnp.exp(theirs - top)
-            total = a + b
-            outs[h] = outs[h] * (a / total) + out_xr[dz, h].astype(f32) * (b / total)
-            joined.append(top + jnp.log(total))
-        return outs, joined
-
-    def neighbour_step(dz, carry):
-        neighbour(dz)
-        return carry
-
-    lax.fori_loop(1, half, neighbour_step, 0)
-    neighbour(0)
-
-    @pl.when(z > 0)
-    def _():
-        hand_on(1, W, 0, partner).wait_recv()
-
-        @pl.when(x == 1)
-        def _():
-            passed_on.start()
-
-    def column_step(dz, carry):
-        outs, logs = owner_part(reader(0, dz))
-        outs, logs = join(outs, logs, dz)
-        for h in range(2):
-            out_zs[dz, h] = outs[h].astype(bf16)
-        log_zs[dz] = row_form(logs, count).T[0:8]
-        log_z(dz).start()
-        out_z(dz).start()
-        return carry
-
-    lax.fori_loop(1, half, column_step, 0)
-    outs, logs = owner_part(me)
-    outs, logs = join(outs, logs, 0)
-    log_zr[0] = row_form(logs, count).T[0:8]
-    for h in range(2):
-        recalled_ref[:, head_cols(h)] = outs[h]
-
-    @pl.when(x == 0)
-    def _():
-        next_one.wait_send()
-
-        @pl.when(z > 0)
-        def _():
-            passed_on.wait_recv()
-
-    @pl.when(x == 1)
-    def _():
-        next_one.wait_recv()
-
-        @pl.when(z > 0)
-        def _():
-            passed_on.wait_send()
-
-    @pl.when(z < half - 1)
-    def _():
-        next_two.wait_send()
-
-    first = me * count
-    start = doc_starts(lengths_ref, first, count)
-    key_place = first - W + lax.broadcasted_iota(jnp.int32, (count, span), 1)
-    seen = key_place >= start
-    for h in range(2):
-        cols = head_cols(h)
-        bias = pltpu.roll(
-            jnp.broadcast_to(bias_ref[h : h + 1, :], (count, span)), 0, 1, stride=1, stride_axis=0
-        )
-        s = nt(q_ref[:, cols], pair_ref[0, :, cols]) * scale + bias
-        s = jnp.where(seen, s, NEG)
-        raised = jnp.exp(s - jnp.max(s, axis=1, keepdims=True))
-        p = raised / jnp.sum(raised, axis=1, keepdims=True)
-        p_ref[h] = p
-        local_ref[:, cols] = nn(p.astype(bf16), pair_ref[1, :, cols])
-
-    def wait_log(dz, top):
-        log_z(dz).wait()
-        return jnp.maximum(top, log_zr[dz])
-
-    top = lax.fori_loop(1, half, wait_log, log_zr[0])
-
-    def add_to(dz, total):
-        return total + jnp.exp(log_zr[dz] - top)
-
-    logs = top + jnp.log(lax.fori_loop(0, half, add_to, jnp.zeros_like(top)))
-    logs_ref[...] = logs
-    share = jnp.exp(log_zr[0] - logs).T
-    for h in range(2):
-        recalled_ref[:, head_cols(h)] *= share[:, h : h + 1]
-
-    def merge(dz, carry):
-        share = jnp.exp(log_zr[dz] - logs).T
-        out_z(dz).wait()
-        for h in range(2):
-            recalled_ref[:, head_cols(h)] += share[:, h : h + 1] * out_zr[dz, h].astype(f32)
-        return carry
-
-    lax.fori_loop(1, half, merge, 0)
-    for h in range(2):
-        cols = head_cols(h)
-        gate = gate_ref[h]
-        mixed = gate * recalled_ref[:, cols] + (1.0 - gate) * local_ref[:, cols]
-        mixed_ref[:, cols] = mixed.astype(bf16)
-
-
-def attend(lengths, gate, q, k, v, bias, q_all, tok, rows):
-    parts, count, width = q_all.shape
-    span, half = W + count, parts // 2
-    smem = pl.BlockSpec(memory_space=pltpu.SMEM)
-    vmem = pl.BlockSpec(memory_space=pltpu.VMEM)
-    hbm = pl.BlockSpec(memory_space=pltpu.HBM)
-    dma = pltpu.SemaphoreType.DMA
-    return pl.pallas_call(
-        functools.partial(attend_kernel, parts=parts, scale=128**-0.5),
-        out_shape=(
-            jax.ShapeDtypeStruct((count, width), bf16),
-            jax.ShapeDtypeStruct((count, width), f32),
-            jax.ShapeDtypeStruct((count, width), f32),
-            jax.ShapeDtypeStruct((8, count), f32),
-            jax.ShapeDtypeStruct((2, count, span), f32),
-            jax.ShapeDtypeStruct((2, span, width), bf16),
-        ),
-        in_specs=[smem, smem] + [vmem] * 5 + [hbm] * 2,
-        out_specs=(vmem,) * 6,
-        scratch_shapes=[pltpu.VMEM((half, 2, count, 128), bf16)] * 4
-        + [pltpu.VMEM((half, 8, count), f32)] * 4
-        + Held.scratch((q_all, rows), parts)
-        + [dma((half,))] * 8
-        + [dma((3,))] * 2,
-        compiler_params=pltpu.CompilerParams(
-            vmem_limit_bytes=58 * MIB, collective_id=1, has_side_effects=True
-        ),
-        cost_estimate=pl.CostEstimate(
-            flops=3 * 10**9, bytes_accessed=100 * MIB, transcendentals=5 * 10**6
-        ),
-        name="attend",
-    )(lengths, gate, q, k, v, bias, tok, q_all, rows)
 
 
 class ScatterSum:
@@ -782,74 +507,6 @@
         dma = pltpu.SemaphoreType.DMA
         count = len(shapes)
         return slots, [dma((count, 2, quarter))] * 2 + [dma((count, quarter))] * 4
-
-
-def close_attn_kernel(*refs, names, parts):
-    r = types.SimpleNamespace(**dict(zip(names, refs, strict=True)))
-    greet(seq=parts, head=4)
-    sums = HeadSum(
-        r.sum, (r.a, r.b, r.c), (r.ss_a, r.rs_a, r.ss_b, r.rs_b), r.full, (r.ss_full, r.rs_full)
-    )
-    sums.start()
-    copies = []
-    if hasattr(r, "cot_other"):
-        crossed = (
-            ("cot", "z", r.cot, r.cot_other),
-            ("normed", "x", r.normed, r.normed_other),
-        )
-        for name, first, left, other in crossed:
-            joined = JoinedSum([(left, other, left, left)], [None] * 4, parts, first)
-            sems = getattr(r, f"{name}_ss"), getattr(r, f"{name}_rs")
-            copies += joined.cross_blocks(0, sems)
-        sems = (r.mixed_ss, r.mixed_rs)
-        joined = JoinedSum([(r.normed, r.normed, r.mixed, r.mixed_other)], [None] * 4, parts, "x")
-        copies += joined.cross(0, sems)
-        for copy in copies:
-            copy.start()
-    sums.relay()
-    branch = sums.total()
-    middle = r.inputs[sums.mine, :].astype(f32) + branch
-    hat = middle * lax.rsqrt(row_mean(middle * middle) + eps)
-    sums.spread(hat * r.gain[...])
-    r.middle[...] = middle
-    r.line[...] = col_sum(branch * branch)
-    sums.forward()
-    sums.settle()
-    for copy in copies:
-        copy.wait()
-
-
-def close_attn(inputs, parts):
-    count, width = inputs["sum"].shape
-    vmem = pl.BlockSpec(memory_space=pltpu.VMEM)
-    dma = pltpu.SemaphoreType.DMA
-    outputs = dict(
-        full=jax.ShapeDtypeStruct((count, width), bf16),
-        middle=jax.ShapeDtypeStruct((count // 4, width), f32),
-        line=jax.ShapeDtypeStruct((1, width), f32),
-    )
-    scratch = dict(zip("abc", HeadSum.scratch(count, width), strict=True))
-    scratch |= dict(zip(("ss_a", "rs_a", "ss_b", "rs_b"), HeadSum.sems(), strict=True))
-    scratch |= dict(zip(("ss_full", "rs_full"), HeadSum.full_scratch(), strict=True))
-    if width // parts % 128 == 0:
-        for name in ("cot", "normed"):
-            outputs[f"{name}_other"] = jax.ShapeDtypeStruct((count, width // 2), bf16)
-            scratch |= {f"{name}_{end}": dma((parts // 2,)) for end in ("ss", "rs")}
-        outputs["mixed_other"] = jax.ShapeDtypeStruct(inputs["mixed"].shape, bf16)
-        scratch |= {f"mixed_{end}": dma((1,)) for end in ("ss", "rs")}
-    found = pl.pallas_call(
-        functools.partial(close_attn_kernel, names=(*inputs, *outputs, *scratch), parts=parts),
-        out_shape=tuple(outputs.values()),
-        in_specs=[vmem] * len(inputs),
-        out_specs=(vmem,) * len(outputs),
-        scratch_shapes=list(scratch.values()),
-        compiler_params=pltpu.CompilerParams(
-            vmem_limit_bytes=16 * MIB, collective_id=3, has_side_effects=True
-        ),
-        cost_estimate=pl.CostEstimate(flops=10**6, bytes_accessed=30 * MIB, transcendentals=0),
-        name="close_attn",
-    )(*inputs.values())
-    return dict(zip(outputs, found, strict=True))
 
 
 def row_mean(x):
@@ -1038,10 +695,10 @@
         return {f"{name}_{part}": spec for part, spec in found.items()}
 
 
-def back_kernel(*refs, names, parts, peers, scale):
+def layer_kernel(*refs, names, parts, peers, scale):
     r = types.SimpleNamespace(**dict(zip(names, refs, strict=True)))
     count, width = r.q.shape
-    span, model = r.pair.shape[1], r.cot.shape[1]
+    span, model = r.pair.shape[1], r.inputs.shape[1]
     per = r.tok.shape[2]
     half = parts // 2
     me = lax.axis_index("seq")
@@ -1051,21 +708,39 @@
     def at(o, c):
         return 2 * o + (x if c == 0 else 1 - x)
 
+    def reader(c, dz):
+        return at(lax.rem(z + half - dz, half), c)
+
     held = Held(((r.q_all_hbm, r.q_all, r.q_sem), (r.rows_hbm, r.rows, r.rows_sem)), parts)
     held.ahead()
-    greet(seq=parts, head=peers)
-
-    def head_sum(name, source, full):
+
+    def fetch(i):
+        name = FETCHED[i]
+        return pltpu.make_async_copy(
+            getattr(r, name + "_hbm"), getattr(r, name), r.fetch_sem.at[i]
+        )
+
+    def fetch_late(i):
+        place = r.w_up.at[:, pl.ds(i * width, width)]
+        return pltpu.make_async_copy(
+            getattr(r, LATE[i] + "_hbm"), place, r.fetch_sem.at[len(FETCHED) + i]
+        )
+
+    for i in range(len(FETCHED)):
+        fetch(i).start()
+
+    def head_sum(name, slots, source, full):
         return HeadSum(
             source,
-            [getattr(r, f"{name}_{i}") for i in range(3)],
+            [getattr(r, f"{slots}_{i}") for i in range(3)],
             [getattr(r, f"{name}_sem_{i}") for i in range(4)],
             full,
             [getattr(r, f"{name}_full_{i}") for i in range(2)],
         )
 
-    sums = head_sum("sum", r.sum, r.branch)
-    feeds = head_sum("feed", r.feed_in, r.layer)
+    sums = head_sum("sum", "turn", r.partial, r.branch)
+    feeds = head_sum("feed", "feed", r.feed_in, r.layer)
+    attn = head_sum("attn", "turn", r.partial, r.normed_two)
     cot_other = getattr(r, "cot_other", None)
     normed_other = getattr(r, "normed_other", None)
     mixed_other = getattr(r, "mixed_other", None)
@@ -1074,16 +749,254 @@
     p_o = Product(r, "o", r.branch, r.mixed, parts, "x", right_other=mixed_other)
     p_kv = Product(r, "kv", r.normed, r.d_kv, parts, "x", left_other=normed_other)
     p_q = Product(r, "q", r.normed, r.d_q, parts, "x", left_other=normed_other)
-
-    sums.start()
-    p_down.begin()
-    p_up.begin_left()
-    p_up.begin()
-    feeds.start()
-    middle = r.middle[...]
+    ids = lax.broadcasted_iota(jnp.int32, (count, per), 0)
+
+    own_pair = [
+        pltpu.make_async_copy(source, r.pair.at[i, pl.ds(W, count)], r.own_sem.at[i])
+        for i, source in enumerate((r.k_hbm, r.v_hbm))
+    ]
+    for copy in own_pair:
+        copy.start()
+    @pl.when(z == 0)
+    def _():
+        r.pair[:, :count] = jnp.zeros_like(r.pair[:, :count])
+
+    @pl.when(me == 0)
+    def _():
+        r.pair[:, count:W] = jnp.zeros_like(r.pair[:, count:W])
+
+
+    for copy in own_pair:
+        copy.wait()
+    greet(seq=parts, head=peers)
+
+    def pair_rows(first):
+        return r.pair.at[:, pl.ds(first, count)]
+
+    def hand_on(i, source, target, peer):
+        return send(
+            pair_rows(source), pair_rows(target), r.next_ss.at[i], r.next_rs.at[i], "seq", peer
+        )
+
+    next_one = hand_on(0, W, count, partner)
+    next_two = hand_on(1, W, 0, me + 2)
+    passed_on = hand_on(2, 0, count, partner)
+
+    @pl.when(z < half - 1)
+    def _():
+        next_two.start()
+
+    @pl.when(x == 0)
+    def _():
+        next_one.start()
+
+    def recall_part(j):
+        q_at, rows_at = held.get(j)
+        outs, logs = [], []
+        for h in range(2):
+            cols = head_cols(h)
+            keep = r.tok[j, h : h + 1, :] == ids
+            s = jnp.where(keep, nt(q_at[:, cols], rows_at[h, :, 0:128]), NEG)
+            top = jnp.max(s, axis=1, keepdims=True)
+            p = jnp.where(keep, jnp.exp((s - top) * scale), 0.0)
+            total = jnp.sum(p, axis=1, keepdims=True)
+            some = total > 0.0
+            safe = jnp.where(some, total, 1.0)
+            outs.append(nn(p.astype(bf16), rows_at[h, :, 128:256]) / safe)
+            logs.append(jnp.where(some, top * scale + jnp.log(safe), NEG))
+        return outs, logs
+
+    def out_x(dz):
+        return (
+            send(r.log_xs.at[dz], r.log_xr.at[dz], r.lx_ss.at[dz], r.lx_rs.at[dz], "seq", partner),
+            send(r.dq_xs.at[dz], r.dq_xr.at[dz], r.ox_ss.at[dz], r.ox_rs.at[dz], "seq", partner),
+        )
+
+    def log_z(dz):
+        return send(
+            r.log_zs.at[dz], r.log_zr.at[dz], r.lz_ss.at[dz], r.lz_rs.at[dz], "seq", reader(0, dz)
+        )
+
+    def out_z(dz):
+        return send(
+            r.dq_zs.at[dz], r.dq_zr.at[dz], r.oz_ss.at[dz], r.oz_rs.at[dz], "seq", reader(0, dz)
+        )
+
+    def lend(dz):
+        outs, logs = recall_part(reader(1, dz))
+        for h in range(2):
+            r.dq_xs[dz, h] = outs[h].astype(bf16)
+        r.log_xs[dz] = row_form(logs, count).T[0:8]
+        for copy in out_x(dz):
+            copy.start()
+
+    def unite(outs, logs, dz):
+        for copy in out_x(dz):
+            copy.wait()
+        other = r.log_xr[dz].T
+        joined = []
+        for h in range(2):
+            theirs = other[:, h : h + 1]
+            top = jnp.maximum(logs[h], theirs)
+            a, b = jnp.exp(logs[h] - top), jnp.exp(theirs - top)
+            total = a + b
+            outs[h] = outs[h] * (a / total) + r.dq_xr[dz, h].astype(f32) * (b / total)
+            joined.append(top + jnp.log(total))
+        return outs, joined
+
+    def lend_step(dz, carry):
+        lend(dz)
+        return carry
+
+    lax.fori_loop(1, half, lend_step, 0)
+    lend(0)
+
+    @pl.when(z > 0)
+    def _():
+        hand_on(1, W, 0, partner).wait_recv()
+
+        @pl.when(x == 1)
+        def _():
+            passed_on.start()
+
+    def keep_step(dz, carry):
+        outs, logs = recall_part(reader(0, dz))
+        outs, logs = unite(outs, logs, dz)
+        for h in range(2):
+            r.dq_zs[dz, h] = outs[h].astype(bf16)
+        r.log_zs[dz] = row_form(logs, count).T[0:8]
+        log_z(dz).start()
+        out_z(dz).start()
+        return carry
+
+    lax.fori_loop(1, half, keep_step, 0)
+    outs, logs = recall_part(me)
+    outs, logs = unite(outs, logs, 0)
+    r.log_zr[0] = row_form(logs, count).T[0:8]
+    for h in range(2):
+        r.recalled[:, head_cols(h)] = outs[h]
+
+    @pl.when(x == 0)
+    def _():
+        next_one.wait_send()
+
+        @pl.when(z > 0)
+        def _():
+            passed_on.wait_recv()
+
+    @pl.when(x == 1)
+    def _():
+        next_one.wait_recv()
+
+        @pl.when(z > 0)
+        def _():
+            passed_on.wait_send()
+
+    @pl.when(z < half - 1)
+    def _():
+        next_two.wait_send()
+
+    first = me * count
+    start = doc_starts(r.lengths, first, count)
+    key_place = first - W + lax.broadcasted_iota(jnp.int32, (count, span), 1)
+    seen = key_place >= start
+    for h in range(2):
+        cols = head_cols(h)
+        bias = pltpu.roll(
+            jnp.broadcast_to(r.bias[h : h + 1, :], (count, span)), 0, 1, stride=1, stride_axis=0
+        )
+        s = nt(r.q[:, cols], r.pair[0, :, cols]) * scale + bias
+        s = jnp.where(seen, s, NEG)
+        raised = jnp.exp(s - jnp.max(s, axis=1, keepdims=True))
+        p = raised / jnp.sum(raised, axis=1, keepdims=True)
+        r.p[h] = p
+        r.local[:, cols] = nn(p.astype(bf16), r.pair[1, :, cols])
+
+    def wait_log(dz, top):
+        log_z(dz).wait()
+        return jnp.maximum(top, r.log_zr[dz])
+
+    top = lax.fori_loop(1, half, wait_log, r.log_zr[0])
+
+    def add_to(dz, total):
+        return total + jnp.exp(r.log_zr[dz] - top)
+
+    logs = top + jnp.log(lax.fori_loop(0, half, add_to, jnp.zeros_like(top)))
+    r.logs[...] = logs
+    share = jnp.exp(r.log_zr[0] - logs).T
+    for h in range(2):
+        r.recalled[:, head_cols(h)] *= share[:, h : h + 1]
+
+    def gather_out(dz, carry):
+        share = jnp.exp(r.log_zr[dz] - logs).T
+        out_z(dz).wait()
+        for h in range(2):
+            r.recalled[:, head_cols(h)] += share[:, h : h + 1] * r.dq_zr[dz, h].astype(f32)
+        return carry
+
+    lax.fori_loop(1, half, gather_out, 0)
+    for h in range(2):
+        cols = head_cols(h)
+        gate = r.gate[h]
+        mixed = gate * r.recalled[:, cols] + (1.0 - gate) * r.local[:, cols]
+        r.mixed[:, cols] = mixed.astype(bf16)
+
+
+    for i in range(len(FETCHED)):
+        fetch(i).wait()
+    for b in range(model // 256):
+        block = slice(256 * b, 256 * b + 256)
+        r.partial[:, block] = nn(r.mixed[...], r.w_o[:, block]).astype(bf16)
+    attn.start()
+    crossing = []
+    if cot_other is not None:
+        for name, first, left, other in (("cot", "z", r.cot, cot_other), ("normed", "x", r.normed, normed_other)):
+            joined = JoinedSum([(left, other, left, left)], [None] * 4, parts, first)
+            sems = getattr(r, f"{name}_ss"), getattr(r, f"{name}_rs")
+            crossing += joined.cross_blocks(0, sems)
+        joined = JoinedSum([(r.normed, r.normed, r.mixed, mixed_other)], [None] * 4, parts, "x")
+        crossing += joined.cross(0, (r.mixed_ss, r.mixed_rs))
+        for copy in crossing:
+            copy.start()
+    attn.relay()
+    branch = attn.total()
+    middle = r.inputs[attn.mine, :].astype(f32) + branch
+    r.middle[...] = middle
     row_scale = lax.rsqrt(row_mean(middle * middle) + eps)
     hat = middle * row_scale
+    attn.spread(hat * r.gain_two[...])
+    r.small_send[17:18] = fold_sum(col_sum(branch * branch))
+    attn.forward()
+    attn.settle()
+
+    p_up.begin_left()
+    for b in range(r.hidden.shape[1] // 256):
+        block = slice(256 * b, 256 * b + 256)
+        up = nn(r.normed_two[...], r.w_up[:, block])
+        square = up * up
+        bent = jnp.tanh(GELU * (up + 0.044715 * up * square))
+        rise = 0.5 * (1.0 + bent)
+        r.hidden[:, block] = (up * rise).astype(bf16)
+        steep = (0.5 * GELU) * up * (1.0 - bent * bent) * (1.0 + (3 * 0.044715) * square)
+        r.slope[:, block] = rise + steep
+    p_down.begin()
+    for b in range(r.hidden.shape[1] // 256):
+        block = slice(256 * b, 256 * b + 256)
+        back = nt(r.cot[...], r.w_down[block, :])
+        r.grad_upward[:, block] = (r.slope[:, block] * back).astype(bf16)
+    p_up.begin()
+    for b in range(model // 256):
+        block = slice(256 * b, 256 * b + 256)
+        r.partial[:, block] = nt(r.grad_upward[...], r.w_up[block, :]).astype(bf16)
+
+    sums.start()
+    for i in range(len(LATE)):
+        fetch_late(i).start()
     sums.relay()
+    for b in range(model // 256):
+        block = slice(256 * b, 256 * b + 256)
+        r.feed_in[:, block] = nn(r.hidden[...], r.w_down[:, block]).astype(bf16)
+    feeds.start()
     grad_normed = sums.total()
     scaled = grad_normed * r.gain_two[...]
     grad_middle = r.cot[sums.mine, :].astype(f32) + row_scale * (
@@ -1147,10 +1060,11 @@
         start(down(z))
 
     start(across(z))
+    for copy in crossing:
+        copy.wait_recv()
     p_down.ready()
     p_down.pair(True)
 
-    dq = []
     for h in range(2):
         cols = head_cols(h)
         rest = 1.0 - r.gate[h]
@@ -1181,13 +1095,10 @@
         r.pair_send.at[:, pl.ds(count, count)], r.halo_x, r.halo_ss.at[0], r.halo_rs.at[0], "seq", partner
     )
     halo_z = send(r.halo_send, r.halo_z, r.halo_ss.at[1], r.halo_rs.at[1], "seq", me - 2)
-    halo_x.start()
-
-    ids = lax.broadcasted_iota(jnp.int32, (count, per), 0)
 
     def owner_part(c, o):
         j = at(o, c)
-        q_at, rows_at = held.get(j)
+        q_at, rows_at = held.get(j, again=True)
         stats = r.st_all[c, o].T
         found = []
         for h in range(2):
@@ -1204,17 +1115,6 @@
     for h in range(2):
         r.dq_sum[:, head_cols(h)] += own[h]
 
-    halo_x.wait()
-    passing = x.astype(f32)
-    r.halo_send[...] = (
-        r.pair_send[:, :count].astype(f32) + r.halo_x[...].astype(f32) * passing
-    ).astype(bf16)
-    r.pair_sum[...] += r.halo_x[...].astype(f32) * (1.0 - passing)
-
-    @pl.when(z > 0)
-    def _():
-        halo_z.start()
-
     def give_x(o):
         return send(r.dq_xs.at[o], r.dq_xr.at[o], r.dx_ss.at[o], r.dx_rs.at[o], "seq", partner)
 
@@ -1293,22 +1193,13 @@
     layer = r.middle[...] + feed_sum
     feeds.spread(layer)
     r.small_send[16:17] = fold_sum(col_sum(layer * layer))
-    r.small_send[17:18] = fold_sum(r.attn_line[...])
     r.small_send[18:19] = fold_sum(col_sum(feed_sum * feed_sum))
     near(lambda o, below: neighbour(o))
+    halo_x.start()
     p_down.pair(False)
     p_o.begin_left()
     p_o.begin()
     p_up.pair(False)
-
-    @pl.when(z > 0)
-    def _():
-        halo_z.wait_send()
-
-    @pl.when(z < half - 1)
-    def _():
-        send(r.halo_send, r.halo_z, r.halo_ss.at[1], r.halo_rs.at[1], "seq", partner).wait_recv()
-        r.pair_sum[...] += r.halo_z[...].astype(f32)
 
     def join(o, below):
         give_x(o).wait()
@@ -1318,12 +1209,18 @@
         give_z(o).start()
 
     near(join)
-    r.d_kv[:, :width] = r.pair_sum[0].astype(bf16)
-    r.d_kv[:, width:] = r.pair_sum[1].astype(bf16)
-    p_kv.begin()
+    halo_x.wait()
+    passing = x.astype(f32)
+    r.halo_send[...] = (
+        r.pair_send[:, :count].astype(f32) + r.halo_x[...].astype(f32) * passing
+    ).astype(bf16)
+    r.pair_sum[...] += r.halo_x[...].astype(f32) * (1.0 - passing)
+
+    @pl.when(z > 0)
+    def _():
+        halo_z.start()
+
     feeds.forward()
-    p_down.far()
-    p_up.far()
     give_x(z).wait()
     for h in range(2):
         r.dq_sum[:, head_cols(h)] += r.dq_xr[z, h].astype(f32)
@@ -1337,14 +1234,29 @@
 
     r.d_q[...] = r.dq_sum[...].astype(bf16)
     p_q.begin()
+    p_down.far()
+    p_up.far()
+    @pl.when(z > 0)
+    def _():
+        halo_z.wait_send()
+
+    @pl.when(z < half - 1)
+    def _():
+        send(r.halo_send, r.halo_z, r.halo_ss.at[1], r.halo_rs.at[1], "seq", partner).wait_recv()
+        r.pair_sum[...] += r.halo_z[...].astype(f32)
+
+    r.d_kv[:, :width] = r.pair_sum[0].astype(bf16)
+    r.d_kv[:, width:] = r.pair_sum[1].astype(bf16)
+    p_kv.begin()
+    for i in range(len(LATE)):
+        fetch_late(i).wait()
     for b in range(model // 256):
         block = slice(256 * b, 256 * b + 256)
-        r.back[:, block] = (
-            nt(r.d_q[...], r.w_q[block, :])
-            + nt(r.d_kv[:, :width], r.w_k[block, :])
-            + nt(r.d_kv[:, width:], r.w_v[block, :])
+        r.partial[:, block] = (
+            nt(r.d_q[...], r.w_up[block, :width])
+            + nt(r.d_kv[...], r.w_up[block, width : 3 * width])
         ).astype(bf16)
-    backs = head_sum("back", r.back, r.input_grad)
+    backs = head_sum("back", "turn", r.partial, r.input_grad)
     backs.start()
     backs.relay()
     p_o.ready()
@@ -1439,17 +1351,24 @@
                 sent(down(o))
 
     near(drain)
-
-
-def back(inputs, parts, peers):
+    for copy in crossing:
+        copy.wait_send()
+
+
+FETCHED = ("cot", "w_o", "w_up", "w_down")
+LATE = ("w_q", "w_k", "w_v")
+GELU = math.sqrt(2 / math.pi)
+
+
+def layer(inputs, parts, peers):
     count, width = inputs["q"].shape
-    model, span = inputs["cot"].shape[1], W + count
+    model, span = inputs["inputs"].shape[1], W + count
     half, own = parts // 2, model // parts
     smem = pl.BlockSpec(memory_space=pltpu.SMEM)
     vmem = pl.BlockSpec(memory_space=pltpu.VMEM)
     hbm = pl.BlockSpec(memory_space=pltpu.HBM)
     dma = pltpu.SemaphoreType.DMA
-    wide = inputs["hidden"].shape[1]
+    wide = inputs["w_up_hbm"].shape[1]
     outputs = dict(
         input_grad=((count, model), bf16),
         layer=((count, model), bf16),
@@ -1464,9 +1383,26 @@
     outputs = {name: jax.ShapeDtypeStruct(*spec) for name, spec in outputs.items()}
     held = Held.scratch((inputs["q_all_hbm"], inputs["rows_hbm"]), parts)
     scratch = dict(zip(("q_all", "rows", "q_sem", "rows_sem"), held, strict=True))
+    scratch |= {name: pltpu.VMEM(inputs[name + "_hbm"].shape, bf16) for name in FETCHED}
     for name, spec in dict(
+        recalled=((count, width), f32),
+        local=((count, width), f32),
+        mixed=((count, width), bf16),
+        logs=((8, count), f32),
+        p=((2, count, span), f32),
+        pair=((2, span, width), bf16),
+        log_xs=((half, 8, count), f32),
+        log_xr=((half, 8, count), f32),
+        log_zs=((half, 8, count), f32),
+        log_zr=((half, 8, count), f32),
+        normed_two=((count, model), bf16),
+        middle=((count // peers, model), f32),
+        hidden=((count, wide), bf16),
+        slope=((count, wide), f32),
+        grad_upward=((count, wide), bf16),
+        partial=((count, model), bf16),
+        feed_in=((count, model), bf16),
         branch=((count, model), bf16),
-        back=((count, model), bf16),
         grad_middle=((count // peers, model), f32),
         g_all=((2, half, count, width), bf16),
         st_all=((2, half, 8, count), f32),
@@ -1491,6 +1427,18 @@
     ).items():
         scratch[name] = pltpu.VMEM(*spec)
     for name, shape in dict(
+        fetch_sem=(len(FETCHED) + len(LATE),),
+        own_sem=(2,),
+        next_ss=(3,),
+        next_rs=(3,),
+        ox_ss=(half,),
+        ox_rs=(half,),
+        oz_ss=(half,),
+        oz_rs=(half,),
+        lx_ss=(half,),
+        lx_rs=(half,),
+        lz_ss=(half,),
+        lz_rs=(half,),
         st_ss=(3, half),
         st_rs=(2, half),
         g_ss=(3, half),
@@ -1507,10 +1455,17 @@
         sq_rs=(parts,),
     ).items():
         scratch[name] = dma(shape)
-    for name in ("sum", "feed", "back"):
+    for name in ("turn", "feed"):
         scratch |= {f"{name}_{i}": s for i, s in enumerate(HeadSum.scratch(count, model))}
+    for name in ("attn", "sum", "feed", "back"):
         scratch |= {f"{name}_sem_{i}": s for i, s in enumerate(HeadSum.sems())}
         scratch |= {f"{name}_full_{i}": s for i, s in enumerate(HeadSum.full_scratch())}
+    if own % 128 == 0:
+        for name in ("cot", "normed"):
+            scratch[f"{name}_other"] = pltpu.VMEM((count, model // 2), bf16)
+            scratch |= {f"{name}_{end}": dma((half,)) for end in ("ss", "rs")}
+        scratch["mixed_other"] = pltpu.VMEM((count, width), bf16)
+        scratch |= {f"mixed_{end}": dma((1,)) for end in ("ss", "rs")}
     for name, columns, left, right in (
         ("down", wide, False, True),
         ("up", wide, True, True),
@@ -1519,10 +1474,11 @@
         ("q", width, False, True),
     ):
         scratch |= Product.scratch(name, count, model, columns, parts, left, right)
-    spaces = dict(gate=smem, q_all_hbm=hbm, rows_hbm=hbm)
+    spaces = dict(gate=smem, lengths=smem)
+    spaces |= {name: hbm for name in inputs if name.endswith("_hbm")}
     found = pl.pallas_call(
         functools.partial(
-            back_kernel,
+            layer_kernel,
             names=(*inputs, *outputs, *scratch),
             parts=parts,
             peers=peers,
@@ -1533,14 +1489,79 @@
         out_specs=(vmem,) * len(outputs),
         scratch_shapes=list(scratch.values()),
         compiler_params=pltpu.CompilerParams(
-            vmem_limit_bytes=(40 if parts <= 8 else 62) * MIB, collective_id=2, has_side_effects=True
+            vmem_limit_bytes=(58 if parts <= 8 else 63) * MIB, collective_id=2, has_side_effects=True
         ),
         cost_estimate=pl.CostEstimate(
             flops=4 * 10**9, bytes_accessed=150 * MIB, transcendentals=5 * 10**6
         ),
-        name="back",
+        name="layer",
     )(*inputs.values())
     return dict(zip(outputs, found, strict=True))
+
+
+def hand_out_kernel(*refs, copied, entries):
+    count = len(copied)
+    sources, (input_grad, small, gate, hot), outs = refs[:count], refs[count : count + 4], refs[count + 4 :]
+    grad_out, gains_out, position_out, gate_out, rms_out = outs[count : count + 5]
+    for source, out in zip(sources, outs):
+        out[...] = source[...]
+    grad_out[...] = input_grad[...].astype(f32)
+    me = lax.axis_index("seq")
+    if gains_out.shape[1] == 128:
+        gains_out[0:1, :] = small[pl.ds(me, 1), :]
+        gains_out[1:2, :] = small[pl.ds(me + 8, 1), :]
+    else:
+        gains_out[...] = small[0:16, :]
+    lines = hot.shape[0] // 128
+    for h in range(2):
+        found = jnp.zeros((1, hot.shape[1]), f32)
+        for i in range(lines):
+            line = small[24 + h * lines + i : 25 + h * lines + i, :]
+            found = found + lax.dot_general(
+                line,
+                hot[128 * i : 128 * i + 128, :],
+                (((1,), (0,)), ((), ())),
+                precision=highest,
+                preferred_element_type=f32,
+            )
+        position_out[h : h + 1, :] = found
+    sums = jnp.sum(small[16:24, :], axis=1, keepdims=True)
+    lane = lax.broadcasted_iota(jnp.int32, (1, 2), 1)
+    steep = jnp.where(lane == 0, gate[0] * (1.0 - gate[0]), gate[1] * (1.0 - gate[1]))
+    gate_out[...] = jnp.where(lane == 0, sums[3:4], sums[4:5]) * steep
+    lane = lax.broadcasted_iota(jnp.int32, (1, 3), 1)
+    squares = jnp.where(lane == 0, sums[0:1], jnp.where(lane == 1, sums[1:2], sums[2:3]))
+    rms_out[...] = jnp.sqrt(squares / entries)
+
+
+def hand_out(done, gate, hot, entries, parts):
+    copied = ("layer", "q_out", "k_out", "v_out", "o_out", "up_out", "down_out")
+    smem = pl.BlockSpec(memory_space=pltpu.SMEM)
+    vmem = pl.BlockSpec(memory_space=pltpu.VMEM)
+    model = done["input_grad"].shape[1]
+    own = model // parts
+    shapes = [jax.ShapeDtypeStruct(done[name].shape, done[name].dtype) for name in copied]
+    shapes += [
+        jax.ShapeDtypeStruct(shape, f32)
+        for shape in (
+            done["input_grad"].shape,
+            (2, 128) if own == 128 else (16, 128),
+            (2, hot.shape[1]),
+            (1, 2),
+            (1, 3),
+        )
+    ]
+    found = pl.pallas_call(
+        functools.partial(hand_out_kernel, copied=copied, entries=entries),
+        out_shape=tuple(shapes),
+        in_specs=[vmem] * len(copied) + [vmem, vmem, smem, vmem],
+        out_specs=(vmem,) * (len(copied) + 5),
+        compiler_params=pltpu.CompilerParams(vmem_limit_bytes=62 * MIB),
+        name="hand_out",
+    )(*(done[name] for name in copied), done["input_grad"], done["small"], gate, hot)
+    named = dict(zip(copied, found))
+    named |= dict(zip(("input_grad", "gains", "position", "gate", "rms"), found[len(copied) :]))
+    return named
 
 
 def norm_stats(values):
@@ -1582,7 +1603,6 @@
 
     x, cot = inputs[0], cotangent[0]
     peers = lax.axis_size("head")
-    gain_one, gain_two = first_gain[None], second_gain[None]
     gate_flat = jax.nn.sigmoid(gate_bias)
     hat_one, _ = norm_stats(x.astype(f32))
     normed_one = (hat_one * first_gain).astype(bf16)
@@ -1591,82 +1611,53 @@
     values = nn(normed_one, value_weight).astype(bf16)
     q_all = lax.all_gather(queries, "seq", axis=0)
 
-    mixed, recalled, local_out, logs, window_weights, pair = attend(
-        lengths[0], gate_flat, queries, keys, values, bias_row, q_all, tok, rows
-    )
-
-    closed = close_attn(
+    done = layer(
         dict(
-            sum=nn(mixed, output_weight).astype(bf16),
+            lengths=lengths[0],
+            gate=gate_flat,
+            q=queries,
+            k_hbm=keys,
+            v_hbm=values,
+            bias=bias_row,
+            tok=tok,
             inputs=x,
-            gain=gain_two,
-            cot=cot,
             normed=normed_one,
-            mixed=mixed,
-        ),
-        seq_count,
-    )
-    normed_two, middle, attn_line = closed.pop("full"), closed.pop("middle"), closed.pop("line")
-    others = closed
-    upward = nn(normed_two, up_weight)
-    gelu_value, gelu_back = jax.vjp(jax.nn.gelu, upward)
-    hidden = gelu_value.astype(bf16)
-    grad_upward = gelu_back(nt(cot, down_weight))[0].astype(bf16)
-    done = back(
-        dict(
-            gate=gate_flat,
-            sum=nt(grad_upward, up_weight).astype(bf16),
-            feed_in=nn(hidden, down_weight).astype(bf16),
-            hidden=hidden,
-            grad_upward=grad_upward,
-            normed_two=normed_two,
-            **others,
-            cot=cot,
-            inputs=x,
-            gain_one=gain_one,
-            gain_two=gain_two,
-            middle=middle,
-            attn_line=attn_line,
-            w_o=output_weight,
-            w_q=query_weight,
-            w_k=key_weight,
-            w_v=value_weight,
-            normed=normed_one,
-            mixed=mixed,
-            q=queries,
-            recalled=recalled,
-            local=local_out,
-            logs=logs,
-            p=window_weights,
-            pair=pair,
-            tok=tok,
+            gain_one=first_gain[None],
+            gain_two=second_gain[None],
             q_all_hbm=q_all,
             rows_hbm=rows,
+            cot_hbm=cot,
+            w_o_hbm=output_weight,
+            w_up_hbm=up_weight,
+            w_down_hbm=down_weight,
+            w_q_hbm=query_weight,
+            w_k_hbm=key_weight,
+            w_v_hbm=value_weight,
         ),
         seq_count,
         peers,
     )
-    small = done["small"]
-    entry_count = float(block_len * model_width * seq_count)
+    entries = float(block_len * model_width * seq_count)
+    out = hand_out(done, gate_flat, jnp.asarray(hot.T), entries, seq_count)
     share = model_width // seq_count
-    gains = small[:16].reshape(2, model_width)
-    own_gains = lax.dynamic_slice_in_dim(gains, lax.axis_index("seq") * share, share, 1)
-    position_grad = jnp.dot(small[24:36].reshape(2, -1), hot.T, precision=highest)
-    gate_grad = jnp.sum(small[19:21], axis=1) * gate_flat * (1.0 - gate_flat)
+    gains = out["gains"]
+    if share != 128:
+        start = lax.axis_index("seq") * share
+        gains = lax.dynamic_slice_in_dim(gains.reshape(2, model_width), start, share, 1)
     return (
-        done["layer"][None],
-        done["input_grad"].astype(f32)[None],
-        done["q_out"],
-        done["k_out"],
-        done["v_out"],
-        done["o_out"],
-        done["up_out"],
-        done["down_out"],
-        own_gains[0],
-        own_gains[1],
-        position_grad,
-        gate_grad,
-        jnp.sqrt(jnp.sum(small[16:19], axis=1) / entry_count),
+        out["layer"][None],
+        out["input_grad"][None],
+        out["q_out"],
+        out["k_out"],
+        out["v_out"],
+        out["o_out"],
+        out["up_out"],
+        out["down_out"],
+        gains[0],
+        gains[1],
+        out["position"],
+        out["gate"][0],
+        out["rms"][0],
     )
 
 

time: 254 us -> 234 us (0.921)
  local copies, waits for them, and re-layouts: 15.4 us -> 4.38 us
  matrix products: 12.4 us -> 4.89 us
  other arithmetic: 8.94 us -> 3.92 us
  Pallas kernels: 200 us -> 205 us
    unnamed x77 -> x20, local copies, waits for them, and re-layouts: 12.6 us -> 2.16 us
    pallas_call x3 -> x2, Pallas kernels: 154 us -> 159 us  [the longest x1 155 us: layer(): pl.pallas_call(functools.partial(layer_kernel, names=(*inputs, *outputs,...]
    dot_general x3 -> x0, matrix products: 3.83 us -> none  [the longest x2 1.96 us: nt(): lax.dot_general(a, b, (((1,), (1,)), ((), ())), preferred_element_type=f32)]
    dot_general x6 -> x3, matrix products: 7.79 us -> 4.12 us  [nn(): lax.dot_general(a, b, (((1,), (0,)), ((), ())), preferred_element_type=f32)]
  transfers between devices with their start and end apart: 1 -> 1, of which waited for: 0 -> 0; matrix products, arithmetic and copies ran while one was open for 2% -> 2% of each run, Pallas kernels for 18% -> 19%
where the time goes in v5:
time: 234 us
  Pallas kernels  205 us (88%)
  between operations  15.6 us (7%)
  matrix products  4.89 us (2%)
  local copies, waits for them, and re-layouts  4.38 us (2%)
  other arithmetic  3.92 us (2%)
    pallas_call x1, Pallas kernels, layer(): pl.pallas_call(functools.partial(layer_kernel, names=(*inputs, *outputs,...  155 us
    pallas_call x1, Pallas kernels, gather_rows(): pl.pallas_call(functools.partial(gather_kernel, unroll=unroll, group=unro...  21.8 us
    pallas_call x1, Pallas kernels, widen(): pl.pallas_call(functools.partial(widen_kernel, chunk=chunk, part=32), out...  14.6 us
    pallas_call x1, Pallas kernels, request(): pl.pallas_call(functools.partial(request_kernel, parts=parts, slots=slots...  8.68 us
  transfers between devices with their start and end apart: 1, of which 0 were waited for; matrix products, arithmetic and copies ran while one was open for 2% of the time, Pallas kernels for 19%

profile of v5, /device:TPU:0, one launch (start us, length us, event | category | flops | bytes accessed | tf_op | source)
XLA Modules:
  0.0 233.5 jit_solution(5441163555674044816)
XLA Ops:
  8.0 0.0 copy-start
  8.0 0.0 sort.9.cloned.1.call-start
  8.1 0.9 fusion.6
  9.0 0.1 copy.31
  9.1 0.8 reshape.46
  9.9 0.0 sort.9.cloned.1.call-update
  9.9 0.0 all-gather.3.cloned.1.call-start
  10.0 1.2 fusion.1
  11.2 1.2 fusion.3.refs_8_
  12.5 0.0 copy-start.3
  12.5 2.2 convolution_convert_fusion.2.refs_2_
  14.7 0.0 all-gather.3.cloned.1.call-update
  14.7 0.0 copy-start.8
  14.7 0.0 copy-start.6
  14.7 0.0 copy-start.7
  14.8 0.0 copy-start.5
  14.8 0.0 copy-start.4
  14.8 14.6 %widen.1.wide_hbm = f32[2,16384,128]{2,1,0:T(8,128)} custom-call(bf16[8192,2,256]{2,1,0:T(2,128)(2,1)} %table_hbm.1), custom_call_target="tpu_custom_call" | custom-call | bytes 41943040 | tf_op jit(solution)/shard_map/widen/pallas_call | solution.py:101
  29.4 0.5 add_divide_fusion.refs_1_.refs_9_
  29.9 0.8 fusion.refs_5_
  30.7 1.0 convolution_convert_fusion.refs_4_
  31.7 1.0 convolution_convert_fusion.1.refs_3_
  32.6 0.8 copy-done.2
  33.5 8.7 %request.1 = (s32[8,2,1024]{2,1,0:T(2,128)S(1)}, s32[8,2,1024]{2,1,0:T(2,128)S(1)}) custom-call(s32[2,8192]{1,0:T(2,128)S(1)} %copy-done.2), custom_call_target="tpu_custom_call" | custom-call | tf_op jit(solution)/shard_map/request/pallas_call | solution.py:283
  42.2 0.0 copy-start.1
  42.2 0.6 copy-done.1
  42.8 0.6 copy.32
  43.4 21.8 %gather_rows.1.refs_12_ = bf16[8,2,1024,256]{3,2,1,0:T(8,128)(2,1)} custom-call(s32[16384]{0:T(1024)} %bitcast.54, f32[2,16384,128]{2,1,0:T(8,128)} %widen.1.wide_hbm), custom_call_target="tpu_custom_call" | custom-call | bytes 104857600 | tf_op jit(solution)/shard_map/gather_rows/pallas_call | solution.py:172
  65.3 0.0 all-gather.3.cloned.1.call-done
  65.3 155.3 %layer.1 = (bf16[256,1024]{1,0:T(8,128)(2,1)}, bf16[256,1024]{1,0:T(8,128)(2,1)}, f32[128,256]{1,0:T(8,128)}, f32[128,256]{1,0:T(8,128)}, f32[128,256]{1,0:T(8,1...) custom-call(s32[4]{0:T(128)} %bitcast.57, ...), custom_call_target="tpu_custom_call" | custom-call | flops 4000000000 | bytes 157286400 | tf_op jit(solution)/shard_map/layer/pallas_call | solution.py:1479
  220.6 4.2 %hand_out.1 = (bf16[256,1024]{1,0:T(8,128)(2,1)}, f32[128,256]{1,0:T(8,128)}, f32[128,256]{1,0:T(8,128)}, f32[128,256]{1,0:T(8,128)}, f32[256,128]{1,0:T(8,128)}...) custom-call(bf16[256,1024]{1,0:T(8,128)(2,1)} %get-tuple-element.38., ...), custom_call_target="tpu_custom_call" | custom-call | tf_op jit(solution)/shard_map/hand_out/pallas_call | solution.py:1554
  224.8 1.3 slice_bitcast_fusion
  (11 shorter events, 0.0 us)
Async XLA Ops:
  8.0 21.9 %copy-start = (f32[2,32]{1,0:T(2,128)S(1)}, f32[2,32]{1,0:T(2,128)}, u32[]{:S(2)}) copy-start(f32[2,32]{1,0:T(2,128)} %param.28) | copy-start | bytes 772
  8.0 24.6 %sort.9.cloned.1.call-start = ((), (), s32[]{:S(2)}) async-start(), calls=%async_computation.1 | async-start | bytes 196640 | tf_op jit(solution)/shard_map/sort | solution.py:1597
  9.9 55.4 %all-gather.3.cloned.1.call-start = ((), (), s32[]{:S(2)}) async-start(), calls=%async_computation | async-start | bytes 1179648 | tf_op jit(solution)/shard_map/all_gather | solution.py:1612
  12.5 19.2 %copy-start.3 = (bf16[256,1024]{1,0:T(8,128)(2,1)}, bf16[256,1024]{1,0:T(8,128)(2,1)S(1)}, u32[]{:S(2)}) copy-start(bf16[256,1024]{1,0:T(8,128)(2,1)S(1)} %fusion.3.refs_8_) | copy-start | bytes 1572868
  14.7 14.7 %copy-start.8 = (f32[2]{0:T(128)S(1)}, f32[2]{0:T(128)}, u32[]{:S(2)}) copy-start(f32[2]{0:T(128)} %param.29) | copy-start | bytes 28
  14.7 15.2 %copy-start.6 = (f32[32,768]{1,0:T(8,128)S(1)}, f32[32,768]{1,0:T(8,128)}, u32[]{:S(2)}) copy-start(f32[32,768]{1,0:T(8,128)} %constant.46.clone) | copy-start | bytes 294916
  14.7 15.2 %copy-start.7 = (f32[768]{0:T(1024)S(1)}, f32[768]{0:T(1024)}, u32[]{:S(2)}) copy-start(f32[768]{0:T(1024)} %constant.53) | copy-start | bytes 9220
  14.8 15.9 %copy-start.5 = (bf16[1024,256]{1,0:T(8,128)(2,1)S(1)}, bf16[1024,256]{1,0:T(8,128)(2,1)}, u32[]{:S(2)}) copy-start(bf16[1024,256]{1,0:T(8,128)(2,1)} %refs_19_.1) | copy-start | bytes 1572868
  14.8 16.9 %copy-start.4 = (bf16[1024,256]{1,0:T(8,128)(2,1)S(1)}, bf16[1024,256]{1,0:T(8,128)(2,1)}, u32[]{:S(2)}) copy-start(bf16[1024,256]{1,0:T(8,128)(2,1)} %refs_18_.1) | copy-start | bytes 1572868
  32.6 0.8 copy-start.2
  42.2 0.6 copy-start.1
Sparse Core Ops, SparseCore 0:
  11.9 16.9 sort.11.cloned.1.call-done
  (1 shorter events, 0.0 us)
Sparse Core Ops, SparseCore 1:
  14.8 43.1 all-gather.2

commit v6 on v5

--- a/solution.py
+++ b/solution.py
@@ -190,7 +190,7 @@
 MESH = pl.DeviceIdType.MESH
 
 
-def greet(**counts):
+def greet(meanwhile=None, **counts):
     barrier = pltpu.get_barrier_semaphore()
     for axis, count in counts.items():
         me = lax.axis_index(axis)
@@ -201,6 +201,8 @@
             return carry
 
         lax.fori_loop(1, count, call, 0)
+    if meanwhile is not None:
+        meanwhile()
     pl.semaphore_wait(barrier, sum(counts.values()) - len(counts))
 
 
@@ -237,7 +239,24 @@
     return wide
 
 
-def request_kernel(codes_ref, place_ref, tok_ref, got, own_sem, ss, rs, *, parts, slots, tokens):
+def request_kernel(
+    codes_ref,
+    normed_ref,
+    wk_ref,
+    wv_ref,
+    place_ref,
+    tok_ref,
+    k_ref,
+    v_ref,
+    got,
+    own_sem,
+    ss,
+    rs,
+    *,
+    parts,
+    slots,
+    tokens,
+):
     rows = codes_ref.shape[1] // parts
     me = lax.axis_index("seq")
 
@@ -246,7 +265,12 @@
 
     keep = pltpu.make_async_copy(part(me), got.at[0], own_sem)
     keep.start()
-    greet(seq=parts)
+
+    def project():
+        k_ref[...] = nn(normed_ref[...], wk_ref[...]).astype(bf16)
+        v_ref[...] = nn(normed_ref[...], wv_ref[...]).astype(bf16)
+
+    greet(project, seq=parts)
 
     def ask(d):
         peer = lax.rem(me + d, parts)
@@ -275,22 +299,23 @@
     lax.fori_loop(1, parts, arrive, 0)
 
 
-def request(codes, parts, slots, tokens):
+def request(codes, normed, wk, wv, parts, slots, tokens):
     rows = codes.shape[1] // parts
     vmem = pl.BlockSpec(memory_space=pltpu.VMEM)
     dma = pltpu.SemaphoreType.DMA
     shape = (parts, 2, rows)
     return pl.pallas_call(
         functools.partial(request_kernel, parts=parts, slots=slots, tokens=tokens),
-        out_shape=(jax.ShapeDtypeStruct(shape, jnp.int32),) * 2,
-        in_specs=[vmem],
-        out_specs=(vmem,) * 2,
+        out_shape=(jax.ShapeDtypeStruct(shape, jnp.int32),) * 2
+        + (jax.ShapeDtypeStruct((tokens, wk.shape[1]), bf16),) * 2,
+        in_specs=[vmem] * 4,
+        out_specs=(vmem,) * 4,
         scratch_shapes=[pltpu.VMEM(shape, jnp.int32), dma, dma((parts,)), dma((parts,))],
         compiler_params=pltpu.CompilerParams(
-            vmem_limit_bytes=8 * MIB, collective_id=6, has_side_effects=True
+            vmem_limit_bytes=16 * MIB, collective_id=6, has_side_effects=True
         ),
         name="request",
-    )(codes)
+    )(codes, normed, wk, wv)
 
 
 class HeadSum:
@@ -798,12 +823,13 @@
             keep = r.tok[j, h : h + 1, :] == ids
             s = jnp.where(keep, nt(q_at[:, cols], rows_at[h, :, 0:128]), NEG)
             top = jnp.max(s, axis=1, keepdims=True)
-            p = jnp.where(keep, jnp.exp((s - top) * scale), 0.0)
+            p = jnp.exp((s - top) * scale)
             total = jnp.sum(p, axis=1, keepdims=True)
-            some = total > 0.0
-            safe = jnp.where(some, total, 1.0)
-            outs.append(nn(p.astype(bf16), rows_at[h, :, 128:256]) / safe)
-            logs.append(jnp.where(some, top * scale + jnp.log(safe), NEG))
+            some = top > 0.5 * NEG
+            outs.append(
+                nn(p.astype(bf16), rows_at[h, :, 128:256]) * jnp.where(some, 1.0 / total, 0.0)
+            )
+            logs.append(jnp.where(some, top * scale + jnp.log(total), NEG))
         return outs, logs
 
     def out_x(dz):
@@ -1196,10 +1222,8 @@
     r.small_send[18:19] = fold_sum(col_sum(feed_sum * feed_sum))
     near(lambda o, below: neighbour(o))
     halo_x.start()
-    p_down.pair(False)
     p_o.begin_left()
     p_o.begin()
-    p_up.pair(False)
 
     def join(o, below):
         give_x(o).wait()
@@ -1231,6 +1255,8 @@
             r.dq_sum[:, head_cols(h)] += r.dq_zr[o, h].astype(f32)
 
     near(merge)
+    p_up.pair(False)
+    p_down.pair(False)
 
     r.d_q[...] = r.dq_sum[...].astype(bf16)
     p_q.begin()
@@ -1502,16 +1528,17 @@
 def hand_out_kernel(*refs, copied, entries):
     count = len(copied)
     sources, (input_grad, small, gate, hot), outs = refs[:count], refs[count : count + 4], refs[count + 4 :]
-    grad_out, gains_out, position_out, gate_out, rms_out = outs[count : count + 5]
+    grad_out, one_out, two_out, position_out, gate_out, rms_out = outs[count : count + 6]
     for source, out in zip(sources, outs):
         out[...] = source[...]
     grad_out[...] = input_grad[...].astype(f32)
     me = lax.axis_index("seq")
-    if gains_out.shape[1] == 128:
-        gains_out[0:1, :] = small[pl.ds(me, 1), :]
-        gains_out[1:2, :] = small[pl.ds(me + 8, 1), :]
+    if one_out.shape[0] == 1:
+        one_out[...] = small[pl.ds(me, 1), :]
+        two_out[...] = small[pl.ds(me + 8, 1), :]
     else:
-        gains_out[...] = small[0:16, :]
+        one_out[...] = small[0:8, :]
+        two_out[...] = small[8:16, :]
     lines = hot.shape[0] // 128
     for h in range(2):
         found = jnp.zeros((1, hot.shape[1]), f32)
@@ -1545,7 +1572,7 @@
         jax.ShapeDtypeStruct(shape, f32)
         for shape in (
             done["input_grad"].shape,
-            (2, 128) if own == 128 else (16, 128),
+            *[(1 if own == 128 else 8, 128)] * 2,
             (2, hot.shape[1]),
             (1, 2),
             (1, 3),
@@ -1555,12 +1582,12 @@
         functools.partial(hand_out_kernel, copied=copied, entries=entries),
         out_shape=tuple(shapes),
         in_specs=[vmem] * len(copied) + [vmem, vmem, smem, vmem],
-        out_specs=(vmem,) * (len(copied) + 5),
+        out_specs=(vmem,) * (len(copied) + 6),
         compiler_params=pltpu.CompilerParams(vmem_limit_bytes=62 * MIB),
         name="hand_out",
     )(*(done[name] for name in copied), done["input_grad"], done["small"], gate, hot)
     named = dict(zip(copied, found))
-    named |= dict(zip(("input_grad", "gains", "position", "gate", "rms"), found[len(copied) :]))
+    named |= dict(zip(("input_grad", "gain_one", "gain_two", "position", "gate", "rms"), found[len(copied) :]))
     return named
 
 
@@ -1595,9 +1622,6 @@
     token = jnp.arange(block_len, dtype=jnp.int32)[None, :, None]
     codes = (wanted // slot_count) * (block_len * slot_count) + token * slot_count + wanted % slot_count
     codes = lax.sort(codes.reshape(2, -1), dimension=1, is_stable=False)
-    places, tok = request(codes, seq_count, slot_count, block_len)
-    rows = gather_rows(places, widen(memory_table))
-
     hot, outside = diagonal_buckets(block_len, bucket_total)
     bias_row = jnp.dot(position_bias, hot, precision=highest) + outside[None]
 
@@ -1607,8 +1631,10 @@
     hat_one, _ = norm_stats(x.astype(f32))
     normed_one = (hat_one * first_gain).astype(bf16)
     queries = nn(normed_one, query_weight).astype(bf16)
-    keys = nn(normed_one, key_weight).astype(bf16)
-    values = nn(normed_one, value_weight).astype(bf16)
+    places, tok, keys, values = request(
+        codes, normed_one, key_weight, value_weight, seq_count, slot_count, block_len
+    )
+    rows = gather_rows(places, widen(memory_table))
     q_all = lax.all_gather(queries, "seq", axis=0)
 
     done = layer(
@@ -1640,10 +1666,10 @@
     entries = float(block_len * model_width * seq_count)
     out = hand_out(done, gate_flat, jnp.asarray(hot.T), entries, seq_count)
     share = model_width // seq_count
-    gains = out["gains"]
+    gains = [out["gain_one"].reshape(-1), out["gain_two"].reshape(-1)]
     if share != 128:
         start = lax.axis_index("seq") * share
-        gains = lax.dynamic_slice_in_dim(gains.reshape(2, model_width), start, share, 1)
+        gains = [lax.dynamic_slice_in_dim(gain, start, share) for gain in gains]
     return (
         out["layer"][None],
         out["input_grad"][None],

time: 234 us -> 225 us (0.962)
  Pallas kernels: 205 us -> 197 us
    pallas_call x1, Pallas kernels: 155 us -> 148 us  [layer(): pl.pallas_call(functools.partial(layer_kernel, names=(*inputs, *outputs,...]
  transfers between devices with their start and end apart: 1 -> 1, of which waited for: 0 -> 0; matrix products, arithmetic and copies ran while one was open for 2% -> 1% of each run, Pallas kernels for 19% -> 20%
where the time goes in v6:
time: 225 us; the launch traced here: 224 us
  Pallas kernels  197 us (88%)
  between operations  15.7 us (7%)
  other arithmetic  3.97 us (2%)
  local copies, waits for them, and re-layouts  3.82 us (2%)
  matrix products  2.96 us (1%)
    pallas_call x1, Pallas kernels, layer(): pl.pallas_call(functools.partial(layer_kernel, names=(*inputs, *outputs,...  148 us
    pallas_call x1, Pallas kernels, gather_rows(): pl.pallas_call(functools.partial(gather_kernel, unroll=unroll, group=unro...  21.8 us
    pallas_call x1, Pallas kernels, widen(): pl.pallas_call(functools.partial(widen_kernel, chunk=chunk, part=32), out...  14.6 us
    pallas_call x1, Pallas kernels, request(): pl.pallas_call(functools.partial(request_kernel, parts=parts, slots=slots...  8.68 us
  transfers between devices with their start and end apart: 1, of which 0 were waited for; matrix products, arithmetic and copies ran while one was open for 1% of the time, Pallas kernels for 20%

profile of v6, /device:TPU:0, one launch (start us, length us, event | category | flops | bytes accessed | tf_op | source)
XLA Modules:
  0.0 223.7 jit_solution(12253521041629482111)
XLA Ops:
  8.0 0.0 copy-start
  8.0 0.0 sort.9.cloned.1.call-start
  8.1 0.9 fusion.6
  9.0 0.1 copy.31
  9.1 0.8 reshape.52
  9.9 0.0 sort.9.cloned.1.call-update
  9.9 0.0 all-gather.3.cloned.1.call-start
  10.0 1.2 fusion.1
  11.2 1.2 fusion.3.normed_ref.refs_8_
  12.5 0.0 copy-start.1
  12.5 2.2 convolution_convert_fusion.refs_2_
  14.7 0.0 all-gather.3.cloned.1.call-update
  14.7 0.0 copy-start.10
  14.7 0.0 copy-start.8
  14.7 0.0 copy-start.9
  14.8 0.0 copy-start.2
  14.8 0.0 copy-start.3
  14.8 14.6 %widen.1.wide_hbm = f32[2,16384,128]{2,1,0:T(8,128)} custom-call(bf16[8192,2,256]{2,1,0:T(2,128)(2,1)} %table_hbm.1), custom_call_target="tpu_custom_call" | custom-call | bytes 41943040 | tf_op jit(solution)/shard_map/widen/pallas_call | solution.py:101
  29.4 0.6 add_divide_fusion.refs_1_.refs_9_
  30.0 0.0 copy-done.8
  30.0 0.8 fusion.refs_5_
  30.8 0.0 copy-start.7
  30.8 0.8 copy-done.7
  31.6 8.7 %request.1 = (s32[8,2,1024]{2,1,0:T(2,128)S(1)}, s32[8,2,1024]{2,1,0:T(2,128)S(1)}, bf16[256,256]{1,0:T(8,128)(2,1)S(1)}, bf16[256,256]{1,0:T(8,128)(2,1)S(1)}) custom-call(s32[2,8192]{1,0:T(2,128)S(1)} %copy-done.7, bf16[256,1024]{1,0:T(8,128)(2,1)S(1)} %fusion.3.normed_ref.refs_8_, bf16[1024,256]{1,0:T(8,128)(2,1)S(1)} %copy-done.2, ...), custom_call_target="tpu_custom_call" | custom-call | tf_op jit(solution)/shard_map/request/pallas_call | solution.py:307
  40.3 0.0 copy-start.4
  40.3 0.6 copy-done.4
  41.0 0.6 copy-done.6
  41.6 0.7 copy.32
  42.3 21.8 %gather_rows.1.refs_12_ = bf16[8,2,1024,256]{3,2,1,0:T(8,128)(2,1)} custom-call(s32[16384]{0:T(1024)} %bitcast.48, f32[2,16384,128]{2,1,0:T(8,128)} %widen.1.wide_hbm), custom_call_target="tpu_custom_call" | custom-call | bytes 104857600 | tf_op jit(solution)/shard_map/gather_rows/pallas_call | solution.py:172
  64.1 0.0 all-gather.3.cloned.1.call-done
  64.1 148.0 %layer.1 = (bf16[256,1024]{1,0:T(8,128)(2,1)}, bf16[256,1024]{1,0:T(8,128)(2,1)}, f32[128,256]{1,0:T(8,128)}, f32[128,256]{1,0:T(8,128)}, f32[128,256]{1,0:T(8,1...) custom-call(s32[4]{0:T(128)} %bitcast.51, ...), custom_call_target="tpu_custom_call" | custom-call | flops 4000000000 | bytes 157286400 | tf_op jit(solution)/shard_map/layer/pallas_call | solution.py:1505
  212.1 4.2 %hand_out.1 = (bf16[256,1024]{1,0:T(8,128)(2,1)}, f32[128,256]{1,0:T(8,128)}, f32[128,256]{1,0:T(8,128)}, f32[128,256]{1,0:T(8,128)}, f32[256,128]{1,0:T(8,128)}...) custom-call(bf16[256,1024]{1,0:T(8,128)(2,1)} %get-tuple-element.43., ...), custom_call_target="tpu_custom_call" | custom-call | tf_op jit(solution)/shard_map/hand_out/pallas_call | solution.py:1581
  (12 shorter events, 0.0 us)
Async XLA Ops:
  8.0 22.0 %copy-start = (f32[2,32]{1,0:T(2,128)S(1)}, f32[2,32]{1,0:T(2,128)}, u32[]{:S(2)}) copy-start(f32[2,32]{1,0:T(2,128)} %param.28) | copy-start | bytes 772
  8.0 22.7 %sort.9.cloned.1.call-start = ((), (), s32[]{:S(2)}) async-start(), calls=%async_computation.1 | async-start | bytes 196640 | tf_op jit(solution)/shard_map/sort | solution.py:1624
  9.9 54.2 %all-gather.3.cloned.1.call-start = ((), (), s32[]{:S(2)}) async-start(), calls=%async_computation | async-start | bytes 1179648 | tf_op jit(solution)/shard_map/all_gather | solution.py:1638
  12.5 18.3 %copy-start.1 = (bf16[256,1024]{1,0:T(8,128)(2,1)}, bf16[256,1024]{1,0:T(8,128)(2,1)S(1)}, u32[]{:S(2)}) copy-start(bf16[256,1024]{1,0:T(8,128)(2,1)S(1)} %fusion.3.normed_ref.refs_8_) | copy-start | bytes 1572868
  14.7 14.7 %copy-start.10 = (f32[2]{0:T(128)S(1)}, f32[2]{0:T(128)}, u32[]{:S(2)}) copy-start(f32[2]{0:T(128)} %param.29) | copy-start | bytes 28
  14.7 15.3 %copy-start.8 = (f32[32,768]{1,0:T(8,128)S(1)}, f32[32,768]{1,0:T(8,128)}, u32[]{:S(2)}) copy-start(f32[32,768]{1,0:T(8,128)} %constant.46.clone) | copy-start | bytes 294916
  14.7 15.3 %copy-start.9 = (f32[768]{0:T(1024)S(1)}, f32[768]{0:T(1024)}, u32[]{:S(2)}) copy-start(f32[768]{0:T(1024)} %constant.53) | copy-start | bytes 9220
  14.8 16.0 %copy-start.2 = (bf16[1024,256]{1,0:T(8,128)(2,1)S(1)}, bf16[1024,256]{1,0:T(8,128)(2,1)}, u32[]{:S(2)}) copy-start(bf16[1024,256]{1,0:T(8,128)(2,1)} %refs_18_.1) | copy-start | bytes 1572868
  14.8 16.0 %copy-start.3 = (bf16[1024,256]{1,0:T(8,128)(2,1)S(1)}, bf16[1024,256]{1,0:T(8,128)(2,1)}, u32[]{:S(2)}) copy-start(bf16[1024,256]{1,0:T(8,128)(2,1)} %refs_19_.1) | copy-start | bytes 1572868
  30.8 0.8 copy-start.7
  40.3 0.7 copy-start.4
  41.0 0.6 copy-start.6
  41.6 22.5 %copy-start.5 = (bf16[256,256]{1,0:T(8,128)(2,1)}, bf16[256,256]{1,0:T(8,128)(2,1)S(1)}, u32[]{:S(2)}) copy-start(bf16[256,256]{1,0:T(8,128)(2,1)S(1)} %get-tuple-element.40.refs_4_) | copy-start | bytes 393220
Sparse Core Ops, SparseCore 0:
  11.9 16.9 sort.11.cloned.1.call-done
  (1 shorter events, 0.0 us)
Sparse Core Ops, SparseCore 1:
  14.8 43.3 all-gather.2

commit v7 on v6

--- a/solution.py
+++ b/solution.py
@@ -164,8 +164,8 @@
     store(1, 1, 1).wait()
 
 
-def gather_rows(places, wide):
-    parts, heads, rows = places.shape
+def gather_rows(places, wide, shape):
+    parts, heads, rows = shape
     unroll = min(64, rows)
     hbm = pl.BlockSpec(memory_space=pltpu.HBM)
     dma = pltpu.SemaphoreType.DMA
@@ -282,10 +282,15 @@
 
     lax.fori_loop(1, parts, start, 0)
     shift = slots.bit_length() - 1
+    lines = rows // 128
 
     def read(d, j):
         code = got[d]
-        place_ref[j] = (code & (slots - 1)) * 2
+        for h in range(2):
+            found = (code[h : h + 1] & (slots - 1)) * 2
+            pieces = [found[:, 128 * i : 128 * i + 128] for i in range(lines)]
+            at = pl.ds(pl.multiple_of((2 * j + h) * lines, lines), lines)
+            place_ref[at, :] = jnp.concatenate(pieces, axis=0)
         tok_ref[j] = (code >> shift) & (tokens - 1)
 
     keep.wait()
@@ -306,7 +311,10 @@
     shape = (parts, 2, rows)
     return pl.pallas_call(
         functools.partial(request_kernel, parts=parts, slots=slots, tokens=tokens),
-        out_shape=(jax.ShapeDtypeStruct(shape, jnp.int32),) * 2
+        out_shape=(
+            jax.ShapeDtypeStruct((parts * 2 * rows // 128, 128), jnp.int32),
+            jax.ShapeDtypeStruct(shape, jnp.int32),
+        )
         + (jax.ShapeDtypeStruct((tokens, wk.shape[1]), bf16),) * 2,
         in_specs=[vmem] * 4,
         out_specs=(vmem,) * 4,
@@ -1634,7 +1642,7 @@
     places, tok, keys, values = request(
         codes, normed_one, key_weight, value_weight, seq_count, slot_count, block_len
     )
-    rows = gather_rows(places, widen(memory_table))
+    rows = gather_rows(places, widen(memory_table), tok.shape)
     q_all = lax.all_gather(queries, "seq", axis=0)
 
     done = layer(

time: 225 us -> 225 us (level)
  no operation moved by 1% of the time
where the time goes in v7:
time: 225 us; the launch traced here: 224 us
  Pallas kernels  197 us (88%)
  between operations  15.7 us (7%)
  other arithmetic  3.98 us (2%)
  local copies, waits for them, and re-layouts  3.77 us (2%)
  matrix products  2.96 us (1%)
    pallas_call x1, Pallas kernels, layer(): pl.pallas_call(functools.partial(layer_kernel, names=(*inputs, *outputs,...  148 us
    pallas_call x1, Pallas kernels, gather_rows(): pl.pallas_call(functools.partial(gather_kernel, unroll=unroll, group=unro...  21.8 us
    pallas_call x1, Pallas kernels, widen(): pl.pallas_call(functools.partial(widen_kernel, chunk=chunk, part=32), out...  14.6 us
    pallas_call x1, Pallas kernels, request(): pl.pallas_call(functools.partial(request_kernel, parts=parts, slots=slots...  8.7 us
  transfers between devices with their start and end apart: 1, of which 0 were waited for; matrix products, arithmetic and copies ran while one was open for 1% of the time, Pallas kernels for 20%

profile of v7, /device:TPU:0, one launch (start us, length us, event | category | flops | bytes accessed | tf_op | source)
XLA Modules:
  0.0 223.7 jit_solution(2548267853785774640)
XLA Ops:
  8.0 0.0 copy-start
  8.0 0.0 sort.9.cloned.1.call-start
  8.1 0.9 fusion.6
  9.0 0.1 copy.31
  9.1 0.8 reshape.52
  9.9 0.0 sort.9.cloned.1.call-update
  9.9 0.0 all-gather.3.cloned.1.call-start
  10.0 1.2 fusion.1
  11.2 1.2 fusion.3.normed_ref.refs_8_
  12.5 0.0 copy-start.1
  12.5 2.2 convolution_convert_fusion.refs_2_
  14.7 0.0 all-gather.3.cloned.1.call-update
  14.7 0.0 copy-start.11
  14.7 0.0 copy-start.9
  14.7 0.0 copy-start.10
  14.8 0.0 copy-start.2
  14.8 0.0 copy-start.3
  14.8 14.6 %widen.1.wide_hbm = f32[2,16384,128]{2,1,0:T(8,128)} custom-call(bf16[8192,2,256]{2,1,0:T(2,128)(2,1)} %table_hbm.1), custom_call_target="tpu_custom_call" | custom-call | bytes 41943040 | tf_op jit(solution)/shard_map/widen/pallas_call | solution.py:101
  29.4 0.6 add_divide_fusion.refs_1_.refs_9_
  30.0 0.0 copy-done
  30.0 0.8 fusion.refs_5_
  30.8 0.0 copy-start.8
  30.8 0.8 copy-done.8
  31.6 8.7 %request.1 = (s32[128,128]{1,0:T(8,128)S(1)}, s32[8,2,1024]{2,1,0:T(2,128)S(1)}, bf16[256,256]{1,0:T(8,128)(2,1)S(1)}, bf16[256,256]{1,0:T(8,128)(2,1)S(1)}) custom-call(s32[2,8192]{1,0:T(2,128)S(1)} %copy-done.8, bf16[256,1024]{1,0:T(8,128)(2,1)S(1)} %fusion.3.normed_ref.refs_8_, bf16[1024,256]{1,0:T(8,128)(2,1)S(1)} %copy-done.2, ...), custom_call_target="tpu_custom_call" | custom-call | tf_op jit(solution)/shard_map/request/pallas_call | solution.py:312
  40.3 0.0 copy-start.4
  40.3 0.6 copy-done.4
  41.0 0.6 copy-done.6
  41.6 0.6 copy-done.7
  42.2 21.8 %gather_rows.1.refs_12_ = bf16[8,2,1024,256]{3,2,1,0:T(8,128)(2,1)} custom-call(s32[16384]{0:T(1024)} %bitcast.43, f32[2,16384,128]{2,1,0:T(8,128)} %widen.1.wide_hbm), custom_call_target="tpu_custom_call" | custom-call | bytes 104857600 | tf_op jit(solution)/shard_map/gather_rows/pallas_call | solution.py:172
  64.1 0.0 all-gather.3.cloned.1.call-done
  64.1 148.0 %layer.1 = (bf16[256,1024]{1,0:T(8,128)(2,1)}, bf16[256,1024]{1,0:T(8,128)(2,1)}, f32[128,256]{1,0:T(8,128)}, f32[128,256]{1,0:T(8,128)}, f32[128,256]{1,0:T(8,1...) custom-call(s32[4]{0:T(128)} %bitcast.49, ...), custom_call_target="tpu_custom_call" | custom-call | flops 4000000000 | bytes 157286400 | tf_op jit(solution)/shard_map/layer/pallas_call | solution.py:1513
  212.1 4.2 %hand_out.1 = (bf16[256,1024]{1,0:T(8,128)(2,1)}, f32[128,256]{1,0:T(8,128)}, f32[128,256]{1,0:T(8,128)}, f32[128,256]{1,0:T(8,128)}, f32[256,128]{1,0:T(8,128)}...) custom-call(bf16[256,1024]{1,0:T(8,128)(2,1)} %get-tuple-element.43., ...), custom_call_target="tpu_custom_call" | custom-call | tf_op jit(solution)/shard_map/hand_out/pallas_call | solution.py:1589
  (13 shorter events, 0.0 us)
Async XLA Ops:
  8.0 22.0 %copy-start = (f32[2,32]{1,0:T(2,128)S(1)}, f32[2,32]{1,0:T(2,128)}, u32[]{:S(2)}) copy-start(f32[2,32]{1,0:T(2,128)} %param.28) | copy-start | bytes 772
  8.0 22.7 %sort.9.cloned.1.call-start = ((), (), s32[]{:S(2)}) async-start(), calls=%async_computation.1 | async-start | bytes 196640 | tf_op jit(solution)/shard_map/sort | solution.py:1632
  9.9 54.2 %all-gather.3.cloned.1.call-start = ((), (), s32[]{:S(2)}) async-start(), calls=%async_computation | async-start | bytes 1179648 | tf_op jit(solution)/shard_map/all_gather | solution.py:1646
  12.5 18.3 %copy-start.1 = (bf16[256,1024]{1,0:T(8,128)(2,1)}, bf16[256,1024]{1,0:T(8,128)(2,1)S(1)}, u32[]{:S(2)}) copy-start(bf16[256,1024]{1,0:T(8,128)(2,1)S(1)} %fusion.3.normed_ref.refs_8_) | copy-start | bytes 1572868
  14.7 14.7 %copy-start.11 = (f32[2]{0:T(128)S(1)}, f32[2]{0:T(128)}, u32[]{:S(2)}) copy-start(f32[2]{0:T(128)} %param.29) | copy-start | bytes 28
  14.7 15.3 %copy-start.9 = (f32[32,768]{1,0:T(8,128)S(1)}, f32[32,768]{1,0:T(8,128)}, u32[]{:S(2)}) copy-start(f32[32,768]{1,0:T(8,128)} %constant.46.clone) | copy-start | bytes 294916
  14.7 15.3 %copy-start.10 = (f32[768]{0:T(1024)S(1)}, f32[768]{0:T(1024)}, u32[]{:S(2)}) copy-start(f32[768]{0:T(1024)} %constant.53) | copy-start | bytes 9220
  14.8 16.0 %copy-start.2 = (bf16[1024,256]{1,0:T(8,128)(2,1)S(1)}, bf16[1024,256]{1,0:T(8,128)(2,1)}, u32[]{:S(2)}) copy-start(bf16[1024,256]{1,0:T(8,128)(2,1)} %refs_18_.1) | copy-start | bytes 1572868
  14.8 16.0 %copy-start.3 = (bf16[1024,256]{1,0:T(8,128)(2,1)S(1)}, bf16[1024,256]{1,0:T(8,128)(2,1)}, u32[]{:S(2)}) copy-start(bf16[1024,256]{1,0:T(8,128)(2,1)} %refs_19_.1) | copy-start | bytes 1572868
  30.8 0.8 copy-start.8
  40.3 0.7 copy-start.4
  41.0 0.6 copy-start.6
  41.6 0.6 copy-start.7
  42.2 21.8 %copy-start.5 = (bf16[256,256]{1,0:T(8,128)(2,1)}, bf16[256,256]{1,0:T(8,128)(2,1)S(1)}, u32[]{:S(2)}) copy-start(bf16[256,256]{1,0:T(8,128)(2,1)S(1)} %get-tuple-element.40.refs_4_) | copy-start | bytes 393220
Sparse Core Ops, SparseCore 0:
  11.9 16.9 sort.11.cloned.1.call-done
  (1 shorter events, 0.0 us)
Sparse Core Ops, SparseCore 1:
  14.8 43.3 all-gather.2
